TPU v7x, 32 devices: a whole 2x2x4 slice. The times are simulated.
32 devices in a mesh: cluster: 16 (over z, y, x), copy: 2 (over core).
Axes of the slice: x: 2, y: 2, z: 4, core: 2. Of those that a mesh axis runs over, the one named last changes fastest.
Arguments:
- points: bfloat16 [512, 128, 512], P(('cluster', 'copy')), may hold values from -18 to 18
- block_ids: int32 [512], P(('cluster', 'copy')), may hold values from 0 to 15, as said below
- block_counts: int32 [32], P(('cluster', 'copy')), may hold values from 11 to 16, as said below
- centroids: bfloat16 [32768, 512], P('cluster'), may hold values from -6 to 6
Outputs:
- new_centroids: bfloat16 [32768, 512], P(('cluster', 'copy'))
Inputs may be any that keep to these rules, and one draw needn't show every extreme that they name: `block_ids`: the 16 blocks of one device name 16 different coarse clusters. For every index along copy, one coarse cluster is named by the first block of every device with that copy index. Only the first block_counts[d] block slots of device d are valid. Some device has all 16 valid.
All inputs are finite; a program needn't handle non-finite values.
Results may differ from a plain program's by a relative error of at most 0.0021.
Values may be sent and summed in bfloat16 or wider, within the bound.
No kernel may reach another device: no remote copies, remote signals or barrier semaphores. Data moves between devices by JAX's collectives and lax.ppermute only.
A program may use at most 64 MiB of HBM per device.

v0:
```python
import math

import jax
import jax.numpy as jnp
from jax import lax
from jax.sharding import PartitionSpec as P

turn_blocks = 4


def owner_sums(received, arrived, centroids):
    slot_total = received.shape[0]
    block_rows = received.shape[1]
    feature = received.shape[2]
    present = arrived > 0.5
    how_many = jnp.sum(present.astype(jnp.int32))
    ranking = jnp.cumsum(present.astype(jnp.int32)) - 1
    listing = jnp.zeros((slot_total + turn_blocks,), jnp.int32)
    listing = listing.at[jnp.where(present, ranking, slot_total + turn_blocks)].set(
        jnp.arange(slot_total, dtype=jnp.int32), mode="drop"
    )
    scale_factor = 3.0 / math.sqrt(feature)

    def visit(step_index, running):
        start_at = step_index * turn_blocks
        chosen = lax.dynamic_slice_in_dim(listing, start_at, turn_blocks)
        usable = start_at + jnp.arange(turn_blocks, dtype=jnp.int32) < how_many
        gathered = received[chosen].reshape(turn_blocks * block_rows, feature)
        logits = (
            jnp.einsum("rd,kd->rk", gathered, centroids, preferred_element_type=jnp.float32)
            * scale_factor
        )
        row_mask = jnp.repeat(usable, block_rows).astype(jnp.float32)[:, None]
        weights = (jax.nn.softmax(logits, axis=-1) * row_mask).astype(jnp.bfloat16)
        return running + jnp.einsum(
            "rk,rd->kd", weights, gathered, preferred_element_type=jnp.float32
        )

    initial = jnp.zeros((centroids.shape[0], feature), jnp.float32)
    return lax.fori_loop(0, (how_many + turn_blocks - 1) // turn_blocks, visit, initial)


def local(points, block_ids, block_counts, centroids):
    held = points.shape[0]
    owners = lax.axis_size("cluster")
    in_range = jnp.arange(held, dtype=jnp.int32) < block_counts[0]
    routing = jnp.where(in_range, block_ids, -1).astype(jnp.bfloat16)
    targets = routing.astype(jnp.int32)
    slot_index = jnp.arange(held, dtype=jnp.int32)
    matches = targets[None, :] == jnp.arange(owners, dtype=jnp.int32)[:, None]
    present = jnp.any(matches, axis=1)
    position = jnp.sum(jnp.where(matches, slot_index[None, :], 0), axis=1)
    outgoing = jnp.where(present[:, None, None], points[position], jnp.zeros((), jnp.bfloat16))
    received, arrived = (
        lax.all_to_all(outgoing, "cluster", split_axis=0, concat_axis=0, tiled=True),
        lax.all_to_all(
            present.astype(jnp.bfloat16), "cluster", split_axis=0, concat_axis=0, tiled=True
        ),
    )
    partial_sums = owner_sums(received, arrived, centroids)
    share = lax.psum_scatter(partial_sums, "copy", scatter_dimension=0, tiled=True)
    share_rows = share.shape[0]
    previous = lax.dynamic_slice_in_dim(
        centroids, lax.axis_index("copy") * share_rows, share_rows, 0
    ).astype(jnp.float32)
    combined = share + previous
    scaled = combined * lax.rsqrt(jnp.mean(combined * combined, axis=-1, keepdims=True) + 1e-06)
    return scaled.astype(jnp.bfloat16)


def solution(mesh):
    return jax.shard_map(
        local,
        mesh=mesh,
        in_specs=(
            P(("cluster", "copy"), None, None),
            P(("cluster", "copy")),
            P(("cluster", "copy")),
            P("cluster", None),
        ),
        out_specs=P(("cluster", "copy"), None),
        check_vma=False,
    )
```

profile of v0, /device:TPU:17, one launch (start us, length us, event | category | flops | bytes accessed | tf_op | source)
XLA Modules:
  0.0 153.0 jit_solution(13361887625355742653)
XLA Ops:
  7.3 0.7 fusion.10
  8.0 0.1 fusion.8
  8.1 0.7 copy.27
  8.8 6.6 %all-to-all-start = ((bf16[16,1,1]{2,1,0:T(2,128)(2,1)}), bf16[16,1,1]{2,1,0:T(2,128)(2,1)S(1)}, u32[]{:S(2)}, u32[]{:S(2)}) async-start(bf16[16,1,1]{2,1,0:T(2,128)(2,1)} %copy.27), calls=%async_computation | async-start | bytes 16384 | tf_op jit(solution)/shard_map/all_to_all | solution.py:56
  15.4 0.1 select_reduce_fusion
  15.5 0.1 copy.30
  15.6 0.1 fusion.7
  15.7 2.0 %gather_fusion.1 = bf16[16,128,512]{2,1,0:T(8,128)(2,1)} fusion(bf16[16,128,512]{2,1,0:T(8,128)(2,1)S(1)} %copy-done, s32[1024]{0:T(1024)S(1)} %pad_clamp_fusion.1), kind=kCustom, calls=%fused_computation.1 | custom fusion | bytes 4194368 | tf_op jit(solution)/shard_map/gather | solution.py:53
  17.8 3.1 %broadcast_select_fusion = bf16[16,128,512]{2,1,0:T(8,128)(2,1)} fusion(bf16[16,128,512]{2,1,0:T(8,128)(2,1)} %gather_fusion.1, pred[16]{0:T(512)(128)(4,1)S(1)} %fusion.8), kind=kLoop, calls=%fused_computation.19 | loop fusion | flops 1048576 | bytes 4194320 | tf_op jit(solution)/shard_map/jit(_where)/select_n | solution.py:53
  20.9 6.4 %all-to-all-start.1 = ((bf16[16,128,512]{2,1,0:T(8,128)(2,1)}), bf16[16,128,512]{2,1,0:T(8,128)(2,1)}, u32[]{:S(2)}, u32[]{:S(2)}) async-start(bf16[16,128,512]{2,1,0:T(8,128)(2,1)} %broadcast_select_fusion), calls=%async_computation.1 | async-start | bytes 4194304 | tf_op jit(solution)/shard_map/all_to_all | solution.py:55
  27.3 0.7 fusion.5
  28.6 0.4 compare_reduce_fusion
  28.9 0.1 copy.28
  29.1 0.1 copy.29
  29.2 0.1 fusion.6
  29.3 0.6 scatter_custom_fusion
  29.9 44.2 %all-to-all-done.1 = bf16[16,128,512]{2,1,0:T(8,128)(2,1)} async-done(((bf16[16,128,512]{2,1,0:T(8,128)(2,1)}), bf16[16,128,512]{2,1,0:T(8,128)(2,1)}, u32[]{:S(2)}, u32[]{:S(2)}) %all-to-all-start.1) | async-done | bytes 2097184 | tf_op jit(solution)/shard_map/all_to_all | solution.py:55
  74.1 2.5 %broadcast_in_dim.50 = f32[2048,512]{1,0:T(8,128)} broadcast(f32[]{:T(128)} %constant.33.clone.1), dimensions={} | broadcast | bytes 4194308 | tf_op jit(solution)/shard_map/broadcast_in_dim | solution.py:39
  76.6 50.4 %while.10 = (s32[]{:T(128)}, f32[2048,512]{1,0:T(8,128)}, s32[]{:T(128)}, s32[20]{0:T(128)S(1)}, bf16[16,128,512]{2,1,0:T(8,128)(2,1)}, /*index=5*/bf16[2048,512...) while((s32[]{:T(128)}, f32[2048,512]{1,0:T(8,128)}, s32[]{:T(128)}, ...), condition=%wide.region_8.9_spmd, body=%wide.region_5.8_spmd.sunk | while | flops 2159017984 | bytes 25184520 | solution.py:40
  76.6 0.1 compare_select_fusion.5
  76.6 2.2 %gather_fusion = bf16[4,128,512]{2,1,0:T(8,128)(2,1)S(1)} fusion(bf16[16,128,512]{2,1,0:T(8,128)(2,1)} %get-tuple-element.134, s32[1024]{0:T(1024)S(1)} %pad_clamp_fusion.3), kind=kCustom, calls=%fused_computation.clone.1 | custom fusion | bytes 1048592 | tf_op jit(solution)/shard_map/while/body/gather | solution.py:28
  78.8 3.0 %multiply_reduce_fusion.3 = (f32[512]{0:T(512)S(1)}, f32[512,2048]{1,0:T(8,128)S(1)}) fusion(bf16[512,512]{1,0:T(8,128)(2,1)S(1)} %bitcast.23, bf16[2048,512]{1,0:T(8,128)(2,1)} %get-tuple-element.135), kind=kOutput, calls=%fused_computation.5.clone.1 | convolution fusion | flops 1075838464 | bytes 6817792 | tf_op jit(solution)/shard_map/while/body/rd,kd->rk/dot_general | solution.py:30
  81.8 0.8 fusion.23
  82.6 0.6 compare_convert_fusion.3
  83.2 0.1 broadcast_bitcast_fusion.2
  83.3 5.9 %convolution_add_fusion.2 = f32[2048,512]{1,0:T(8,128)} fusion(f32[2048,512]{1,0:T(8,128)} %get-tuple-element.120, bf16[512,512]{1,0:T(8,128)(2,1)S(1)} %bitcast.24, f32[512,2048]{1,0:T(8,128)S(1)} %get-tuple-element.106, f32[512]{0:T(512)S(1)} %broadcast_bitcast_fusion.2, f32[512]{0:T(512)S(1)} %fusion.23, f32[512]{0:T(512)S(1)} %get-tuple-element.107), kind=kOutput, calls=%fused_computation.7.clone.1 | convolution fusion | flops 1080033280 | bytes 13113344 | tf_op jit(solution)/shard_map/while/body/rk,rd->kd/dot_general | solution.py:35
  89.2 0.1 compare_select_fusion.5
  89.2 2.2 %gather_fusion = bf16[4,128,512]{2,1,0:T(8,128)(2,1)S(1)} fusion(bf16[16,128,512]{2,1,0:T(8,128)(2,1)} %get-tuple-element.134, s32[1024]{0:T(1024)S(1)} %pad_clamp_fusion.3), kind=kCustom, calls=%fused_computation.clone.1 | custom fusion | bytes 1048592 | tf_op jit(solution)/shard_map/while/body/gather | solution.py:28
  91.4 3.0 %multiply_reduce_fusion.3 = (f32[512]{0:T(512)S(1)}, f32[512,2048]{1,0:T(8,128)S(1)}) fusion(bf16[512,512]{1,0:T(8,128)(2,1)S(1)} %bitcast.23, bf16[2048,512]{1,0:T(8,128)(2,1)} %get-tuple-element.135), kind=kOutput, calls=%fused_computation.5.clone.1 | convolution fusion | flops 1075838464 | bytes 6817792 | tf_op jit(solution)/shard_map/while/body/rd,kd->rk/dot_general | solution.py:30
  94.4 0.8 fusion.23
  95.2 0.6 compare_convert_fusion.3
  95.9 5.9 %convolution_add_fusion.2 = f32[2048,512]{1,0:T(8,128)} fusion(f32[2048,512]{1,0:T(8,128)} %get-tuple-element.120, bf16[512,512]{1,0:T(8,128)(2,1)S(1)} %bitcast.24, f32[512,2048]{1,0:T(8,128)S(1)} %get-tuple-element.106, f32[512]{0:T(512)S(1)} %broadcast_bitcast_fusion.2, f32[512]{0:T(512)S(1)} %fusion.23, f32[512]{0:T(512)S(1)} %get-tuple-element.107), kind=kOutput, calls=%fused_computation.7.clone.1 | convolution fusion | flops 1080033280 | bytes 13113344 | tf_op jit(solution)/shard_map/while/body/rk,rd->kd/dot_general | solution.py:35
  101.7 0.1 compare_select_fusion.5
  101.8 2.2 %gather_fusion = bf16[4,128,512]{2,1,0:T(8,128)(2,1)S(1)} fusion(bf16[16,128,512]{2,1,0:T(8,128)(2,1)} %get-tuple-element.134, s32[1024]{0:T(1024)S(1)} %pad_clamp_fusion.3), kind=kCustom, calls=%fused_computation.clone.1 | custom fusion | bytes 1048592 | tf_op jit(solution)/shard_map/while/body/gather | solution.py:28
  104.0 3.0 %multiply_reduce_fusion.3 = (f32[512]{0:T(512)S(1)}, f32[512,2048]{1,0:T(8,128)S(1)}) fusion(bf16[512,512]{1,0:T(8,128)(2,1)S(1)} %bitcast.23, bf16[2048,512]{1,0:T(8,128)(2,1)} %get-tuple-element.135), kind=kOutput, calls=%fused_computation.5.clone.1 | convolution fusion | flops 1075838464 | bytes 6817792 | tf_op jit(solution)/shard_map/while/body/rd,kd->rk/dot_general | solution.py:30
  107.0 0.8 fusion.23
  107.8 0.6 compare_convert_fusion.3
  108.5 5.9 %convolution_add_fusion.2 = f32[2048,512]{1,0:T(8,128)} fusion(f32[2048,512]{1,0:T(8,128)} %get-tuple-element.120, bf16[512,512]{1,0:T(8,128)(2,1)S(1)} %bitcast.24, f32[512,2048]{1,0:T(8,128)S(1)} %get-tuple-element.106, f32[512]{0:T(512)S(1)} %broadcast_bitcast_fusion.2, f32[512]{0:T(512)S(1)} %fusion.23, f32[512]{0:T(512)S(1)} %get-tuple-element.107), kind=kOutput, calls=%fused_computation.7.clone.1 | convolution fusion | flops 1080033280 | bytes 13113344 | tf_op jit(solution)/shard_map/while/body/rk,rd->kd/dot_general | solution.py:35
  114.3 0.1 compare_select_fusion.5
  114.4 2.2 %gather_fusion = bf16[4,128,512]{2,1,0:T(8,128)(2,1)S(1)} fusion(bf16[16,128,512]{2,1,0:T(8,128)(2,1)} %get-tuple-element.134, s32[1024]{0:T(1024)S(1)} %pad_clamp_fusion.3), kind=kCustom, calls=%fused_computation.clone.1 | custom fusion | bytes 1048592 | tf_op jit(solution)/shard_map/while/body/gather | solution.py:28
  116.6 3.0 %multiply_reduce_fusion.3 = (f32[512]{0:T(512)S(1)}, f32[512,2048]{1,0:T(8,128)S(1)}) fusion(bf16[512,512]{1,0:T(8,128)(2,1)S(1)} %bitcast.23, bf16[2048,512]{1,0:T(8,128)(2,1)} %get-tuple-element.135), kind=kOutput, calls=%fused_computation.5.clone.1 | convolution fusion | flops 1075838464 | bytes 6817792 | tf_op jit(solution)/shard_map/while/body/rd,kd->rk/dot_general | solution.py:30
  119.6 0.8 fusion.23
  120.4 0.6 compare_convert_fusion.3
  121.0 5.9 %convolution_add_fusion.2 = f32[2048,512]{1,0:T(8,128)} fusion(f32[2048,512]{1,0:T(8,128)} %get-tuple-element.120, bf16[512,512]{1,0:T(8,128)(2,1)S(1)} %bitcast.24, f32[512,2048]{1,0:T(8,128)S(1)} %get-tuple-element.106, f32[512]{0:T(512)S(1)} %broadcast_bitcast_fusion.2, f32[512]{0:T(512)S(1)} %fusion.23, f32[512]{0:T(512)S(1)} %get-tuple-element.107), kind=kOutput, calls=%fused_computation.7.clone.1 | convolution fusion | flops 1080033280 | bytes 13113344 | tf_op jit(solution)/shard_map/while/body/rk,rd->kd/dot_general | solution.py:35
  127.0 13.8 %reduce-scatter.2.cloned.1.call-done = f32[1024,512]{1,0:T(8,128)} async-done(((f32[2048,512]{1,0:T(8,128)}), f32[1024,512]{1,0:T(8,128)}) %reduce-scatter.2.cloned.1.call-update) | async-done | bytes 2097168 | tf_op jit(solution)/shard_map/reduce_scatter | solution.py:61
  140.7 2.3 %multiply_reduce_fusion.1 = f32[1024]{0:T(1024)S(1)} fusion(f32[1024,512]{1,0:T(8,128)} %reduce-scatter.2.cloned.1.call-done, bf16[2048,512]{1,0:T(8,128)(2,1)} %get-tuple-element.142, s32[]{:T(128)S(6)} %select_n.63), kind=kLoop, calls=%fused_computation.17 | loop fusion | flops 2096128 | bytes 3149828 | tf_op jit(solution)/shard_map/reduce_sum | solution.py:67
  143.1 0.2 copy-done.1
  143.2 2.9 %multiply_convert_fusion.2 = bf16[1024,512]{1,0:T(8,128)(2,1)} fusion(f32[1024,512]{1,0:T(8,128)} %reduce-scatter.2.cloned.1.call-done, f32[1024]{0:T(1024)S(1)} %add_rsqrt_fusion, bf16[2048,512]{1,0:T(8,128)(2,1)S(1)} %copy-done.1, s32[]{:T(128)S(6)} %select_n.63), kind=kLoop, calls=%fused_computation.16 | loop fusion | flops 2097152 | bytes 4198404 | tf_op jit(solution)/shard_map/convert_element_type | solution.py:68
  (19 shorter events, 0.4 us)
Async XLA Ops:
  6.5 9.2 %copy-start = (bf16[16,128,512]{2,1,0:T(8,128)(2,1)S(1)}, bf16[16,128,512]{2,1,0:T(8,128)(2,1)}, u32[]{:S(2)}) copy-start(bf16[16,128,512]{2,1,0:T(8,128)(2,1)} %param.6) | copy-start | bytes 6291460
  8.8 12.1 %all-to-all-start = ((bf16[16,1,1]{2,1,0:T(2,128)(2,1)}), bf16[16,1,1]{2,1,0:T(2,128)(2,1)S(1)}, u32[]{:S(2)}, u32[]{:S(2)}) async-start(bf16[16,1,1]{2,1,0:T(2,128)(2,1)} %copy.27), calls=%async_computation | async-start | bytes 16384 | tf_op jit(solution)/shard_map/all_to_all | solution.py:56
  20.9 53.2 %all-to-all-start.1 = ((bf16[16,128,512]{2,1,0:T(8,128)(2,1)}), bf16[16,128,512]{2,1,0:T(8,128)(2,1)}, u32[]{:S(2)}, u32[]{:S(2)}) async-start(bf16[16,128,512]{2,1,0:T(8,128)(2,1)} %broadcast_select_fusion), calls=%async_computation.1 | async-start | bytes 4194304 | tf_op jit(solution)/shard_map/all_to_all | solution.py:55
  27.3 113.4 %reduce-scatter.2.cloned.1.call-start = ((), (), s32[]{:S(2)}) async-start(), calls=%async_computation.3 | async-start | bytes 6291456 | tf_op jit(solution)/shard_map/reduce_scatter | solution.py:61
  140.7 2.5 %copy-start.1 = (bf16[2048,512]{1,0:T(8,128)(2,1)S(1)}, bf16[2048,512]{1,0:T(8,128)(2,1)}, u32[]{:S(2)}) copy-start(bf16[2048,512]{1,0:T(8,128)(2,1)} %get-tuple-element.142) | copy-start | bytes 6291460
Sparse Core Ops, SparseCore 0:
  127.1 13.5 reduce-scatter.1
where the time goes:
time: 155 us; the launch traced here: 153 us
  waiting for transfers between devices  57.9 us (37%)
  matrix products  35.4 us (23%)
  other arithmetic  16.6 us (11%)
  local copies, waits for them, and re-layouts  15.2 us (10%)
  between operations  14.8 us (10%)
  starting transfers between devices  12.9 us (8%)
    all_to_all x1, waiting for transfers between devices, local(): lax.all_to_all(outgoing, 'cluster', split_axis=0, concat_axis=0, tiled=True)  44.2 us
    dot_general x4, matrix products, visit(): jnp.einsum('rk,rd->kd', weights, gathered, preferred_element_type=jnp.flo...  23.5 us
    reduce_scatter x1, waiting for transfers between devices, local(): lax.psum_scatter(partial_sums, 'copy', scatter_dimension=0, tiled=True)  13.8 us
    dot_general x4, matrix products, visit(): jnp.einsum('rd,kd->rk', gathered, centroids, preferred_element_type=jnp.f...  11.9 us
    gather x4, local copies, waits for them, and re-layouts, visit(): gathered = received[chosen].reshape(turn_blocks * block_rows, feature)  8.68 us
    all_to_all x1, starting transfers between devices, local(): lax.all_to_all(present.astype(jnp.bfloat16), 'cluster', split_axis=0, con...  6.55 us
    all_to_all x1, starting transfers between devices, local(): lax.all_to_all(outgoing, 'cluster', split_axis=0, concat_axis=0, tiled=True)  6.36 us
    reduce_sum x4, other arithmetic, visit(): weights = (jax.nn.softmax(logits, axis=-1) * row_mask).astype(jnp.bfloat16)  3.29 us
  transfers between devices with their start and end apart: 3, of which 2 were waited for; matrix products, arithmetic and copies ran while one was open for 5% of the time, Pallas kernels for 0%

commit v1 on v0

v1 whole, which is shorter than its diff:
```python
import functools
import math

import jax
import jax.numpy as jnp
from jax import lax
from jax.experimental import pallas as pl
from jax.experimental.pallas import tpu as pltpu
from jax.sharding import PartitionSpec as P

F32 = jnp.float32
BF16 = jnp.bfloat16
TILE = 256
TURN = 4
MIB = 1 << 20


def partner(index, offset, size):
    if size & (size - 1) == 0:
        return index ^ offset
    return lax.rem(index + offset, size) if not isinstance(index, int) else (index + offset) % size


def pairs(offset, size):
    return [(i, partner(i, offset, size)) for i in range(size)]


def stage_kernel(owners, ids, counts, points, *refs):
    outs, (where, zeros, sems) = refs[:owners], refs[owners:]
    slots = points.shape[0]
    me = lax.axis_index("cluster")
    zeros[...] = jnp.zeros_like(zeros)
    for o in range(owners):
        where[o] = -1
    for s in range(slots):

        @pl.when(s < counts[0])
        def _():
            where[ids[s]] = s

    for k in range(owners):
        slot = where[partner(me, k, owners)]

        @pl.when(slot >= 0)
        def _():
            pltpu.make_async_copy(points.at[jnp.maximum(slot, 0)], outs[k], sems.at[k]).start()

        @pl.when(slot < 0)
        def _():
            pltpu.make_async_copy(zeros, outs[k], sems.at[k]).start()

    for k in range(owners):
        pltpu.make_async_copy(zeros, outs[k], sems.at[k]).wait()


def stage(points, ids, counts, owners):
    block = points.shape[1:]
    return pl.pallas_call(
        functools.partial(stage_kernel, owners),
        out_shape=[jax.ShapeDtypeStruct(block, points.dtype)] * owners,
        in_specs=[
            pl.BlockSpec(memory_space=pltpu.SMEM),
            pl.BlockSpec(memory_space=pltpu.SMEM),
            pl.BlockSpec(memory_space=pl.ANY),
        ],
        out_specs=[pl.BlockSpec(memory_space=pl.ANY)] * owners,
        scratch_shapes=[
            pltpu.SMEM((owners,), jnp.int32),
            pltpu.VMEM(block, points.dtype),
            pltpu.SemaphoreType.DMA((owners,)),
        ],
        name="stage",
    )(ids, counts, points)


def sums_kernel(blocks, replicas, parts, earlier, last, *refs):
    xs, rest = refs[:blocks], refs[blocks:]
    cents, rest = rest[0], rest[1:]
    befores, rest = rest[: parts * earlier], rest[parts * earlier :]
    outs, rest = rest[:parts], rest[parts:]
    cv, xv, lt, av, bv, ov, sx, sc, sb, so = rest
    total, feature = cv.shape
    rows = xs[0].shape[0]
    share = total // replicas
    tile = min(TILE, share)
    tiles = share // tile
    scale = 3.0 / math.sqrt(feature) * math.log2(math.e)
    me = lax.axis_index("copy")

    x_copies = [
        pltpu.make_async_copy(xs[b], xv.at[pl.ds(b * rows, rows)], sx.at[b]) for b in range(blocks)
    ]
    for copy in x_copies:
        copy.start()
    c_copies = []
    for q in range(replicas):
        start = lax.rem(me + q, replicas) * share
        for t in range(tiles):
            i = q * tiles + t
            c_copies.append(
                pltpu.make_async_copy(
                    cents.at[pl.ds(pl.multiple_of(start + t * tile, tile), tile)],
                    cv.at[pl.ds(i * tile, tile)],
                    sc.at[i],
                )
            )
    for copy in c_copies:
        copy.start()
    b_copies = []
    for e in range(earlier):
        for q in range(parts):
            i = e * parts + q
            b_copies.append(
                pltpu.make_async_copy(befores[i], bv.at[pl.ds(i * share, share)], sb.at[i])
            )
    for copy in b_copies:
        copy.start()

    out_copies = []
    for first in range(0, blocks, TURN):
        some = min(TURN, blocks - first)
        n = some * rows
        for copy in x_copies[first : first + some]:
            copy.wait()
        x = xv[pl.ds(first * rows, n), :]
        xt = x.T
        high = jnp.full((8, n), -jnp.inf, F32)
        for i in range(total // tile):
            if first == 0:
                c_copies[i].wait()
            logits = jnp.dot(cv[pl.ds(i * tile, tile), :], xt, preferred_element_type=F32)
            lt[pl.ds(i * tile, tile), pl.ds(0, n)] = logits
            high = jnp.maximum(high, jnp.max(logits.reshape(tile // 8, 8, n), axis=0))
        high = jnp.max(high, axis=0, keepdims=True) * scale
        norm = jnp.zeros((8, n), F32)
        for i in range(total // tile):
            e = jnp.exp2(lt[pl.ds(i * tile, tile), pl.ds(0, n)] * scale - high)
            lt[pl.ds(i * tile, tile), pl.ds(0, n)] = e
            norm = norm + jnp.sum(e.reshape(tile // 8, 8, n), axis=0)
        inverse = 1.0 / jnp.sum(norm, axis=0, keepdims=True)
        for q in reversed(range(parts)):
            if first == 0:
                for e in range(earlier):
                    b_copies[e * parts + q].wait()
            for t in range(tiles):
                i = q * tiles + t
                here = pl.ds(i * tile, tile)
                weights = (lt[here, pl.ds(0, n)] * inverse).astype(BF16)
                s = jnp.dot(weights, x, preferred_element_type=F32)
                if first == 0:
                    for e in range(earlier):
                        s = s + bv[pl.ds((e * parts + q) * share + t * tile, tile), :]
                else:
                    s = s + av[here, :]
                if first + some < blocks:
                    av[here, :] = s
                    continue
                if last:
                    v = s + cv[here, :].astype(F32)
                    mean = jnp.mean(v * v, axis=-1, keepdims=True)
                    ov[here, :] = (v * lax.rsqrt(mean + 1e-06)).astype(BF16)
                    source = ov
                else:
                    av[here, :] = s
                    source = av
                copy = pltpu.make_async_copy(
                    source.at[here], outs[q].at[pl.ds(t * tile, tile)], so.at[i]
                )
                copy.start()
                out_copies.append(copy)
    for copy in out_copies:
        copy.wait()


def sums(xs, centroids, befores, replicas, parts, last=False):
    blocks = len(xs)
    rows, feature = xs[0].shape
    total = centroids.shape[0]
    share = total // replicas
    tile = min(TILE, share)
    earlier = len(befores) // parts
    points = blocks * rows
    any_spec = pl.BlockSpec(memory_space=pl.ANY)
    out = jax.ShapeDtypeStruct((share, feature), BF16 if last else F32)
    small = (8, feature)
    return pl.pallas_call(
        functools.partial(sums_kernel, blocks, replicas, parts, earlier, last),
        out_shape=[out] * parts,
        in_specs=[any_spec] * (blocks + 1 + len(befores)),
        out_specs=[any_spec] * parts,
        scratch_shapes=[
            pltpu.VMEM((total, feature), BF16),
            pltpu.VMEM((points, feature), BF16),
            pltpu.VMEM((total, min(TURN, blocks) * rows), F32),
            pltpu.VMEM((parts * share, feature), F32),
            pltpu.VMEM((max(len(befores), 1) * share, feature), F32),
            pltpu.VMEM((parts * share, feature) if last else (16, feature), BF16),
            pltpu.SemaphoreType.DMA((blocks,)),
            pltpu.SemaphoreType.DMA((total // tile,)),
            pltpu.SemaphoreType.DMA((max(len(befores), 1),)),
            pltpu.SemaphoreType.DMA((parts * share // tile,)),
        ],
        compiler_params=pltpu.CompilerParams(vmem_limit_bytes=48 * MIB),
        cost_estimate=pl.CostEstimate(
            flops=2 * points * feature * (total + parts * share),
            bytes_accessed=2 * total * feature + 2 * points * feature + 4 * parts * share * feature,
            transcendentals=points * total,
        ),
        name="last_sums" if last else "sums",
    )(*xs, centroids, *befores)


def local(points, block_ids, block_counts, centroids):
    owners = lax.axis_size("cluster")
    replicas = lax.axis_size("copy")
    staged = stage(points, block_ids, block_counts, owners)

    half = owners // 2
    near, far = list(range(1, half)), list(range(half, owners))
    order = []
    for i in range(max(len(near), len(far))):
        order += far[i : i + 1] + near[i : i + 1]
    arrived = {0: staged[0]}
    for k in order:
        arrived[k] = lax.ppermute(staged[k], "cluster", pairs(k, owners))

    def others(array, r):
        return lax.ppermute(array, "copy", [(i, (i + r) % replicas) for i in range(replicas)])

    def everyone(blocks):
        return blocks + [others(b, r) for r in range(1, replicas) for b in blocks]

    cut = max(len(far) - 3, 1)
    first = [arrived[0]] + [arrived[k] for k in near]
    second = [arrived[k] for k in far[:cut]]
    third = [arrived[k] for k in far[cut:-1]]
    fourth = [arrived[far[-1]]]

    early = sums(first, centroids, [], replicas, replicas)
    early = sums(second, centroids, early, replicas, replicas)
    mine = [early[0]] + [others(early[r], r) for r in range(1, replicas)]
    mine = sums(everyone(third), centroids, mine, replicas, 1)
    return sums(everyone(fourth), centroids, mine, replicas, 1, last=True)[0]


def solution(mesh):
    return jax.shard_map(
        local,
        mesh=mesh,
        in_specs=(
            P(("cluster", "copy"), None, None),
            P(("cluster", "copy")),
            P(("cluster", "copy")),
            P("cluster", None),
        ),
        out_specs=P(("cluster", "copy"), None),
        check_vma=False,
    )
```

time: 155 us -> 152 us (0.981)
  Pallas kernels: 0 us -> 94 us
  matrix products: 35.4 us -> 0 us
  waiting for transfers between devices: 57.9 us -> 23 us
  other arithmetic: 16.6 us -> 0 us
  starting transfers between devices: 12.9 us -> 26.9 us
  between operations: 14.8 us -> 0.92 us
  local copies, waits for them, and re-layouts: 15.2 us -> 6.2 us
    pallas_call x0 -> x5, Pallas kernels: none -> 94 us  [the longest x1 61.5 us: stage(): pl.pallas_call(functools.partial(stage_kernel, owners), out_shape=[jax.Sh...]
    all_to_all x2 -> x0, waiting for transfers between devices: 44.2 us -> none  [the longest x1 44.2 us: local(): lax.all_to_all(outgoing, 'cluster', split_axis=0, concat_axis=0, tiled=True)]
    dot_general x8 -> x0, matrix products: 35.4 us -> none  [the longest x4 23.5 us: visit(): jnp.einsum('rk,rd->kd', weights, gathered, preferred_element_type=jnp.flo...]
    ppermute x0 -> x19, starting transfers between devices: none -> 26.9 us  [the longest x15 21.9 us: local(): arrived[k] = lax.ppermute(staged[k], 'cluster', pairs(k, owners))]
    ppermute x0 -> x19, waiting for transfers between devices: none -> 23 us  [the longest x15 23 us: local(): arrived[k] = lax.ppermute(staged[k], 'cluster', pairs(k, owners))]
    reduce_scatter x1 -> x0, waiting for transfers between devices: 13.8 us -> none  [local(): lax.psum_scatter(partial_sums, 'copy', scatter_dimension=0, tiled=True)]
    all_to_all x2 -> x0, starting transfers between devices: 12.9 us -> none  [the longest x1 6.55 us: local(): lax.all_to_all(present.astype(jnp.bfloat16), 'cluster', split_axis=0, con...]
    gather x5 -> x0, local copies, waits for them, and re-layouts: 10.7 us -> none  [the longest x4 8.68 us: visit(): gathered = received[chosen].reshape(turn_blocks * block_rows, feature)]
  transfers between devices with their start and end apart: 3 -> 19, of which waited for: 2 -> 8; matrix products, arithmetic and copies ran while one was open for 5% -> 0% of each run, Pallas kernels for 0% -> 12%
where the time goes in v1:
time: 152 us; the launch traced here: 151 us
  Pallas kernels  94 us (62%)
  starting transfers between devices  26.9 us (18%)
  waiting for transfers between devices  23 us (15%)
  local copies, waits for them, and re-layouts  6.2 us (4%)
    pallas_call x1, Pallas kernels, stage(): pl.pallas_call(functools.partial(stage_kernel, owners), out_shape=[jax.Sh...  61.5 us
    pallas_call x4, Pallas kernels, sums(): pl.pallas_call(functools.partial(sums_kernel, blocks, replicas, parts, ea...  32.5 us
    ppermute x15, waiting for transfers between devices, local(): arrived[k] = lax.ppermute(staged[k], 'cluster', pairs(k, owners))  23 us
    ppermute x15, starting transfers between devices, local(): arrived[k] = lax.ppermute(staged[k], 'cluster', pairs(k, owners))  21.9 us
    unnamed x18, local copies, waits for them, and re-layouts  6.2 us
    ppermute x4, starting transfers between devices, others(): lax.ppermute(array, 'copy', [(i, (i + r) % replicas) for i in range(repli...  4.95 us
  transfers between devices with their start and end apart: 19, of which 8 were waited for; matrix products, arithmetic and copies ran while one was open for 0% of the time, Pallas kernels for 12%

profile of v1, /device:TPU:17, one launch (start us, length us, event | category | flops | bytes accessed | tf_op | source)
XLA Modules:
  0.0 151.0 jit_solution(13636206380825997301)
XLA Ops:
  0.7 61.5 %stage.1 = (bf16[128,512]{1,0:T(8,128)(2,1)}, bf16[128,512]{1,0:T(8,128)(2,1)}, bf16[128,512]{1,0:T(8,128)(2,1)}, bf16[128,512]{1,0:T(8,128)(2,1)}, bf16[128,512...) custom-call(s32[16]{0:T(128)} %ids.1, ...), custom_call_target="tpu_custom_call" | custom-call | tf_op jit(solution)/shard_map/stage/pallas_call | solution.py:58
  62.2 0.1 collective-permute-start.11
  62.2 6.4 %collective-permute-start.12 = (bf16[128,512]{1,0:T(8,128)(2,1)}, bf16[128,512]{1,0:T(8,128)(2,1)S(1)}, u32[]{:S(2)}, u32[]{:S(2)}) collective-permute-start(bf16[128,512]{1,0:T(8,128)(2,1)} %get-tuple-element.35), channel_id=1, source_target_pairs={{0,4},{2,6},{4,0},{6,2},{8,12},{10,14},{12,8},{14,10},{16,20},{18,... | collective-permute-start | bytes 393224 | tf_op jit(solution)/shard_map/ppermute | solution.py:225
  68.7 0.0 collective-permute-start.13
  68.7 0.0 collective-permute-start.14
  68.7 2.4 %collective-permute-start.15 = (bf16[128,512]{1,0:T(8,128)(2,1)}, bf16[128,512]{1,0:T(8,128)(2,1)S(1)}, u32[]{:S(2)}, u32[]{:S(2)}) collective-permute-start(bf16[128,512]{1,0:T(8,128)(2,1)} %get-tuple-element.38), channel_id=1, source_target_pairs={{0,10},{2,8},{4,14},{6,12},{8,2},{10,0},{12,6},{14,4},{16,26},{18,... | collective-permute-start | bytes 393224 | tf_op jit(solution)/shard_map/ppermute | solution.py:225
  71.0 0.0 collective-permute-done.11.refs_1_
  71.0 1.2 collective-permute-start.16
  72.2 2.3 %collective-permute-done.12.refs_2_ = bf16[128,512]{1,0:T(8,128)(2,1)S(1)} collective-permute-done((bf16[128,512]{1,0:T(8,128)(2,1)}, bf16[128,512]{1,0:T(8,128)(2,1)S(1)}, u32[]{:S(2)}, u32[]{:S(2)}) %collective-permute-start.12) | collective-permute-done | bytes 131104 | tf_op jit(solution)/shard_map/ppermute | solution.py:225
  74.5 0.0 collective-permute-start.17
  74.6 0.6 collective-permute-done.13.refs_3_
  75.1 0.5 collective-permute-start.10
  75.7 0.0 collective-permute-done.14.refs_4_
  75.7 2.7 %collective-permute-start.6 = (bf16[128,512]{1,0:T(8,128)(2,1)}, bf16[128,512]{1,0:T(8,128)(2,1)S(1)}, u32[]{:S(2)}, u32[]{:S(2)}) collective-permute-start(bf16[128,512]{1,0:T(8,128)(2,1)} %get-tuple-element.28), channel_id=1, source_target_pairs={{0,16},{2,18},{4,20},{6,22},{8,24},{10,26},{12,28},{14,30},{16,0},... | collective-permute-start | bytes 393224 | tf_op jit(solution)/shard_map/ppermute | solution.py:225
  78.4 0.0 collective-permute-done.15.refs_5_
  78.4 2.6 %collective-permute-start.7 = (bf16[128,512]{1,0:T(8,128)(2,1)}, bf16[128,512]{1,0:T(8,128)(2,1)S(1)}, u32[]{:S(2)}, u32[]{:S(2)}) collective-permute-start(bf16[128,512]{1,0:T(8,128)(2,1)} %get-tuple-element.29), channel_id=1, source_target_pairs={{0,18},{2,16},{4,22},{6,20},{8,26},{10,24},{12,30},{14,28},{16,2},... | collective-permute-start | bytes 393224 | tf_op jit(solution)/shard_map/ppermute | solution.py:225
  80.9 0.0 collective-permute-done.16.refs_6_
  80.9 1.3 collective-permute-start.8
  82.3 1.9 %collective-permute-done.17.refs_7_ = bf16[128,512]{1,0:T(8,128)(2,1)S(1)} collective-permute-done((bf16[128,512]{1,0:T(8,128)(2,1)}, bf16[128,512]{1,0:T(8,128)(2,1)S(1)}, u32[]{:S(2)}, u32[]{:S(2)}) %collective-permute-start.17) | collective-permute-done | bytes 131104 | tf_op jit(solution)/shard_map/ppermute | solution.py:225
  84.2 0.7 collective-permute-start.9
  84.9 0.9 copy-done.2
  85.8 11.7 %sums.3 = (f32[1024,512]{1,0:T(8,128)S(1)}, f32[1024,512]{1,0:T(8,128)S(1)}) custom-call(bf16[128,512]{1,0:T(8,128)(2,1)S(1)} %copy-done.2, bf16[128,512]{1,0:T(8,128)(2,1)S(1)} %collective-permute-done.11.refs_1_, bf16[128,512]{1,0:T(8,128)(2,1)S(1)} %collective-permute-done.12.refs_2_, bf16[128,512]{1,0:T(8,128)(2,1)S(1)} %collective-permute-done.13.refs_3_, ...), custom_call_target="tpu_custom_call" | custom-call | flops 4294967296 | bytes 7340032 | tf_op jit(solution)/shard_map/sums/pallas_call | solution.py:186
  97.5 1.3 copy-done.3
  98.9 1.3 copy-done.4
  100.2 0.0 collective-permute-done.10.refs_4_
  100.2 0.0 collective-permute-done.6.refs_0_
  100.2 0.0 collective-permute-done.7.refs_1_
  100.2 1.4 collective-permute-done.8.refs_2_
  101.6 2.8 %collective-permute-done.9.refs_3_ = bf16[128,512]{1,0:T(8,128)(2,1)S(1)} collective-permute-done((bf16[128,512]{1,0:T(8,128)(2,1)}, bf16[128,512]{1,0:T(8,128)(2,1)S(1)}, u32[]{:S(2)}, u32[]{:S(2)}) %collective-permute-start.9) | collective-permute-done | bytes 131104 | tf_op jit(solution)/shard_map/ppermute | solution.py:225
  104.4 9.7 %sums.4 = (f32[1024,512]{1,0:T(8,128)S(1)}, f32[1024,512]{1,0:T(8,128)S(1)}) custom-call(bf16[128,512]{1,0:T(8,128)(2,1)S(1)} %collective-permute-done.6.refs_0_, bf16[128,512]{1,0:T(8,128)(2,1)S(1)} %collective-permute-done.7.refs_1_, bf16[128,512]{1,0:T(8,128)(2,1)S(1)} %collective-permute-done.8.refs_2_, ...), custom_call_target="tpu_custom_call" | custom-call | flops 2684354560 | bytes 6946816 | tf_op jit(solution)/shard_map/sums/pallas_call | solution.py:186
  114.1 1.3 copy-done.1
  115.5 1.9 %collective-permute-start.18 = (f32[1024,512]{1,0:T(8,128)S(1)}, f32[1024,512]{1,0:T(8,128)S(1)}, u32[]{:S(2)}, u32[]{:S(2)}) collective-permute-start(f32[1024,512]{1,0:T(8,128)S(1)} %get-tuple-element.44), channel_id=1, source_target_pairs={{0,1},{1,0},{2,3},{3,2},{4,5},{5,4},{6,7},{7,6},{8,9},{9,8},{10,11... | collective-permute-start | bytes 6291464 | tf_op jit(solution)/shard_map/ppermute | solution.py:228
  117.4 0.7 collective-permute-start.2
  118.1 1.7 %collective-permute-start.3 = (bf16[128,512]{1,0:T(8,128)(2,1)S(1)}, bf16[128,512]{1,0:T(8,128)(2,1)S(1)}, u32[]{:S(2)}, u32[]{:S(2)}) collective-permute-start(bf16[128,512]{1,0:T(8,128)(2,1)S(1)} %copy-done.7), channel_id=1, source_target_pairs={{0,28},{2,30},{4,24},{6,26},{8,20},{10,22},{12,16},{14,18},{16,12}... | collective-permute-start | bytes 393224 | tf_op jit(solution)/shard_map/ppermute | solution.py:225
  119.8 1.6 %collective-permute-start = (bf16[128,512]{1,0:T(8,128)(2,1)S(1)}, bf16[128,512]{1,0:T(8,128)(2,1)S(1)}, u32[]{:S(2)}, u32[]{:S(2)}) collective-permute-start(bf16[128,512]{1,0:T(8,128)(2,1)S(1)} %copy-done.6), channel_id=1, source_target_pairs={{0,30},{2,28},{4,26},{6,24},{8,22},{10,20},{12,18},{14,16},{16,14}... | collective-permute-start | bytes 393224 | tf_op jit(solution)/shard_map/ppermute | solution.py:225
  121.4 2.0 %collective-permute-done.2.refs_0_ = bf16[128,512]{1,0:T(8,128)(2,1)S(1)} collective-permute-done((bf16[128,512]{1,0:T(8,128)(2,1)S(1)}, bf16[128,512]{1,0:T(8,128)(2,1)S(1)}, u32[]{:S(2)}, u32[]{:S(2)}) %collective-permute-start.2) | collective-permute-done | bytes 131104 | tf_op jit(solution)/shard_map/ppermute | solution.py:225
  123.4 1.2 collective-permute-start.4
  124.6 10.1 %collective-permute-done.3.refs_1_ = bf16[128,512]{1,0:T(8,128)(2,1)S(1)} collective-permute-done((bf16[128,512]{1,0:T(8,128)(2,1)S(1)}, bf16[128,512]{1,0:T(8,128)(2,1)S(1)}, u32[]{:S(2)}, u32[]{:S(2)}) %collective-permute-start.3) | collective-permute-done | bytes 131104 | tf_op jit(solution)/shard_map/ppermute | solution.py:225
  134.7 1.2 collective-permute-start.5
  135.9 1.9 %collective-permute-done.refs_0_ = bf16[128,512]{1,0:T(8,128)(2,1)S(1)} collective-permute-done((bf16[128,512]{1,0:T(8,128)(2,1)S(1)}, bf16[128,512]{1,0:T(8,128)(2,1)S(1)}, u32[]{:S(2)}, u32[]{:S(2)}) %collective-permute-start) | collective-permute-done | bytes 131104 | tf_op jit(solution)/shard_map/ppermute | solution.py:225
  137.8 0.7 collective-permute-start.1
  138.5 0.0 collective-permute-done.4.refs_2_
  138.5 0.0 collective-permute-done.5.refs_3_
  138.5 0.0 collective-permute-done.18.refs_6_
  138.5 1.3 copy-done.5
  139.8 5.9 %sums.5.refs_3_ = f32[1024,512]{1,0:T(8,128)S(1)} custom-call(bf16[128,512]{1,0:T(8,128)(2,1)S(1)} %collective-permute-done.2.refs_0_, bf16[128,512]{1,0:T(8,128)(2,1)S(1)} %collective-permute-done.3.refs_1_, bf16[128,512]{1,0:T(8,128)(2,1)S(1)} %collective-permute-done.4.refs_2_, bf16[128,512]{1,0:T(8,128)(2,1)S(1)} %collective-permute-done.5.refs_3_, ...), custom_call_target="tpu_custom_call" | custom-call | flops 1610612736 | bytes 4718592 | tf_op jit(solution)/shard_map/sums/pallas_call | solution.py:186
  145.7 0.0 collective-permute-done.1.refs_1_
  145.7 5.2 %last_sums.1 = bf16[1024,512]{1,0:T(8,128)(2,1)} custom-call(bf16[128,512]{1,0:T(8,128)(2,1)S(1)} %collective-permute-done.refs_0_, bf16[128,512]{1,0:T(8,128)(2,1)S(1)} %collective-permute-done.1.refs_1_, bf16[2048,512]{1,0:T(8,128)(2,1)S(1)} %copy-done, f32[1024,512]{1,0:T(8,128)S(1)} %sums.5.refs_3_), custom_call_target="tpu_custom_call" | custom-call | flops 805306368 | bytes 4456448 | tf_op jit(solution)/shard_map/last_sums/pallas_call | solution.py:186
  (13 shorter events, 0.0 us)
Async XLA Ops:
  62.2 8.9 %collective-permute-start.11 = (bf16[128,512]{1,0:T(8,128)(2,1)}, bf16[128,512]{1,0:T(8,128)(2,1)S(1)}, u32[]{:S(2)}, u32[]{:S(2)}) collective-permute-start(bf16[128,512]{1,0:T(8,128)(2,1)} %get-tuple-element.34), channel_id=1, source_target_pairs={{0,2},{2,0},{4,6},{6,4},{8,10},{10,8},{12,14},{14,12},{16,18},{18,... | collective-permute-start | bytes 393224 | tf_op jit(solution)/shard_map/ppermute | solution.py:225
  62.2 12.3 %collective-permute-start.12 = (bf16[128,512]{1,0:T(8,128)(2,1)}, bf16[128,512]{1,0:T(8,128)(2,1)S(1)}, u32[]{:S(2)}, u32[]{:S(2)}) collective-permute-start(bf16[128,512]{1,0:T(8,128)(2,1)} %get-tuple-element.35), channel_id=1, source_target_pairs={{0,4},{2,6},{4,0},{6,2},{8,12},{10,14},{12,8},{14,10},{16,20},{18,... | collective-permute-start | bytes 393224 | tf_op jit(solution)/shard_map/ppermute | solution.py:225
  68.7 6.5 %collective-permute-start.13 = (bf16[128,512]{1,0:T(8,128)(2,1)}, bf16[128,512]{1,0:T(8,128)(2,1)S(1)}, u32[]{:S(2)}, u32[]{:S(2)}) collective-permute-start(bf16[128,512]{1,0:T(8,128)(2,1)} %get-tuple-element.36), channel_id=1, source_target_pairs={{0,6},{2,4},{4,2},{6,0},{8,14},{10,12},{12,10},{14,8},{16,22},{18,... | collective-permute-start | bytes 393224 | tf_op jit(solution)/shard_map/ppermute | solution.py:225
  68.7 7.0 %collective-permute-start.14 = (bf16[128,512]{1,0:T(8,128)(2,1)}, bf16[128,512]{1,0:T(8,128)(2,1)S(1)}, u32[]{:S(2)}, u32[]{:S(2)}) collective-permute-start(bf16[128,512]{1,0:T(8,128)(2,1)} %get-tuple-element.37), channel_id=1, source_target_pairs={{0,8},{2,10},{4,12},{6,14},{8,0},{10,2},{12,4},{14,6},{16,24},{18,... | collective-permute-start | bytes 393224 | tf_op jit(solution)/shard_map/ppermute | solution.py:225
  68.7 9.7 %collective-permute-start.15 = (bf16[128,512]{1,0:T(8,128)(2,1)}, bf16[128,512]{1,0:T(8,128)(2,1)S(1)}, u32[]{:S(2)}, u32[]{:S(2)}) collective-permute-start(bf16[128,512]{1,0:T(8,128)(2,1)} %get-tuple-element.38), channel_id=1, source_target_pairs={{0,10},{2,8},{4,14},{6,12},{8,2},{10,0},{12,6},{14,4},{16,26},{18,... | collective-permute-start | bytes 393224 | tf_op jit(solution)/shard_map/ppermute | solution.py:225
  71.0 9.9 %collective-permute-start.16 = (bf16[128,512]{1,0:T(8,128)(2,1)}, bf16[128,512]{1,0:T(8,128)(2,1)S(1)}, u32[]{:S(2)}, u32[]{:S(2)}) collective-permute-start(bf16[128,512]{1,0:T(8,128)(2,1)} %get-tuple-element.39), channel_id=1, source_target_pairs={{0,12},{2,14},{4,8},{6,10},{8,4},{10,6},{12,0},{14,2},{16,28},{18,... | collective-permute-start | bytes 393224 | tf_op jit(solution)/shard_map/ppermute | solution.py:225
  74.5 9.6 %collective-permute-start.17 = (bf16[128,512]{1,0:T(8,128)(2,1)}, bf16[128,512]{1,0:T(8,128)(2,1)S(1)}, u32[]{:S(2)}, u32[]{:S(2)}) collective-permute-start(bf16[128,512]{1,0:T(8,128)(2,1)} %get-tuple-element.40), channel_id=1, source_target_pairs={{0,14},{2,12},{4,10},{6,8},{8,6},{10,4},{12,2},{14,0},{16,30},{18,... | collective-permute-start | bytes 393224 | tf_op jit(solution)/shard_map/ppermute | solution.py:225
  75.1 25.0 %collective-permute-start.10 = (bf16[128,512]{1,0:T(8,128)(2,1)}, bf16[128,512]{1,0:T(8,128)(2,1)S(1)}, u32[]{:S(2)}, u32[]{:S(2)}) collective-permute-start(bf16[128,512]{1,0:T(8,128)(2,1)} %get-tuple-element.32), channel_id=1, source_target_pairs={{0,24},{2,26},{4,28},{6,30},{8,16},{10,18},{12,20},{14,22},{16,8},... | collective-permute-start | bytes 393224 | tf_op jit(solution)/shard_map/ppermute | solution.py:225
  75.7 24.5 %collective-permute-start.6 = (bf16[128,512]{1,0:T(8,128)(2,1)}, bf16[128,512]{1,0:T(8,128)(2,1)S(1)}, u32[]{:S(2)}, u32[]{:S(2)}) collective-permute-start(bf16[128,512]{1,0:T(8,128)(2,1)} %get-tuple-element.28), channel_id=1, source_target_pairs={{0,16},{2,18},{4,20},{6,22},{8,24},{10,26},{12,28},{14,30},{16,0},... | collective-permute-start | bytes 393224 | tf_op jit(solution)/shard_map/ppermute | solution.py:225
  78.4 21.8 %collective-permute-start.7 = (bf16[128,512]{1,0:T(8,128)(2,1)}, bf16[128,512]{1,0:T(8,128)(2,1)S(1)}, u32[]{:S(2)}, u32[]{:S(2)}) collective-permute-start(bf16[128,512]{1,0:T(8,128)(2,1)} %get-tuple-element.29), channel_id=1, source_target_pairs={{0,18},{2,16},{4,22},{6,20},{8,26},{10,24},{12,30},{14,28},{16,2},... | collective-permute-start | bytes 393224 | tf_op jit(solution)/shard_map/ppermute | solution.py:225
  80.9 20.6 %collective-permute-start.8 = (bf16[128,512]{1,0:T(8,128)(2,1)}, bf16[128,512]{1,0:T(8,128)(2,1)S(1)}, u32[]{:S(2)}, u32[]{:S(2)}) collective-permute-start(bf16[128,512]{1,0:T(8,128)(2,1)} %get-tuple-element.30), channel_id=1, source_target_pairs={{0,20},{2,22},{4,16},{6,18},{8,28},{10,30},{12,24},{14,26},{16,4},... | collective-permute-start | bytes 393224 | tf_op jit(solution)/shard_map/ppermute | solution.py:225
  84.2 20.2 %collective-permute-start.9 = (bf16[128,512]{1,0:T(8,128)(2,1)}, bf16[128,512]{1,0:T(8,128)(2,1)S(1)}, u32[]{:S(2)}, u32[]{:S(2)}) collective-permute-start(bf16[128,512]{1,0:T(8,128)(2,1)} %get-tuple-element.31), channel_id=1, source_target_pairs={{0,22},{2,20},{4,18},{6,16},{8,30},{10,28},{12,26},{14,24},{16,6},... | collective-permute-start | bytes 393224 | tf_op jit(solution)/shard_map/ppermute | solution.py:225
  84.9 0.9 copy-start.2
  97.5 1.4 copy-start.3
  98.9 1.3 copy-start.4
  104.4 13.0 %copy-start.8 = (bf16[128,512]{1,0:T(8,128)(2,1)S(1)}, bf16[128,512]{1,0:T(8,128)(2,1)}, u32[]{:S(2)}) copy-start(bf16[128,512]{1,0:T(8,128)(2,1)} %get-tuple-element.26) | copy-start | bytes 393220
  104.4 13.7 %copy-start.7 = (bf16[128,512]{1,0:T(8,128)(2,1)S(1)}, bf16[128,512]{1,0:T(8,128)(2,1)}, u32[]{:S(2)}) copy-start(bf16[128,512]{1,0:T(8,128)(2,1)} %get-tuple-element.27) | copy-start | bytes 393220
  104.4 15.4 %copy-start.6 = (bf16[128,512]{1,0:T(8,128)(2,1)S(1)}, bf16[128,512]{1,0:T(8,128)(2,1)}, u32[]{:S(2)}) copy-start(bf16[128,512]{1,0:T(8,128)(2,1)} %get-tuple-element.25) | copy-start | bytes 393220
  104.4 35.4 %copy-start = (bf16[2048,512]{1,0:T(8,128)(2,1)S(1)}, bf16[2048,512]{1,0:T(8,128)(2,1)}, u32[]{:S(2)}) copy-start(bf16[2048,512]{1,0:T(8,128)(2,1)} %refs_2_.1) | copy-start | bytes 6291460
  114.1 1.4 copy-start.1
  115.5 23.0 %collective-permute-start.18 = (f32[1024,512]{1,0:T(8,128)S(1)}, f32[1024,512]{1,0:T(8,128)S(1)}, u32[]{:S(2)}, u32[]{:S(2)}) collective-permute-start(f32[1024,512]{1,0:T(8,128)S(1)} %get-tuple-element.44), channel_id=1, source_target_pairs={{0,1},{1,0},{2,3},{3,2},{4,5},{5,4},{6,7},{7,6},{8,9},{9,8},{10,11... | collective-permute-start | bytes 6291464 | tf_op jit(solution)/shard_map/ppermute | solution.py:228
  117.4 6.0 %collective-permute-start.2 = (bf16[128,512]{1,0:T(8,128)(2,1)S(1)}, bf16[128,512]{1,0:T(8,128)(2,1)S(1)}, u32[]{:S(2)}, u32[]{:S(2)}) collective-permute-start(bf16[128,512]{1,0:T(8,128)(2,1)S(1)} %copy-done.8), channel_id=1, source_target_pairs={{0,26},{2,24},{4,30},{6,28},{8,18},{10,16},{12,22},{14,20},{16,10}... | collective-permute-start | bytes 393224 | tf_op jit(solution)/shard_map/ppermute | solution.py:225
  118.1 16.6 %collective-permute-start.3 = (bf16[128,512]{1,0:T(8,128)(2,1)S(1)}, bf16[128,512]{1,0:T(8,128)(2,1)S(1)}, u32[]{:S(2)}, u32[]{:S(2)}) collective-permute-start(bf16[128,512]{1,0:T(8,128)(2,1)S(1)} %copy-done.7), channel_id=1, source_target_pairs={{0,28},{2,30},{4,24},{6,26},{8,20},{10,22},{12,16},{14,18},{16,12}... | collective-permute-start | bytes 393224 | tf_op jit(solution)/shard_map/ppermute | solution.py:225
  119.8 17.9 %collective-permute-start = (bf16[128,512]{1,0:T(8,128)(2,1)S(1)}, bf16[128,512]{1,0:T(8,128)(2,1)S(1)}, u32[]{:S(2)}, u32[]{:S(2)}) collective-permute-start(bf16[128,512]{1,0:T(8,128)(2,1)S(1)} %copy-done.6), channel_id=1, source_target_pairs={{0,30},{2,28},{4,26},{6,24},{8,22},{10,20},{12,18},{14,16},{16,14}... | collective-permute-start | bytes 393224 | tf_op jit(solution)/shard_map/ppermute | solution.py:225
  123.4 15.1 %collective-permute-start.4 = (bf16[128,512]{1,0:T(8,128)(2,1)S(1)}, bf16[128,512]{1,0:T(8,128)(2,1)S(1)}, u32[]{:S(2)}, u32[]{:S(2)}) collective-permute-start(bf16[128,512]{1,0:T(8,128)(2,1)S(1)} %collective-permute-done.2.refs_0_), channel_id=1, source_target_pairs={{0,1},{1,0},{2,3},{3,2},{4,5},{5,4},{6,7},{7,6},{8,9},{9,8},{10,11... | collective-permute-start | bytes 393224 | tf_op jit(solution)/shard_map/ppermute | solution.py:228
  134.7 3.8 %collective-permute-start.5 = (bf16[128,512]{1,0:T(8,128)(2,1)S(1)}, bf16[128,512]{1,0:T(8,128)(2,1)S(1)}, u32[]{:S(2)}, u32[]{:S(2)}) collective-permute-start(bf16[128,512]{1,0:T(8,128)(2,1)S(1)} %collective-permute-done.3.refs_1_), channel_id=1, source_target_pairs={{0,1},{1,0},{2,3},{3,2},{4,5},{5,4},{6,7},{7,6},{8,9},{9,8},{10,11... | collective-permute-start | bytes 393224 | tf_op jit(solution)/shard_map/ppermute | solution.py:228
  137.8 8.0 %collective-permute-start.1 = (bf16[128,512]{1,0:T(8,128)(2,1)S(1)}, bf16[128,512]{1,0:T(8,128)(2,1)S(1)}, u32[]{:S(2)}, u32[]{:S(2)}) collective-permute-start(bf16[128,512]{1,0:T(8,128)(2,1)S(1)} %collective-permute-done.refs_0_), channel_id=1, source_target_pairs={{0,1},{1,0},{2,3},{3,2},{4,5},{5,4},{6,7},{7,6},{8,9},{9,8},{10,11... | collective-permute-start | bytes 393224 | tf_op jit(solution)/shard_map/ppermute | solution.py:228
  138.5 1.3 copy-start.5

commit v2 on v0

v2 whole, which is shorter than its diff:
```python
import functools
import math

import jax
import jax.numpy as jnp
from jax import lax
from jax.experimental import pallas as pl
from jax.experimental.pallas import tpu as pltpu
from jax.sharding import PartitionSpec as P

F32 = jnp.float32
BF16 = jnp.bfloat16
TILE = 256
TURN = 4
MIB = 1 << 20


def in_hbm(array):
    return pltpu.with_memory_space_constraint(array, pltpu.HBM)


def in_vmem(array):
    return pltpu.with_memory_space_constraint(array, pltpu.VMEM)


def after(array, *others):
    return lax.optimization_barrier((array, *others))[0]


def stage_kernel(offsets, ids_in, counts, points, *refs):
    owners = len(offsets)
    outs, (where, ids, held, zeros, reads, writes, small) = refs[:owners], refs[owners:]
    slots = points.shape[0]
    me = lax.axis_index("cluster")
    ids_copy = pltpu.make_async_copy(ids_in, ids, small)
    ids_copy.start()
    for o in range(owners):
        where[o] = -1
    zeros[...] = jnp.zeros_like(zeros)
    ids_copy.wait()
    for s in range(slots):

        @pl.when(s < counts[0])
        def _():
            where[ids[s]] = s

    for i, k in enumerate(offsets):
        slot = where[me ^ k]

        @pl.when(slot >= 0)
        def _():
            pltpu.make_async_copy(points.at[jnp.maximum(slot, 0)], held.at[i], reads.at[i]).start()

        @pl.when(slot < 0)
        def _():
            pltpu.make_async_copy(zeros, outs[i], writes.at[i]).start()

    for i, k in enumerate(offsets):

        @pl.when(where[me ^ k] >= 0)
        def _():
            pltpu.make_async_copy(points.at[0], held.at[i], reads.at[i]).wait()
            pltpu.make_async_copy(held.at[i], outs[i], writes.at[i]).start()

    for i in range(owners):
        pltpu.make_async_copy(zeros, outs[i], writes.at[i]).wait()


def stage(points, ids, counts, offsets):
    block = points.shape[1:]
    owners = len(offsets)
    spec = pl.BlockSpec(memory_space=pltpu.HBM)
    outs = pl.pallas_call(
        functools.partial(stage_kernel, offsets),
        out_shape=[pltpu.HBM(block, points.dtype)] * owners,
        in_specs=[spec, pl.BlockSpec(memory_space=pltpu.SMEM), spec],
        out_specs=[spec] * owners,
        scratch_shapes=[
            pltpu.SMEM((owners,), jnp.int32),
            pltpu.SMEM(ids.shape, jnp.int32),
            pltpu.VMEM((owners, *block), points.dtype),
            pltpu.VMEM(block, points.dtype),
            pltpu.SemaphoreType.DMA((owners,)),
            pltpu.SemaphoreType.DMA((owners,)),
            pltpu.SemaphoreType.DMA,
        ],
        compiler_params=pltpu.CompilerParams(vmem_limit_bytes=16 * MIB),
        name="stage",
    )(in_hbm(ids), counts, in_hbm(points))
    return dict(zip(offsets, outs))


def sums_kernel(blocks, replicas, send, *refs):
    xs, rest = refs[:blocks], refs[blocks:]
    cents, rest = rest[0], rest[1:]
    befores, outs, lt = rest[: -replicas - 1], rest[-replicas - 1 : -1], rest[-1]
    total, feature = cents.shape
    rows = xs[0].shape[0]
    share = total // replicas
    tile = min(TILE, share)
    scale = 3.0 / math.sqrt(feature) * math.log2(math.e)
    me = lax.axis_index("copy")

    for first in range(0, blocks, TURN):
        some = min(TURN, blocks - first)
        n = some * rows
        x = jnp.concatenate([r[...] for r in xs[first : first + some]], axis=0)
        xt = x.T
        high = jnp.full((8, n), -jnp.inf, F32)
        for i in range(total // tile):
            here = pl.ds(i * tile, tile)
            logits = jnp.dot(cents[here, :], xt, preferred_element_type=F32)
            lt[here, pl.ds(0, n)] = logits
            high = jnp.maximum(high, jnp.max(logits.reshape(tile // 8, 8, n), axis=0))
        high = jnp.max(high, axis=0, keepdims=True) * scale
        norm = jnp.zeros((8, n), F32)
        for i in range(total // tile):
            here = pl.ds(i * tile, tile)
            e = jnp.exp2(lt[here, pl.ds(0, n)] * scale - high)
            lt[here, pl.ds(0, n)] = e
            norm = norm + jnp.sum(e.reshape(tile // 8, 8, n), axis=0)
        inverse = 1.0 / jnp.sum(norm, axis=0, keepdims=True)
        for q in range(replicas):
            start = lax.rem(me + q, replicas) * share
            for t in range(share // tile):
                here = pl.ds(pl.multiple_of(start + t * tile, tile), tile)
                there = pl.ds(t * tile, tile)
                weights = (lt[here, pl.ds(0, n)] * inverse).astype(BF16)
                s = jnp.dot(weights, x, preferred_element_type=F32)
                if first:
                    s = s + outs[q][there, :]
                elif befores:
                    s = s + befores[q][there, :]
                outs[q][there, :] = s.astype(outs[q].dtype)


def sums(xs, centroids, befores, replicas, send=False):
    blocks = len(xs)
    assert blocks <= TURN or not send
    rows, feature = xs[0].shape
    total = centroids.shape[0]
    share = total // replicas
    points = blocks * rows
    spec = pl.BlockSpec(memory_space=pltpu.VMEM)
    outs = [
        jax.ShapeDtypeStruct((share, feature), BF16 if send and q else F32) for q in range(replicas)
    ]
    return pl.pallas_call(
        functools.partial(sums_kernel, blocks, replicas, send),
        out_shape=outs,
        in_specs=[spec] * (blocks + 1 + len(befores)),
        out_specs=[spec] * replicas,
        scratch_shapes=[pltpu.VMEM((total, min(TURN, blocks) * rows), F32)],
        compiler_params=pltpu.CompilerParams(vmem_limit_bytes=28 * MIB),
        cost_estimate=pl.CostEstimate(flops=1024, bytes_accessed=1024, transcendentals=0),
        name="sums",
    )(*xs, centroids, *befores)


def close_kernel(cents, *refs):
    terms, out = refs[:-1], refs[-1]
    share, feature = out.shape
    start = lax.axis_index("copy") * share
    tile = min(TILE, share)
    for t in range(share // tile):
        there = pl.ds(t * tile, tile)
        v = cents[pl.ds(pl.multiple_of(start + t * tile, tile), tile), :].astype(F32)
        for term in terms:
            v = v + term[there, :].astype(F32)
        mean = jnp.mean(v * v, axis=-1, keepdims=True)
        out[there, :] = (v * lax.rsqrt(mean + 1e-06)).astype(BF16)


def close(centroids, terms):
    spec = pl.BlockSpec(memory_space=pltpu.VMEM)
    share, feature = terms[0].shape
    return pl.pallas_call(
        close_kernel,
        out_shape=jax.ShapeDtypeStruct((share, feature), BF16),
        in_specs=[spec] * (1 + len(terms)),
        out_specs=spec,
        compiler_params=pltpu.CompilerParams(vmem_limit_bytes=28 * MIB),
        cost_estimate=pl.CostEstimate(
            flops=8 * share * feature, bytes_accessed=12 * share * feature, transcendentals=share
        ),
        name="close",
    )(centroids, *terms)


def plan(owners):
    half = owners // 2
    near, far = list(range(1, half)), list(range(half, owners))
    groups = [[0] + near[:2]]
    rest = near[2:]
    for i in range(0, len(far) - 2, 2):
        groups.append(far[i : i + 1] + rest[:1] + far[i + 1 : i + 2] + rest[1:2])
        rest = rest[2:]
    return near, far, groups + [[k] for k in far[-2:]]


def local(points, block_ids, block_counts, centroids):
    owners = lax.axis_size("cluster")
    replicas = lax.axis_size("copy")
    assert owners >= 16 and owners & (owners - 1) == 0
    near, far, groups = plan(owners)
    first = [k for pair in zip(far, near) for k in pair]
    rest = [k for k in range(owners) if k not in first]
    staged = stage(points, block_ids, block_counts, first + rest)
    arrived = {0: staged[0]}

    def send(k, *others):
        block = after(staged[k], *others) if others else staged[k]
        arrived[k] = lax.ppermute(block, "cluster", [(d, d ^ k) for d in range(owners)])

    for i, k in enumerate(near):
        send(k, *[arrived[j] for j in near[max(i - 2, 0) : max(i - 1, 0)]])
    for k in far[:3]:
        send(k)
    total, sent = [], 3
    for g, group in enumerate(groups):
        while sent < min(2 * g + 4, len(far)) and g:
            others = [arrived[far[sent - 3]]]
            if sent == 4:
                others.append(arrived[near[3]])
            if sent % 2 == 0 and sent > 4 or sent == 3:
                others.append(total[0])
            send(far[sent], *others)
            sent += 1
        blocks = [arrived[k] for k in group]
        total = sums(blocks, centroids, total, replicas, g == len(groups) - 1)
    received = [
        lax.ppermute(total[r], "copy", [(i, (i + r) % replicas) for i in range(replicas)])
        for r in range(1, replicas)
    ]
    return close(centroids, [total[0]] + received)


def solution(mesh):
    return jax.shard_map(
        local,
        mesh=mesh,
        in_specs=(
            P(("cluster", "copy"), None, None),
            P(("cluster", "copy")),
            P(("cluster", "copy")),
            P("cluster", None),
        ),
        out_specs=P(("cluster", "copy"), None),
        check_vma=False,
    )
```

time: 155 us -> 62.5 us (0.40)
  waiting for transfers between devices: 57.9 us -> 12.9 us
  matrix products: 35.4 us -> 0 us
  Pallas kernels: 0 us -> 20.4 us
  other arithmetic: 16.6 us -> 0 us
  local copies, waits for them, and re-layouts: 15.2 us -> 0.94 us
  between operations: 14.8 us -> 0.96 us
  starting transfers between devices: 12.9 us -> 26.5 us
    all_to_all x2 -> x0, waiting for transfers between devices: 44.2 us -> none  [the longest x1 44.2 us: local(): lax.all_to_all(outgoing, 'cluster', split_axis=0, concat_axis=0, tiled=True)]
    dot_general x8 -> x0, matrix products: 35.4 us -> none  [the longest x4 23.5 us: visit(): jnp.einsum('rk,rd->kd', weights, gathered, preferred_element_type=jnp.flo...]
    ppermute x0 -> x16, starting transfers between devices: none -> 26.5 us  [the longest x15 24.6 us: send(): lax.ppermute(block, 'cluster', [(d, d ^ k) for d in range(owners)])]
    pallas_call x0 -> x8, Pallas kernels: none -> 20.4 us  [the longest x6 15.6 us: sums(): pl.pallas_call(functools.partial(sums_kernel, blocks, replicas, send), ou...]
    reduce_scatter x1 -> x0, waiting for transfers between devices: 13.8 us -> none  [local(): lax.psum_scatter(partial_sums, 'copy', scatter_dimension=0, tiled=True)]
    ppermute x0 -> x16, waiting for transfers between devices: none -> 12.9 us  [the longest x15 10.6 us: send(): lax.ppermute(block, 'cluster', [(d, d ^ k) for d in range(owners)])]
    all_to_all x2 -> x0, starting transfers between devices: 12.9 us -> none  [the longest x1 6.55 us: local(): lax.all_to_all(present.astype(jnp.bfloat16), 'cluster', split_axis=0, con...]
    gather x5 -> x0, local copies, waits for them, and re-layouts: 10.7 us -> none  [the longest x4 8.68 us: visit(): gathered = received[chosen].reshape(turn_blocks * block_rows, feature)]
  transfers between devices with their start and end apart: 3 -> 16, of which waited for: 2 -> 6; matrix products, arithmetic and copies ran while one was open for 5% -> 0% of each run, Pallas kernels for 0% -> 23%
where the time goes in v2:
time: 62.5 us; the launch traced here: 61.7 us
  starting transfers between devices  26.5 us (42%)
  Pallas kernels  20.4 us (33%)
  waiting for transfers between devices  12.9 us (21%)
  between operations  0.96 us (2%)
  local copies, waits for them, and re-layouts  0.94 us (2%)
    ppermute x15, starting transfers between devices, send(): lax.ppermute(block, 'cluster', [(d, d ^ k) for d in range(owners)])  24.6 us
    pallas_call x6, Pallas kernels, sums(): pl.pallas_call(functools.partial(sums_kernel, blocks, replicas, send), ou...  15.6 us
    ppermute x15, waiting for transfers between devices, send(): lax.ppermute(block, 'cluster', [(d, d ^ k) for d in range(owners)])  10.6 us
    pallas_call x1, Pallas kernels, stage(): pl.pallas_call(functools.partial(stage_kernel, offsets), out_shape=[pltpu...  3.29 us
    ppermute x1, waiting for transfers between devices, local(): lax.ppermute(total[r], 'copy', [(i, (i + r) % replicas) for i in range(re...  2.29 us
    ppermute x1, starting transfers between devices, local(): lax.ppermute(total[r], 'copy', [(i, (i + r) % replicas) for i in range(re...  1.9 us
    pallas_call x1, Pallas kernels, close(): pl.pallas_call(close_kernel, out_shape=jax.ShapeDtypeStruct((share, featu...  1.52 us
  transfers between devices with their start and end apart: 16, of which 6 were waited for; matrix products, arithmetic and copies ran while one was open for 0% of the time, Pallas kernels for 23%

profile of v2, /device:TPU:17, one launch (start us, length us, event | category | flops | bytes accessed | tf_op | source)
XLA Modules:
  0.0 61.7 jit_solution(10824753523156973182)
XLA Ops:
  0.8 3.3 %stage.1 = (bf16[128,512]{1,0:T(8,128)(2,1)}, bf16[128,512]{1,0:T(8,128)(2,1)}, bf16[128,512]{1,0:T(8,128)(2,1)}, bf16[128,512]{1,0:T(8,128)(2,1)}, bf16[128,512...) custom-call(s32[16]{0:T(128)} %ids_in.1, ...), custom_call_target="tpu_custom_call" | custom-call | tf_op jit(solution)/shard_map/stage/pallas_call | solution.py:73
  4.1 1.3 %collective-permute-start.6 = (bf16[128,512]{1,0:T(8,128)(2,1)}, bf16[128,512]{1,0:T(8,128)(2,1)S(1)}, u32[]{:S(2)}, u32[]{:S(2)}) collective-permute-start(bf16[128,512]{1,0:T(8,128)(2,1)} %get-tuple-element.55), channel_id=1, source_target_pairs={{0,2},{2,0},{4,6},{6,4},{8,10},{10,8},{12,14},{14,12},{16,18},{18,... | collective-permute-start | bytes 393224 | tf_op jit(solution)/shard_map/ppermute | solution.py:213
  5.4 1.2 %collective-permute-start.1 = (bf16[128,512]{1,0:T(8,128)(2,1)}, bf16[128,512]{1,0:T(8,128)(2,1)S(1)}, u32[]{:S(2)}, u32[]{:S(2)}) collective-permute-start(bf16[128,512]{1,0:T(8,128)(2,1)} %get-tuple-element.47), channel_id=1, source_target_pairs={{0,4},{2,6},{4,0},{6,2},{8,12},{10,14},{12,8},{14,10},{16,20},{18,... | collective-permute-start | bytes 393224 | tf_op jit(solution)/shard_map/ppermute | solution.py:213
  6.6 0.0 collective-permute-start.5
  6.7 2.1 %collective-permute-done.6.refs_1_ = bf16[128,512]{1,0:T(8,128)(2,1)S(1)} collective-permute-done((bf16[128,512]{1,0:T(8,128)(2,1)}, bf16[128,512]{1,0:T(8,128)(2,1)S(1)}, u32[]{:S(2)}, u32[]{:S(2)}) %collective-permute-start.6) | collective-permute-done | bytes 131104 | tf_op jit(solution)/shard_map/ppermute | solution.py:213
  8.7 2.2 %collective-permute-start.8 = (bf16[128,512]{1,0:T(8,128)(2,1)}, bf16[128,512]{1,0:T(8,128)(2,1)S(1)}, u32[]{:S(2)}, u32[]{:S(2)}) collective-permute-start(bf16[128,512]{1,0:T(8,128)(2,1)} %get-tuple-element.59), channel_id=1, source_target_pairs={{0,6},{2,4},{4,2},{6,0},{8,14},{10,12},{12,10},{14,8},{16,22},{18,... | collective-permute-start | bytes 393224 | tf_op jit(solution)/shard_map/ppermute | solution.py:213
  10.9 0.0 collective-permute-start
  10.9 0.0 collective-permute-done.1.refs_2_
  10.9 1.3 %collective-permute-start.2 = (bf16[128,512]{1,0:T(8,128)(2,1)}, bf16[128,512]{1,0:T(8,128)(2,1)S(1)}, u32[]{:S(2)}, u32[]{:S(2)}) collective-permute-start(bf16[128,512]{1,0:T(8,128)(2,1)} %get-tuple-element.48), channel_id=1, source_target_pairs={{0,8},{2,10},{4,12},{6,14},{8,0},{10,2},{12,4},{14,6},{16,24},{18,... | collective-permute-start | bytes 393224 | tf_op jit(solution)/shard_map/ppermute | solution.py:213
  12.2 2.4 %collective-permute-start.12 = (bf16[128,512]{1,0:T(8,128)(2,1)}, bf16[128,512]{1,0:T(8,128)(2,1)S(1)}, u32[]{:S(2)}, u32[]{:S(2)}) collective-permute-start(bf16[128,512]{1,0:T(8,128)(2,1)} %get-tuple-element.68), channel_id=1, source_target_pairs={{0,20},{2,22},{4,16},{6,18},{8,28},{10,30},{12,24},{14,26},{16,4},... | collective-permute-start | bytes 393224 | tf_op jit(solution)/shard_map/ppermute | solution.py:213
  14.6 0.0 copy-done
  14.6 0.9 %copy-done.1 = bf16[128,512]{1,0:T(8,128)(2,1)S(1)} copy-done((bf16[128,512]{1,0:T(8,128)(2,1)S(1)}, bf16[128,512]{1,0:T(8,128)(2,1)}, u32[]{:S(2)}) %copy-start.1) | copy-done | bytes 131096
  15.5 0.0 copy-start.6
  15.5 3.0 %sums.6 = (f32[1024,512]{1,0:T(8,128)S(1)}, f32[1024,512]{1,0:T(8,128)S(1)}) custom-call(bf16[128,512]{1,0:T(8,128)(2,1)S(1)} %copy-done.1, bf16[128,512]{1,0:T(8,128)(2,1)S(1)} %collective-permute-done.6.refs_1_, bf16[128,512]{1,0:T(8,128)(2,1)S(1)} %collective-permute-done.1.refs_2_, bf16[2048,512]{1,0:T(8,128)(2,1)S(1)} %copy-done), custom_call_target="tpu_custom_call" | custom-call | flops 1024 | bytes 1024 | tf_op jit(solution)/shard_map/sums/pallas_call | solution.py:148
  18.5 0.0 collective-permute-done.5.refs_0_
  18.5 0.0 copy-done.9
  18.5 1.9 %collective-permute-start.7 = (bf16[128,512]{1,0:T(8,128)(2,1)S(1)}, bf16[128,512]{1,0:T(8,128)(2,1)S(1)}, u32[]{:S(2)}, u32[]{:S(2)}) collective-permute-start(bf16[128,512]{1,0:T(8,128)(2,1)S(1)} %copy-done.9), channel_id=1, source_target_pairs={{0,22},{2,20},{4,18},{6,16},{8,30},{10,28},{12,26},{14,24},{16,6},... | collective-permute-start | bytes 393224 | tf_op jit(solution)/shard_map/ppermute | solution.py:213
  20.4 0.0 collective-permute-done.8.refs_1_
  20.4 0.0 copy-done.8
  20.4 0.2 collective-permute-start.10
  20.6 0.0 collective-permute-done.refs_2_
  20.6 0.0 collective-permute-done.2.refs_3_
  20.6 3.0 %collective-permute-start.3 = (bf16[128,512]{1,0:T(8,128)(2,1)S(1)}, bf16[128,512]{1,0:T(8,128)(2,1)S(1)}, u32[]{:S(2)}, u32[]{:S(2)}) collective-permute-start(bf16[128,512]{1,0:T(8,128)(2,1)S(1)} %copy-done.7), channel_id=1, source_target_pairs={{0,24},{2,26},{4,28},{6,30},{8,16},{10,18},{12,20},{14,22},{16,8},... | collective-permute-start | bytes 393224 | tf_op jit(solution)/shard_map/ppermute | solution.py:213
  23.6 3.5 %collective-permute-done.12.refs_0_ = bf16[128,512]{1,0:T(8,128)(2,1)S(1)} collective-permute-done((bf16[128,512]{1,0:T(8,128)(2,1)}, bf16[128,512]{1,0:T(8,128)(2,1)S(1)}, u32[]{:S(2)}, u32[]{:S(2)}) %collective-permute-start.12) | collective-permute-done | bytes 131104 | tf_op jit(solution)/shard_map/ppermute | solution.py:213
  27.1 1.5 %collective-permute-start.13 = (bf16[128,512]{1,0:T(8,128)(2,1)S(1)}, bf16[128,512]{1,0:T(8,128)(2,1)S(1)}, u32[]{:S(2)}, u32[]{:S(2)}) collective-permute-start(bf16[128,512]{1,0:T(8,128)(2,1)S(1)} %copy-done.5), channel_id=1, source_target_pairs={{0,26},{2,24},{4,30},{6,28},{8,18},{10,16},{12,22},{14,20},{16,10}... | collective-permute-start | bytes 393224 | tf_op jit(solution)/shard_map/ppermute | solution.py:213
  28.6 5.1 %collective-permute-start.14 = (bf16[128,512]{1,0:T(8,128)(2,1)S(1)}, bf16[128,512]{1,0:T(8,128)(2,1)S(1)}, u32[]{:S(2)}, u32[]{:S(2)}) collective-permute-start(bf16[128,512]{1,0:T(8,128)(2,1)S(1)} %copy-done.6), channel_id=1, source_target_pairs={{0,12},{2,14},{4,8},{6,10},{8,4},{10,6},{12,0},{14,2},{16,28},{18,... | collective-permute-start | bytes 393224 | tf_op jit(solution)/shard_map/ppermute | solution.py:213
  33.7 3.2 %sums.7 = (f32[1024,512]{1,0:T(8,128)S(1)}, f32[1024,512]{1,0:T(8,128)S(1)}) custom-call(bf16[128,512]{1,0:T(8,128)(2,1)S(1)} %collective-permute-done.5.refs_0_, bf16[128,512]{1,0:T(8,128)(2,1)S(1)} %collective-permute-done.8.refs_1_, bf16[128,512]{1,0:T(8,128)(2,1)S(1)} %collective-permute-done.refs_2_, ...), custom_call_target="tpu_custom_call" | custom-call | flops 1024 | bytes 1024 | tf_op jit(solution)/shard_map/sums/pallas_call | solution.py:148
  36.9 0.0 collective-permute-done.7.refs_2_
  36.9 0.0 collective-permute-done.10.refs_1_
  36.9 0.0 copy-done.4
  36.9 4.5 %collective-permute-start.11 = (bf16[128,512]{1,0:T(8,128)(2,1)S(1)}, bf16[128,512]{1,0:T(8,128)(2,1)S(1)}, u32[]{:S(2)}, u32[]{:S(2)}) collective-permute-start(bf16[128,512]{1,0:T(8,128)(2,1)S(1)} %copy-done.4), channel_id=1, source_target_pairs={{0,14},{2,12},{4,10},{6,8},{8,6},{10,4},{12,2},{14,0},{16,30},{18,... | collective-permute-start | bytes 393224 | tf_op jit(solution)/shard_map/ppermute | solution.py:213
  41.4 0.0 copy-done.3
  41.4 0.0 collective-permute-start.9
  41.4 0.0 collective-permute-done.3.refs_0_
  41.4 0.0 copy-done.2
  41.4 0.1 collective-permute-start.4
  41.5 0.0 collective-permute-done.14.refs_3_
  41.5 3.2 %sums.8 = (f32[1024,512]{1,0:T(8,128)S(1)}, f32[1024,512]{1,0:T(8,128)S(1)}) custom-call(bf16[128,512]{1,0:T(8,128)(2,1)S(1)} %collective-permute-done.12.refs_0_, bf16[128,512]{1,0:T(8,128)(2,1)S(1)} %collective-permute-done.10.refs_1_, bf16[128,512]{1,0:T(8,128)(2,1)S(1)} %collective-permute-done.7.refs_2_, ...), custom_call_target="tpu_custom_call" | custom-call | flops 1024 | bytes 1024 | tf_op jit(solution)/shard_map/sums/pallas_call | solution.py:148
  44.7 0.1 collective-permute-done.13.refs_2_
  44.8 0.7 %collective-permute-done.11.refs_1_ = bf16[128,512]{1,0:T(8,128)(2,1)S(1)} collective-permute-done((bf16[128,512]{1,0:T(8,128)(2,1)S(1)}, bf16[128,512]{1,0:T(8,128)(2,1)S(1)}, u32[]{:S(2)}, u32[]{:S(2)}) %collective-permute-start.11) | collective-permute-done | bytes 131104 | tf_op jit(solution)/shard_map/ppermute | solution.py:213
  45.5 3.0 %sums.9 = (f32[1024,512]{1,0:T(8,128)S(1)}, f32[1024,512]{1,0:T(8,128)S(1)}) custom-call(bf16[128,512]{1,0:T(8,128)(2,1)S(1)} %collective-permute-done.3.refs_0_, bf16[128,512]{1,0:T(8,128)(2,1)S(1)} %collective-permute-done.11.refs_1_, bf16[128,512]{1,0:T(8,128)(2,1)S(1)} %collective-permute-done.13.refs_2_, bf16[2048,512]{1,0:T(8,128)(2,1)S(1)} %copy-done, ...), custom_call_target="tpu_custom_call" | custom-call | flops 1024 | bytes 1024 | tf_op jit(solution)/shard_map/sums/pallas_call | solution.py:148
  48.4 4.2 %collective-permute-done.9.refs_0_ = bf16[128,512]{1,0:T(8,128)(2,1)S(1)} collective-permute-done((bf16[128,512]{1,0:T(8,128)(2,1)S(1)}, bf16[128,512]{1,0:T(8,128)(2,1)S(1)}, u32[]{:S(2)}, u32[]{:S(2)}) %collective-permute-start.9) | collective-permute-done | bytes 131104 | tf_op jit(solution)/shard_map/ppermute | solution.py:213
  52.7 1.8 %sums.10 = (f32[1024,512]{1,0:T(8,128)S(1)}, f32[1024,512]{1,0:T(8,128)S(1)}) custom-call(bf16[128,512]{1,0:T(8,128)(2,1)S(1)} %collective-permute-done.9.refs_0_, bf16[2048,512]{1,0:T(8,128)(2,1)S(1)} %copy-done, f32[1024,512]{1,0:T(8,128)S(1)} %get-tuple-element.75.refs_2_, f32[1024,512]{1,0:T(8,128)S(1)} %get-tuple-element.76.refs_3_), custom_call_target="tpu_custom_call" | custom-call | flops 1024 | bytes 1024 | tf_op jit(solution)/shard_map/sums/pallas_call | solution.py:148
  54.4 0.0 collective-permute-done.4.refs_0_
  54.5 1.6 %sums.11 = (f32[1024,512]{1,0:T(8,128)S(1)}, bf16[1024,512]{1,0:T(8,128)(2,1)S(1)}) custom-call(bf16[128,512]{1,0:T(8,128)(2,1)S(1)} %collective-permute-done.4.refs_0_, bf16[2048,512]{1,0:T(8,128)(2,1)S(1)} %copy-done, f32[1024,512]{1,0:T(8,128)S(1)} %get-tuple-element.77.refs_2_, f32[1024,512]{1,0:T(8,128)S(1)} %get-tuple-element.78.refs_3_), custom_call_target="tpu_custom_call" | custom-call | flops 1024 | bytes 1024 | tf_op jit(solution)/shard_map/sums/pallas_call | solution.py:148
  56.0 1.9 %collective-permute-start.15 = (bf16[1024,512]{1,0:T(8,128)(2,1)S(1)}, bf16[1024,512]{1,0:T(8,128)(2,1)S(1)}, u32[]{:S(2)}, u32[]{:S(2)}) collective-permute-start(bf16[1024,512]{1,0:T(8,128)(2,1)S(1)} %get-tuple-element.80), channel_id=1, source_target_pairs={{0,1},{1,0},{2,3},{3,2},{4,5},{5,4},{6,7},{7,6},{8,9},{9,8},{10,11... | collective-permute-start | bytes 3145736 | tf_op jit(solution)/shard_map/ppermute | solution.py:232
  57.9 2.3 %collective-permute-done.15.refs_1_ = bf16[1024,512]{1,0:T(8,128)(2,1)S(1)} collective-permute-done((bf16[1024,512]{1,0:T(8,128)(2,1)S(1)}, bf16[1024,512]{1,0:T(8,128)(2,1)S(1)}, u32[]{:S(2)}, u32[]{:S(2)}) %collective-permute-start.15) | collective-permute-done | bytes 1048608 | tf_op jit(solution)/shard_map/ppermute | solution.py:232
  60.2 1.5 %close.1 = bf16[1024,512]{1,0:T(8,128)(2,1)} custom-call(bf16[2048,512]{1,0:T(8,128)(2,1)S(1)} %copy-done, f32[1024,512]{1,0:T(8,128)S(1)} %get-tuple-element.79.refs_0_, bf16[1024,512]{1,0:T(8,128)(2,1)S(1)} %collective-permute-done.15.refs_1_), custom_call_target="tpu_custom_call" | custom-call | flops 4194304 | bytes 6291456 | tf_op jit(solution)/shard_map/close/pallas_call | solution.py:177
  (12 shorter events, 0.0 us)
Async XLA Ops:
  0.0 14.6 %copy-start = (bf16[2048,512]{1,0:T(8,128)(2,1)S(1)}, bf16[2048,512]{1,0:T(8,128)(2,1)}, u32[]{:S(2)}) copy-start(bf16[2048,512]{1,0:T(8,128)(2,1)} %cents.1) | copy-start | bytes 6291460
  4.1 4.6 %collective-permute-start.6 = (bf16[128,512]{1,0:T(8,128)(2,1)}, bf16[128,512]{1,0:T(8,128)(2,1)S(1)}, u32[]{:S(2)}, u32[]{:S(2)}) collective-permute-start(bf16[128,512]{1,0:T(8,128)(2,1)} %get-tuple-element.55), channel_id=1, source_target_pairs={{0,2},{2,0},{4,6},{6,4},{8,10},{10,8},{12,14},{14,12},{16,18},{18,... | collective-permute-start | bytes 393224 | tf_op jit(solution)/shard_map/ppermute | solution.py:213
  5.4 5.5 %collective-permute-start.1 = (bf16[128,512]{1,0:T(8,128)(2,1)}, bf16[128,512]{1,0:T(8,128)(2,1)S(1)}, u32[]{:S(2)}, u32[]{:S(2)}) collective-permute-start(bf16[128,512]{1,0:T(8,128)(2,1)} %get-tuple-element.47), channel_id=1, source_target_pairs={{0,4},{2,6},{4,0},{6,2},{8,12},{10,14},{12,8},{14,10},{16,20},{18,... | collective-permute-start | bytes 393224 | tf_op jit(solution)/shard_map/ppermute | solution.py:213
  6.6 11.9 %collective-permute-start.5 = (bf16[128,512]{1,0:T(8,128)(2,1)}, bf16[128,512]{1,0:T(8,128)(2,1)S(1)}, u32[]{:S(2)}, u32[]{:S(2)}) collective-permute-start(bf16[128,512]{1,0:T(8,128)(2,1)} %get-tuple-element.53), channel_id=1, source_target_pairs={{0,16},{2,18},{4,20},{6,22},{8,24},{10,26},{12,28},{14,30},{16,0},... | collective-permute-start | bytes 393224 | tf_op jit(solution)/shard_map/ppermute | solution.py:213
  8.7 11.6 %collective-permute-start.8 = (bf16[128,512]{1,0:T(8,128)(2,1)}, bf16[128,512]{1,0:T(8,128)(2,1)S(1)}, u32[]{:S(2)}, u32[]{:S(2)}) collective-permute-start(bf16[128,512]{1,0:T(8,128)(2,1)} %get-tuple-element.59), channel_id=1, source_target_pairs={{0,6},{2,4},{4,2},{6,0},{8,14},{10,12},{12,10},{14,8},{16,22},{18,... | collective-permute-start | bytes 393224 | tf_op jit(solution)/shard_map/ppermute | solution.py:213
  10.9 9.7 %collective-permute-start = (bf16[128,512]{1,0:T(8,128)(2,1)}, bf16[128,512]{1,0:T(8,128)(2,1)S(1)}, u32[]{:S(2)}, u32[]{:S(2)}) collective-permute-start(bf16[128,512]{1,0:T(8,128)(2,1)} %get-tuple-element.45), channel_id=1, source_target_pairs={{0,18},{2,16},{4,22},{6,20},{8,26},{10,24},{12,30},{14,28},{16,2},... | collective-permute-start | bytes 393224 | tf_op jit(solution)/shard_map/ppermute | solution.py:213
  10.9 9.6 %collective-permute-start.2 = (bf16[128,512]{1,0:T(8,128)(2,1)}, bf16[128,512]{1,0:T(8,128)(2,1)S(1)}, u32[]{:S(2)}, u32[]{:S(2)}) collective-permute-start(bf16[128,512]{1,0:T(8,128)(2,1)} %get-tuple-element.48), channel_id=1, source_target_pairs={{0,8},{2,10},{4,12},{6,14},{8,0},{10,2},{12,4},{14,6},{16,24},{18,... | collective-permute-start | bytes 393224 | tf_op jit(solution)/shard_map/ppermute | solution.py:213
  12.2 14.9 %collective-permute-start.12 = (bf16[128,512]{1,0:T(8,128)(2,1)}, bf16[128,512]{1,0:T(8,128)(2,1)S(1)}, u32[]{:S(2)}, u32[]{:S(2)}) collective-permute-start(bf16[128,512]{1,0:T(8,128)(2,1)} %get-tuple-element.68), channel_id=1, source_target_pairs={{0,20},{2,22},{4,16},{6,18},{8,28},{10,30},{12,24},{14,26},{16,4},... | collective-permute-start | bytes 393224 | tf_op jit(solution)/shard_map/ppermute | solution.py:213
  14.6 0.9 %copy-start.1 = (bf16[128,512]{1,0:T(8,128)(2,1)S(1)}, bf16[128,512]{1,0:T(8,128)(2,1)}, u32[]{:S(2)}) copy-start(bf16[128,512]{1,0:T(8,128)(2,1)} %get-tuple-element.54.refs_0_) | copy-start | bytes 393220
  15.5 3.0 %copy-start.9 = (bf16[128,512]{1,0:T(8,128)(2,1)S(1)}, bf16[128,512]{1,0:T(8,128)(2,1)}, u32[]{:S(2)}) copy-start(bf16[128,512]{1,0:T(8,128)(2,1)} %get-tuple-element.57) | copy-start | bytes 393220
  15.5 4.9 %copy-start.8 = (bf16[128,512]{1,0:T(8,128)(2,1)S(1)}, bf16[128,512]{1,0:T(8,128)(2,1)}, u32[]{:S(2)}) copy-start(bf16[128,512]{1,0:T(8,128)(2,1)} %get-tuple-element.65) | copy-start | bytes 393220
  15.5 5.0 %copy-start.7 = (bf16[128,512]{1,0:T(8,128)(2,1)S(1)}, bf16[128,512]{1,0:T(8,128)(2,1)}, u32[]{:S(2)}) copy-start(bf16[128,512]{1,0:T(8,128)(2,1)} %get-tuple-element.49) | copy-start | bytes 393220
  15.5 11.6 %copy-start.5 = (bf16[128,512]{1,0:T(8,128)(2,1)S(1)}, bf16[128,512]{1,0:T(8,128)(2,1)}, u32[]{:S(2)}) copy-start(bf16[128,512]{1,0:T(8,128)(2,1)} %get-tuple-element.69) | copy-start | bytes 393220
  15.5 13.1 %copy-start.6 = (bf16[128,512]{1,0:T(8,128)(2,1)S(1)}, bf16[128,512]{1,0:T(8,128)(2,1)}, u32[]{:S(2)}) copy-start(bf16[128,512]{1,0:T(8,128)(2,1)} %get-tuple-element.71) | copy-start | bytes 393220
  18.5 18.4 %collective-permute-start.7 = (bf16[128,512]{1,0:T(8,128)(2,1)S(1)}, bf16[128,512]{1,0:T(8,128)(2,1)S(1)}, u32[]{:S(2)}, u32[]{:S(2)}) collective-permute-start(bf16[128,512]{1,0:T(8,128)(2,1)S(1)} %copy-done.9), channel_id=1, source_target_pairs={{0,22},{2,20},{4,18},{6,16},{8,30},{10,28},{12,26},{14,24},{16,6},... | collective-permute-start | bytes 393224 | tf_op jit(solution)/shard_map/ppermute | solution.py:213
  20.4 16.5 %collective-permute-start.10 = (bf16[128,512]{1,0:T(8,128)(2,1)S(1)}, bf16[128,512]{1,0:T(8,128)(2,1)S(1)}, u32[]{:S(2)}, u32[]{:S(2)}) collective-permute-start(bf16[128,512]{1,0:T(8,128)(2,1)S(1)} %copy-done.8), channel_id=1, source_target_pairs={{0,10},{2,8},{4,14},{6,12},{8,2},{10,0},{12,6},{14,4},{16,26},{18,... | collective-permute-start | bytes 393224 | tf_op jit(solution)/shard_map/ppermute | solution.py:213
  20.6 20.8 %collective-permute-start.3 = (bf16[128,512]{1,0:T(8,128)(2,1)S(1)}, bf16[128,512]{1,0:T(8,128)(2,1)S(1)}, u32[]{:S(2)}, u32[]{:S(2)}) collective-permute-start(bf16[128,512]{1,0:T(8,128)(2,1)S(1)} %copy-done.7), channel_id=1, source_target_pairs={{0,24},{2,26},{4,28},{6,30},{8,16},{10,18},{12,20},{14,22},{16,8},... | collective-permute-start | bytes 393224 | tf_op jit(solution)/shard_map/ppermute | solution.py:213
  27.1 17.7 %collective-permute-start.13 = (bf16[128,512]{1,0:T(8,128)(2,1)S(1)}, bf16[128,512]{1,0:T(8,128)(2,1)S(1)}, u32[]{:S(2)}, u32[]{:S(2)}) collective-permute-start(bf16[128,512]{1,0:T(8,128)(2,1)S(1)} %copy-done.5), channel_id=1, source_target_pairs={{0,26},{2,24},{4,30},{6,28},{8,18},{10,16},{12,22},{14,20},{16,10}... | collective-permute-start | bytes 393224 | tf_op jit(solution)/shard_map/ppermute | solution.py:213
  28.6 12.9 %collective-permute-start.14 = (bf16[128,512]{1,0:T(8,128)(2,1)S(1)}, bf16[128,512]{1,0:T(8,128)(2,1)S(1)}, u32[]{:S(2)}, u32[]{:S(2)}) collective-permute-start(bf16[128,512]{1,0:T(8,128)(2,1)S(1)} %copy-done.6), channel_id=1, source_target_pairs={{0,12},{2,14},{4,8},{6,10},{8,4},{10,6},{12,0},{14,2},{16,28},{18,... | collective-permute-start | bytes 393224 | tf_op jit(solution)/shard_map/ppermute | solution.py:213
  33.7 3.2 %copy-start.4 = (bf16[128,512]{1,0:T(8,128)(2,1)S(1)}, bf16[128,512]{1,0:T(8,128)(2,1)}, u32[]{:S(2)}) copy-start(bf16[128,512]{1,0:T(8,128)(2,1)} %get-tuple-element.66) | copy-start | bytes 393220
  33.7 7.7 %copy-start.3 = (bf16[128,512]{1,0:T(8,128)(2,1)S(1)}, bf16[128,512]{1,0:T(8,128)(2,1)}, u32[]{:S(2)}) copy-start(bf16[128,512]{1,0:T(8,128)(2,1)} %get-tuple-element.62) | copy-start | bytes 393220
  33.7 7.7 %copy-start.2 = (bf16[128,512]{1,0:T(8,128)(2,1)S(1)}, bf16[128,512]{1,0:T(8,128)(2,1)}, u32[]{:S(2)}) copy-start(bf16[128,512]{1,0:T(8,128)(2,1)} %get-tuple-element.50) | copy-start | bytes 393220
  36.9 8.5 %collective-permute-start.11 = (bf16[128,512]{1,0:T(8,128)(2,1)S(1)}, bf16[128,512]{1,0:T(8,128)(2,1)S(1)}, u32[]{:S(2)}, u32[]{:S(2)}) collective-permute-start(bf16[128,512]{1,0:T(8,128)(2,1)S(1)} %copy-done.4), channel_id=1, source_target_pairs={{0,14},{2,12},{4,10},{6,8},{8,6},{10,4},{12,2},{14,0},{16,30},{18,... | collective-permute-start | bytes 393224 | tf_op jit(solution)/shard_map/ppermute | solution.py:213
  41.4 11.3 %collective-permute-start.9 = (bf16[128,512]{1,0:T(8,128)(2,1)S(1)}, bf16[128,512]{1,0:T(8,128)(2,1)S(1)}, u32[]{:S(2)}, u32[]{:S(2)}) collective-permute-start(bf16[128,512]{1,0:T(8,128)(2,1)S(1)} %copy-done.3), channel_id=1, source_target_pairs={{0,28},{2,30},{4,24},{6,26},{8,20},{10,22},{12,16},{14,18},{16,12}... | collective-permute-start | bytes 393224 | tf_op jit(solution)/shard_map/ppermute | solution.py:213
  41.4 13.0 %collective-permute-start.4 = (bf16[128,512]{1,0:T(8,128)(2,1)S(1)}, bf16[128,512]{1,0:T(8,128)(2,1)S(1)}, u32[]{:S(2)}, u32[]{:S(2)}) collective-permute-start(bf16[128,512]{1,0:T(8,128)(2,1)S(1)} %copy-done.2), channel_id=1, source_target_pairs={{0,30},{2,28},{4,26},{6,24},{8,22},{10,20},{12,18},{14,16},{16,14}... | collective-permute-start | bytes 393224 | tf_op jit(solution)/shard_map/ppermute | solution.py:213
  56.0 4.2 %collective-permute-start.15 = (bf16[1024,512]{1,0:T(8,128)(2,1)S(1)}, bf16[1024,512]{1,0:T(8,128)(2,1)S(1)}, u32[]{:S(2)}, u32[]{:S(2)}) collective-permute-start(bf16[1024,512]{1,0:T(8,128)(2,1)S(1)} %get-tuple-element.80), channel_id=1, source_target_pairs={{0,1},{1,0},{2,3},{3,2},{4,5},{5,4},{6,7},{7,6},{8,9},{9,8},{10,11... | collective-permute-start | bytes 3145736 | tf_op jit(solution)/shard_map/ppermute | solution.py:232

commit v3 on v0

v3 whole, which is shorter than its diff:
```python
import functools
import math

import jax
import jax.numpy as jnp
from jax import lax
from jax.experimental import pallas as pl
from jax.experimental.pallas import tpu as pltpu
from jax.sharding import PartitionSpec as P

F32 = jnp.float32
BF16 = jnp.bfloat16
TILE = 512
TURN = 256
MIB = 1 << 20
HALVES = 2


def in_hbm(array):
    return pltpu.with_memory_space_constraint(array, pltpu.HBM)


def in_vmem(array):
    return pltpu.with_memory_space_constraint(array, pltpu.VMEM)


def after(array, *others):
    return lax.optimization_barrier((array, *others))[0]


def stage_kernel(alone, paired, ids_in, counts, points, *refs):
    singles, rest = refs[: len(alone)], refs[len(alone) :]
    keeps, (give, where, ids, held, zeros, reads, writes, small) = rest[: len(paired)], rest[len(paired) :]
    slots, rows = points.shape[:2]
    me, core = lax.axis_index("cluster"), lax.rem(lax.axis_index("copy"), 2)
    ids_copy = pltpu.make_async_copy(ids_in, ids, small)
    ids_copy.start()
    for s in range(slots):
        pltpu.make_async_copy(points.at[s], held.at[s], reads.at[s]).start()
    for o in range(where.shape[0]):
        where[o] = -1
    zeros[...] = jnp.zeros_like(zeros)
    ids_copy.wait()
    for s in range(slots):

        @pl.when(s < counts[0])
        def _():
            where[ids[s]] = s

    for s in range(slots):
        pltpu.make_async_copy(points.at[s], held.at[s], reads.at[s]).wait()
    targets = [(k, out) for k, out in zip(alone, singles)]
    targets += [(k + 1 - core, give.at[pl.ds(i * rows, rows)]) for i, k in enumerate(paired)]
    targets += [(k + core, out.at[pl.ds(0, rows)]) for k, out in zip(paired, keeps)]
    for i, (k, out) in enumerate(targets):
        slot = where[me ^ k]

        @pl.when(slot >= 0)
        def _():
            pltpu.make_async_copy(held.at[jnp.maximum(slot, 0)], out, writes.at[i]).start()

        @pl.when(slot < 0)
        def _():
            pltpu.make_async_copy(zeros, out, writes.at[i]).start()

    for i, (k, out) in enumerate(targets):
        pltpu.make_async_copy(zeros, out, writes.at[i]).wait()


def stage(points, ids, counts, owners, alone, paired):
    rows, feature = points.shape[1:]
    spec = pl.BlockSpec(memory_space=pltpu.HBM)
    hbm = lambda n: pltpu.HBM((n, feature), points.dtype)
    outs = pl.pallas_call(
        functools.partial(stage_kernel, alone, paired),
        out_shape=[hbm(rows)] * len(alone) + [hbm(2 * rows)] * len(paired) + [hbm(len(paired) * rows)],
        in_specs=[spec, pl.BlockSpec(memory_space=pltpu.SMEM), spec],
        out_specs=[spec] * (len(alone) + len(paired) + 1),
        scratch_shapes=[
            pltpu.SMEM((owners,), jnp.int32),
            pltpu.SMEM(ids.shape, jnp.int32),
            pltpu.VMEM(points.shape, points.dtype),
            pltpu.VMEM((rows, feature), points.dtype),
            pltpu.SemaphoreType.DMA((points.shape[0],)),
            pltpu.SemaphoreType.DMA((len(alone) + 2 * len(paired),)),
            pltpu.SemaphoreType.DMA,
        ],
        compiler_params=pltpu.CompilerParams(vmem_limit_bytes=16 * MIB),
        name="stage",
    )(in_hbm(ids), counts, in_hbm(points))
    return dict(zip(alone, outs)), dict(zip(paired, outs[len(alone) : -1])), outs[-1]


def merge_kernel(got, *refs):
    outs, sems = refs[len(refs) // 2 : -1], refs[-1]
    rows = got.shape[0] // len(outs)
    copies = [
        pltpu.make_async_copy(got.at[pl.ds(i * rows, rows)], out.at[pl.ds(rows, rows)], sems.at[i])
        for i, out in enumerate(outs)
    ]
    for copy in copies:
        copy.start()
    for copy in copies:
        copy.wait()


def merge(keeps, got):
    spec = pl.BlockSpec(memory_space=pltpu.HBM)
    return pl.pallas_call(
        merge_kernel,
        out_shape=[pltpu.HBM(k.shape, k.dtype) for k in keeps],
        in_specs=[pl.BlockSpec(memory_space=pltpu.VMEM)] + [spec] * len(keeps),
        out_specs=[spec] * len(keeps),
        input_output_aliases={1 + i: i for i in range(len(keeps))},
        scratch_shapes=[pltpu.SemaphoreType.DMA((len(keeps),))],
        compiler_params=pltpu.CompilerParams(vmem_limit_bytes=16 * MIB),
        name="merge",
    )(in_vmem(got), *keeps)


def turns(xs):
    found, left = [], 0
    for i, x in enumerate(xs):
        start = 0
        while start < x.shape[0]:
            if not left:
                found.append([])
                left = TURN
            size = min(left, x.shape[0] - start)
            found[-1].append((i, start, start + size))
            start, left = start + size, left - size
    return found


def sums_kernel(blocks, replicas, last, *refs):
    xs, rest = refs[:blocks], refs[blocks:]
    cents, rest = rest[0], rest[1:]
    results = (1 + (replicas - 1) * HALVES) if last else replicas
    befores, outs, lts = rest[: -results - 2], rest[-results - 2 : -2], rest[-2:]
    total, feature = cents.shape
    share = total // replicas
    tile = min(TILE, share // HALVES if last else share)
    tiles = total // tile
    scale = 3.0 / math.sqrt(feature) * math.log2(math.e)
    me = lax.axis_index("copy")

    def logits(i, x, lt, high):
        here = pl.ds(i * tile, tile)
        n = x.shape[0]
        l = jnp.dot(cents[here, :], x.T, preferred_element_type=F32)
        lt[here, pl.ds(0, n)] = l
        return jnp.maximum(high, jnp.max(l.reshape(tile // 8, 8, n), axis=0))

    def exponentials(i, lt, high, norm):
        here, n = pl.ds(i * tile, tile), high.shape[1]
        e = jnp.exp2(lt[here, pl.ds(0, n)] * scale - high)
        lt[here, pl.ds(0, n)] = e
        return norm + jnp.sum(e.reshape(tile // 8, 8, n), axis=0)

    def add(i, x, lt, inverse, fresh):
        q, t = i // (share // tile), i % (share // tile)
        here = pl.ds(pl.multiple_of(lax.rem(me + q, replicas) * share + t * tile, tile), tile)
        there = pl.ds(t * tile, tile)
        weights = (lt[here, pl.ds(0, x.shape[0])] * inverse).astype(BF16)
        if last and not q:
            outs[0][there, :] = weights
            return
        s = jnp.dot(weights, x, preferred_element_type=F32)
        if not fresh:
            s = s + outs[q][there, :]
        elif befores:
            s = s + befores[q][there, :]
        if last:
            size = share // HALVES
            outs[1 + (q - 1) * HALVES + t * tile // size][pl.ds(t * tile % size, tile), :] = s
        else:
            outs[q][there, :] = s

    waiting = None
    for first, pieces in enumerate(turns(xs)):
        x = jnp.concatenate([xs[i][a:b, :] for i, a, b in pieces], axis=0)
        lt = lts[first % 2]
        n = x.shape[0]
        high = jnp.full((8, n), -jnp.inf, F32)
        if waiting:
            px, plt, phigh, fresh = waiting
            pnorm = jnp.zeros((8, px.shape[0]), F32)
        for i in range(tiles):
            high = logits(i, x, lt, high)
            if waiting:
                pnorm = exponentials(i, plt, phigh, pnorm)
        if waiting:
            inverse = 1.0 / jnp.sum(pnorm, axis=0, keepdims=True)
            for i in range(tiles):
                add(i, px, plt, inverse, fresh)
        high = jnp.max(high, axis=0, keepdims=True) * scale
        waiting = x, lt, high, first == 0
    x, lt, high, fresh = waiting
    norm = jnp.zeros((8, x.shape[0]), F32)
    for i in range(tiles):
        norm = exponentials(i, lt, high, norm)
    inverse = 1.0 / jnp.sum(norm, axis=0, keepdims=True)
    for i in range(tiles):
        add(i, x, lt, inverse, fresh)


def sums(xs, centroids, befores, replicas, last=False):
    total, feature = centroids.shape
    share = total // replicas
    points = sum(x.shape[0] for x in xs)
    assert points <= TURN or not last
    spec = pl.BlockSpec(memory_space=pltpu.VMEM)
    outs = [jax.ShapeDtypeStruct((share, feature), F32)] * replicas
    if last:
        outs = [jax.ShapeDtypeStruct((share, points), BF16)]
        outs += [jax.ShapeDtypeStruct((share // HALVES, feature), F32)] * ((replicas - 1) * HALVES)
    return pl.pallas_call(
        functools.partial(sums_kernel, len(xs), replicas, last),
        out_shape=outs,
        in_specs=[spec] * (len(xs) + 1 + len(befores)),
        out_specs=[spec] * len(outs),
        scratch_shapes=[pltpu.VMEM((total, min(TURN, points)), F32)] * 2,
        compiler_params=pltpu.CompilerParams(vmem_limit_bytes=28 * MIB),
        cost_estimate=pl.CostEstimate(flops=1024, bytes_accessed=1024, transcendentals=0),
        name="sums",
    )(*xs, centroids, *befores)


def own_kernel(blocks, *refs):
    xs, (weights, before, cents, out) = refs[:blocks], refs[blocks:]
    share = out.shape[0]
    tile = min(TILE, share)
    x = jnp.concatenate([r[...] for r in xs], axis=0)
    for t in range(share // tile):
        there = pl.ds(t * tile, tile)
        here = pl.ds(pl.multiple_of(lax.axis_index("copy") * share + t * tile, tile), tile)
        s = jnp.dot(weights[there, :], x, preferred_element_type=F32)
        out[there, :] = s + before[there, :] + cents[here, :].astype(F32)


def own(xs, weights, before, centroids):
    spec = pl.BlockSpec(memory_space=pltpu.VMEM)
    return pl.pallas_call(
        functools.partial(own_kernel, len(xs)),
        out_shape=jax.ShapeDtypeStruct(before.shape, F32),
        in_specs=[spec] * (len(xs) + 3),
        out_specs=spec,
        compiler_params=pltpu.CompilerParams(vmem_limit_bytes=28 * MIB),
        cost_estimate=pl.CostEstimate(flops=1024, bytes_accessed=1024, transcendentals=0),
        name="own",
    )(*xs, weights, before, centroids)


def close_kernel(h, terms, own, *refs):
    received, (out, held, sems) = refs[:terms], refs[-3:]
    size, feature = received[0].shape
    tile = size // 2
    copies = []
    for t in range(size // tile):
        there = pl.ds(t * tile, tile)
        v = own[pl.ds(h * size + t * tile, tile), :]
        for term in received:
            v = v + term[there, :]
        mean = jnp.mean(v * v, axis=-1, keepdims=True)
        held[there, :] = (v * lax.rsqrt(mean + 1e-06)).astype(BF16)
        copies.append(pltpu.make_async_copy(held.at[there], out.at[pl.ds(h * size + t * tile, tile)], sems.at[t]))
        copies[-1].start()
    for copy in copies:
        copy.wait()


def close(own, received, out, h):
    vmem, hbm = pl.BlockSpec(memory_space=pltpu.VMEM), pl.BlockSpec(memory_space=pl.ANY)
    terms = len(received)
    return pl.pallas_call(
        functools.partial(close_kernel, h, terms),
        out_shape=jax.ShapeDtypeStruct(own.shape, BF16),
        in_specs=[vmem] * (1 + terms) + [hbm] * len(out),
        out_specs=hbm,
        input_output_aliases={1 + terms: 0} if out else {},
        scratch_shapes=[pltpu.VMEM(received[0].shape, BF16), pltpu.SemaphoreType.DMA((2,))],
        compiler_params=pltpu.CompilerParams(vmem_limit_bytes=28 * MIB),
        cost_estimate=pl.CostEstimate(flops=1024, bytes_accessed=1024, transcendentals=0),
        name="close",
    )(own, *received, *out)


def local(points, block_ids, block_counts, centroids):
    owners = lax.axis_size("cluster")
    replicas = lax.axis_size("copy")
    assert owners >= 16 and owners & (owners - 1) == 0 and replicas % 2 == 0
    half = owners // 2
    far, paired = list(range(half, owners)), list(range(2, half, 2))
    singles, keeps, give = stage(points, block_ids, block_counts, owners, far + [0, 1], paired)
    give = lax.ppermute(give, "copy", [(k, k ^ 1) for k in range(replicas)])
    both = merge([keeps[k] for k in paired], give)
    arrived = {0: singles[0]}

    def send(k, *others):
        array = singles[k] if k in singles else both[paired.index(k)]
        pairs = []
        for d in range(owners):
            for r in range(replicas):
                to = d ^ (k + r % 2 if k in paired else k)
                pairs.append((d * replicas + r, to * replicas + r))
        array = after(array, *others) if others else array
        arrived[k] = lax.ppermute(array, ("cluster", "copy"), pairs)

    groups = [[0, 1, paired[0]]]
    for i in range(0, len(far) - 2, 2):
        groups.append(far[i : i + 2] + paired[1 + i // 2 : 2 + i // 2])
    groups += [far[-2:-1], far[-1:]]
    totals = []

    def work():
        group = groups[len(totals)]
        for k in group:
            if k not in arrived:
                i = paired.index(k) if k in paired else 0
                send(k, *([arrived[1 if i < 3 else paired[i - 3]]] if i else []))
        before = totals[-1] if totals else []
        last = len(totals) == len(groups) - 1
        totals.append(sums([arrived[k] for k in group], centroids, before, replicas, last))

    for i, k in enumerate(far):
        others = [arrived[far[i - 3]]] if i >= 3 else []
        if i >= 6:
            ahead = min(i - 6, i // 2 - 2)
            while len(totals) <= ahead:
                work()
            others.append(totals[ahead][0])
        send(k, *others)
    while len(totals) < len(groups):
        work()
    before, (weights, *shares) = totals[-2:]

    mine = own([arrived[k] for k in groups[-1]], weights, before[0], centroids)
    received = []
    for h in range(HALVES):
        received.append([
            lax.ppermute(shares[(r - 1) * HALVES + h], "copy", [(i, (i + r) % replicas) for i in range(replicas)])
            for r in range(1, replicas)
        ])
    out = []
    for h in range(HALVES):
        out = [close(mine, received[h], out, h)]
    return out[0]


def solution(mesh):
    return jax.shard_map(
        local,
        mesh=mesh,
        in_specs=(
            P(("cluster", "copy"), None, None),
            P(("cluster", "copy")),
            P(("cluster", "copy")),
            P("cluster", None),
        ),
        out_specs=P(("cluster", "copy"), None),
        check_vma=False,
    )
```

time: 155 us -> 62.7 us (0.40); the launches traced: 153 us -> 62.5 us
  waiting for transfers between devices: 57.9 us -> 15.3 us
  matrix products: 35.4 us -> 0 us
  Pallas kernels: 0 us -> 19.6 us
  other arithmetic: 16.6 us -> 0 us
  local copies, waits for them, and re-layouts: 15.2 us -> 0.91 us
  between operations: 14.8 us -> 0.93 us
  starting transfers between devices: 12.9 us -> 25.8 us
    all_to_all x2 -> x0, waiting for transfers between devices: 44.2 us -> none  [the longest x1 44.2 us: local(): lax.all_to_all(outgoing, 'cluster', split_axis=0, concat_axis=0, tiled=True)]
    dot_general x8 -> x0, matrix products: 35.4 us -> none  [the longest x4 23.5 us: visit(): jnp.einsum('rk,rd->kd', weights, gathered, preferred_element_type=jnp.flo...]
    ppermute x0 -> x15, starting transfers between devices: none -> 25.8 us  [the longest x12 24.4 us: send(): arrived[k] = lax.ppermute(array, ('cluster', 'copy'), pairs)]
    pallas_call x0 -> x11, Pallas kernels: none -> 19.6 us  [the longest x6 13.3 us: sums(): pl.pallas_call(functools.partial(sums_kernel, len(xs), replicas, last), o...]
    ppermute x0 -> x15, waiting for transfers between devices: none -> 15.3 us  [the longest x12 12.7 us: send(): arrived[k] = lax.ppermute(array, ('cluster', 'copy'), pairs)]
    reduce_scatter x1 -> x0, waiting for transfers between devices: 13.8 us -> none  [local(): lax.psum_scatter(partial_sums, 'copy', scatter_dimension=0, tiled=True)]
    all_to_all x2 -> x0, starting transfers between devices: 12.9 us -> none  [the longest x1 6.55 us: local(): lax.all_to_all(present.astype(jnp.bfloat16), 'cluster', split_axis=0, con...]
    gather x5 -> x0, local copies, waits for them, and re-layouts: 10.7 us -> none  [the longest x4 8.68 us: visit(): gathered = received[chosen].reshape(turn_blocks * block_rows, feature)]
  transfers between devices with their start and end apart: 3 -> 15, of which waited for: 2 -> 8; matrix products, arithmetic and copies ran while one was open for 5% -> 0% of each run, Pallas kernels for 0% -> 23%
where the time goes in v3:
time: 62.7 us; the launch traced here: 62.5 us
  starting transfers between devices  25.8 us (41%)
  Pallas kernels  19.6 us (31%)
  waiting for transfers between devices  15.3 us (24%)
  between operations  0.93 us (1%)
  local copies, waits for them, and re-layouts  0.91 us (1%)
    ppermute x12, starting transfers between devices, send(): arrived[k] = lax.ppermute(array, ('cluster', 'copy'), pairs)  24.4 us
    pallas_call x6, Pallas kernels, sums(): pl.pallas_call(functools.partial(sums_kernel, len(xs), replicas, last), o...  13.3 us
    ppermute x12, waiting for transfers between devices, send(): arrived[k] = lax.ppermute(array, ('cluster', 'copy'), pairs)  12.7 us
    pallas_call x1, Pallas kernels, stage(): pl.pallas_call(functools.partial(stage_kernel, alone, paired), out_shape=...  3.2 us
    ppermute x2, waiting for transfers between devices, local(): lax.ppermute(shares[(r - 1) * HALVES + h], 'copy', [(i, (i + r) % replica...  2.32 us
    pallas_call x2, Pallas kernels, close(): pl.pallas_call(functools.partial(close_kernel, h, terms), out_shape=jax.S...  1.91 us
  transfers between devices with their start and end apart: 15, of which 8 were waited for; matrix products, arithmetic and copies ran while one was open for 0% of the time, Pallas kernels for 23%

profile of v3, /device:TPU:17, one launch (start us, length us, event | category | flops | bytes accessed | tf_op | source)
XLA Modules:
  0.0 62.5 jit_solution(11461332419681441325)
XLA Ops:
  0.0 0.0 copy-start
  0.8 3.2 %stage.1 = (bf16[128,512]{1,0:T(8,128)(2,1)}, bf16[128,512]{1,0:T(8,128)(2,1)}, bf16[128,512]{1,0:T(8,128)(2,1)}, bf16[128,512]{1,0:T(8,128)(2,1)}, bf16[128,512...) custom-call(s32[16]{0:T(128)} %ids_in.1, ...), custom_call_target="tpu_custom_call" | custom-call | tf_op jit(solution)/shard_map/stage/pallas_call | solution.py:74
  4.0 0.0 copy-start.3
  4.0 0.7 %collective-permute-start.3 = (bf16[384,512]{1,0:T(8,128)(2,1)}, bf16[384,512]{1,0:T(8,128)(2,1)S(1)}, u32[]{:S(2)}, u32[]{:S(2)}) collective-permute-start(bf16[384,512]{1,0:T(8,128)(2,1)} %get-tuple-element.47), channel_id=1, source_target_pairs={{0,1},{1,0},{2,3},{3,2},{4,5},{5,4},{6,7},{7,6},{8,9},{9,8},{10,11... | collective-permute-start | bytes 1179656 | tf_op jit(solution)/shard_map/ppermute | solution.py:295
  4.8 1.2 %collective-permute-start.4 = (bf16[128,512]{1,0:T(8,128)(2,1)}, bf16[128,512]{1,0:T(8,128)(2,1)S(1)}, u32[]{:S(2)}, u32[]{:S(2)}) collective-permute-start(bf16[128,512]{1,0:T(8,128)(2,1)} %get-tuple-element.52), channel_id=1, source_target_pairs={{0,2},{1,3},{2,0},{3,1},{4,6},{5,7},{6,4},{7,5},{8,10},{9,11},{10,... | collective-permute-start | bytes 393224 | tf_op jit(solution)/shard_map/ppermute | solution.py:307
  6.0 0.1 collective-permute-start.2
  6.0 0.3 collective-permute-done.3.got
  6.3 0.8 %merge.1 = (bf16[256,512]{1,0:T(8,128)(2,1)}, bf16[256,512]{1,0:T(8,128)(2,1)}, bf16[256,512]{1,0:T(8,128)(2,1)}) custom-call(bf16[384,512]{1,0:T(8,128)(2,1)S(1)} %collective-permute-done.3.got, bf16[256,512]{1,0:T(8,128)(2,1)} %get-tuple-element.48.refs_0_, ...), custom_call_target="tpu_custom_call", output_to_operand_aliasing={{0}: (1, {}), {1}: (2, {}), {2}: (3, {})} | custom-call | tf_op jit(solution)/shard_map/merge/pallas_call | solution.py:109
  7.1 2.2 %collective-permute-start.6 = (bf16[256,512]{1,0:T(8,128)(2,1)}, bf16[256,512]{1,0:T(8,128)(2,1)S(1)}, u32[]{:S(2)}, u32[]{:S(2)}) collective-permute-start(bf16[256,512]{1,0:T(8,128)(2,1)} %get-tuple-element.55), channel_id=1, source_target_pairs={{0,4},{1,7},{2,6},{3,5},{4,0},{5,3},{6,2},{7,1},{8,12},{9,15},{10,... | collective-permute-start | bytes 786440 | tf_op jit(solution)/shard_map/ppermute | solution.py:307
  9.4 2.0 %collective-permute-start = (bf16[128,512]{1,0:T(8,128)(2,1)}, bf16[128,512]{1,0:T(8,128)(2,1)S(1)}, u32[]{:S(2)}, u32[]{:S(2)}) collective-permute-start(bf16[128,512]{1,0:T(8,128)(2,1)} %get-tuple-element.44), channel_id=1, source_target_pairs={{0,18},{1,19},{2,16},{3,17},{4,22},{5,23},{6,20},{7,21},{8,26},{9,... | collective-permute-start | bytes 393224 | tf_op jit(solution)/shard_map/ppermute | solution.py:307
  11.4 0.0 collective-permute-done.4.refs_1_
  11.4 1.3 %collective-permute-start.5 = (bf16[256,512]{1,0:T(8,128)(2,1)}, bf16[256,512]{1,0:T(8,128)(2,1)S(1)}, u32[]{:S(2)}, u32[]{:S(2)}) collective-permute-start(bf16[256,512]{1,0:T(8,128)(2,1)} %get-tuple-element.53), channel_id=1, source_target_pairs={{0,8},{1,11},{2,10},{3,9},{4,12},{5,15},{6,14},{7,13},{8,0},{9,3},... | collective-permute-start | bytes 786440 | tf_op jit(solution)/shard_map/ppermute | solution.py:307
  12.6 1.2 %collective-permute-start.10 = (bf16[128,512]{1,0:T(8,128)(2,1)}, bf16[128,512]{1,0:T(8,128)(2,1)S(1)}, u32[]{:S(2)}, u32[]{:S(2)}) collective-permute-start(bf16[128,512]{1,0:T(8,128)(2,1)} %get-tuple-element.65), channel_id=1, source_target_pairs={{0,20},{1,21},{2,22},{3,23},{4,16},{5,17},{6,18},{7,19},{8,28},{9,... | collective-permute-start | bytes 393224 | tf_op jit(solution)/shard_map/ppermute | solution.py:307
  13.9 0.0 collective-permute-done.2.refs_0_
  13.9 3.0 %collective-permute-start.8 = (bf16[128,512]{1,0:T(8,128)(2,1)}, bf16[128,512]{1,0:T(8,128)(2,1)S(1)}, u32[]{:S(2)}, u32[]{:S(2)}) collective-permute-start(bf16[128,512]{1,0:T(8,128)(2,1)} %get-tuple-element.62), channel_id=1, source_target_pairs={{0,22},{1,23},{2,20},{3,21},{4,18},{5,19},{6,16},{7,17},{8,30},{9,... | collective-permute-start | bytes 393224 | tf_op jit(solution)/shard_map/ppermute | solution.py:307
  16.8 1.0 %collective-permute-done.refs_1_ = bf16[128,512]{1,0:T(8,128)(2,1)S(1)} collective-permute-done((bf16[128,512]{1,0:T(8,128)(2,1)}, bf16[128,512]{1,0:T(8,128)(2,1)S(1)}, u32[]{:S(2)}, u32[]{:S(2)}) %collective-permute-start) | collective-permute-done | bytes 131104 | tf_op jit(solution)/shard_map/ppermute | solution.py:307
  17.9 6.7 %collective-permute-start.12 = (bf16[256,512]{1,0:T(8,128)(2,1)}, bf16[256,512]{1,0:T(8,128)(2,1)S(1)}, u32[]{:S(2)}, u32[]{:S(2)}) collective-permute-start(bf16[256,512]{1,0:T(8,128)(2,1)} %get-tuple-element.68), channel_id=1, source_target_pairs={{0,12},{1,15},{2,14},{3,13},{4,8},{5,11},{6,10},{7,9},{8,4},{9,7},... | collective-permute-start | bytes 786440 | tf_op jit(solution)/shard_map/ppermute | solution.py:307
  24.6 0.0 collective-permute-done.10.refs_0_
  24.6 4.5 %collective-permute-start.1 = (bf16[128,512]{1,0:T(8,128)(2,1)}, bf16[128,512]{1,0:T(8,128)(2,1)S(1)}, u32[]{:S(2)}, u32[]{:S(2)}) collective-permute-start(bf16[128,512]{1,0:T(8,128)(2,1)} %get-tuple-element.45), channel_id=1, source_target_pairs={{0,24},{1,25},{2,26},{3,27},{4,28},{5,29},{6,30},{7,31},{8,16},{9,... | collective-permute-start | bytes 393224 | tf_op jit(solution)/shard_map/ppermute | solution.py:307
  29.2 0.0 collective-permute-done.6.refs_2_
  29.2 0.0 collective-permute-start.11
  29.2 0.0 copy-done
  29.2 0.0 copy-start.1
  29.2 0.9 %copy-done.1 = bf16[128,512]{1,0:T(8,128)(2,1)S(1)} copy-done((bf16[128,512]{1,0:T(8,128)(2,1)S(1)}, bf16[128,512]{1,0:T(8,128)(2,1)}, u32[]{:S(2)}) %copy-start.1) | copy-done | bytes 131096
  30.1 2.9 %sums.6 = (f32[1024,512]{1,0:T(8,128)S(1)}, f32[1024,512]{1,0:T(8,128)S(1)}) custom-call(bf16[128,512]{1,0:T(8,128)(2,1)S(1)} %copy-done.1, bf16[128,512]{1,0:T(8,128)(2,1)S(1)} %collective-permute-done.4.refs_1_, bf16[256,512]{1,0:T(8,128)(2,1)S(1)} %collective-permute-done.6.refs_2_, bf16[2048,512]{1,0:T(8,128)(2,1)S(1)} %copy-done), custom_call_target="tpu_custom_call" | custom-call | flops 1024 | bytes 1024 | tf_op jit(solution)/shard_map/sums/pallas_call | solution.py:217
  32.9 0.0 collective-permute-done.8.refs_1_
  33.0 0.0 copy-done.3
  33.0 2.1 %collective-permute-start.9 = (bf16[128,512]{1,0:T(8,128)(2,1)S(1)}, bf16[128,512]{1,0:T(8,128)(2,1)S(1)}, u32[]{:S(2)}, u32[]{:S(2)}) collective-permute-start(bf16[128,512]{1,0:T(8,128)(2,1)S(1)} %copy-done.3), channel_id=1, source_target_pairs={{0,28},{1,29},{2,30},{3,31},{4,24},{5,25},{6,26},{7,27},{8,20},{9,... | collective-permute-start | bytes 393224 | tf_op jit(solution)/shard_map/ppermute | solution.py:307
  35.1 0.0 collective-permute-done.5.refs_2_
  35.1 2.9 %sums.7 = (f32[1024,512]{1,0:T(8,128)S(1)}, f32[1024,512]{1,0:T(8,128)S(1)}) custom-call(bf16[128,512]{1,0:T(8,128)(2,1)S(1)} %collective-permute-done.2.refs_0_, bf16[128,512]{1,0:T(8,128)(2,1)S(1)} %collective-permute-done.refs_1_, bf16[256,512]{1,0:T(8,128)(2,1)S(1)} %collective-permute-done.5.refs_2_, bf16[2048,512]{1,0:T(8,128)(2,1)S(1)} %copy-done, ...), custom_call_target="tpu_custom_call" | custom-call | flops 1024 | bytes 1024 | tf_op jit(solution)/shard_map/sums/pallas_call | solution.py:217
  38.0 3.4 %collective-permute-done.1.refs_0_ = bf16[128,512]{1,0:T(8,128)(2,1)S(1)} collective-permute-done((bf16[128,512]{1,0:T(8,128)(2,1)}, bf16[128,512]{1,0:T(8,128)(2,1)S(1)}, u32[]{:S(2)}, u32[]{:S(2)}) %collective-permute-start.1) | collective-permute-done | bytes 131104 | tf_op jit(solution)/shard_map/ppermute | solution.py:307
  41.5 0.0 copy-done.2
  41.5 0.0 collective-permute-start.7
  41.5 3.4 %collective-permute-done.12.refs_2_ = bf16[256,512]{1,0:T(8,128)(2,1)S(1)} collective-permute-done((bf16[256,512]{1,0:T(8,128)(2,1)}, bf16[256,512]{1,0:T(8,128)(2,1)S(1)}, u32[]{:S(2)}, u32[]{:S(2)}) %collective-permute-start.12) | collective-permute-done | bytes 262176 | tf_op jit(solution)/shard_map/ppermute | solution.py:307
  44.8 2.9 %sums.8 = (f32[1024,512]{1,0:T(8,128)S(1)}, f32[1024,512]{1,0:T(8,128)S(1)}) custom-call(bf16[128,512]{1,0:T(8,128)(2,1)S(1)} %collective-permute-done.10.refs_0_, bf16[128,512]{1,0:T(8,128)(2,1)S(1)} %collective-permute-done.8.refs_1_, bf16[256,512]{1,0:T(8,128)(2,1)S(1)} %collective-permute-done.12.refs_2_, bf16[2048,512]{1,0:T(8,128)(2,1)S(1)} %copy-done, ...), custom_call_target="tpu_custom_call" | custom-call | flops 1024 | bytes 1024 | tf_op jit(solution)/shard_map/sums/pallas_call | solution.py:217
  47.7 0.0 collective-permute-done.11.refs_1_
  47.7 1.8 %sums.9 = (f32[1024,512]{1,0:T(8,128)S(1)}, f32[1024,512]{1,0:T(8,128)S(1)}) custom-call(bf16[128,512]{1,0:T(8,128)(2,1)S(1)} %collective-permute-done.1.refs_0_, bf16[128,512]{1,0:T(8,128)(2,1)S(1)} %collective-permute-done.11.refs_1_, bf16[2048,512]{1,0:T(8,128)(2,1)S(1)} %copy-done, f32[1024,512]{1,0:T(8,128)S(1)} %get-tuple-element.70.refs_3_, ...), custom_call_target="tpu_custom_call" | custom-call | flops 1024 | bytes 1024 | tf_op jit(solution)/shard_map/sums/pallas_call | solution.py:217
  49.5 3.6 %collective-permute-done.9.refs_0_ = bf16[128,512]{1,0:T(8,128)(2,1)S(1)} collective-permute-done((bf16[128,512]{1,0:T(8,128)(2,1)S(1)}, bf16[128,512]{1,0:T(8,128)(2,1)S(1)}, u32[]{:S(2)}, u32[]{:S(2)}) %collective-permute-start.9) | collective-permute-done | bytes 131104 | tf_op jit(solution)/shard_map/ppermute | solution.py:307
  53.1 1.6 %sums.10 = (f32[1024,512]{1,0:T(8,128)S(1)}, f32[1024,512]{1,0:T(8,128)S(1)}) custom-call(bf16[128,512]{1,0:T(8,128)(2,1)S(1)} %collective-permute-done.9.refs_0_, bf16[2048,512]{1,0:T(8,128)(2,1)S(1)} %copy-done, f32[1024,512]{1,0:T(8,128)S(1)} %get-tuple-element.72.refs_2_, f32[1024,512]{1,0:T(8,128)S(1)} %get-tuple-element.73.refs_3_), custom_call_target="tpu_custom_call" | custom-call | flops 1024 | bytes 1024 | tf_op jit(solution)/shard_map/sums/pallas_call | solution.py:217
  54.6 1.2 %collective-permute-done.7.refs_0_ = bf16[128,512]{1,0:T(8,128)(2,1)S(1)} collective-permute-done((bf16[128,512]{1,0:T(8,128)(2,1)S(1)}, bf16[128,512]{1,0:T(8,128)(2,1)S(1)}, u32[]{:S(2)}, u32[]{:S(2)}) %collective-permute-start.7) | collective-permute-done | bytes 131104 | tf_op jit(solution)/shard_map/ppermute | solution.py:307
  55.9 1.3 %sums.11 = (bf16[1024,128]{1,0:T(8,128)(2,1)S(1)}, f32[512,512]{1,0:T(8,128)S(1)}, f32[512,512]{1,0:T(8,128)S(1)}) custom-call(bf16[128,512]{1,0:T(8,128)(2,1)S(1)} %collective-permute-done.7.refs_0_, bf16[2048,512]{1,0:T(8,128)(2,1)S(1)} %copy-done, f32[1024,512]{1,0:T(8,128)S(1)} %get-tuple-element.74.refs_2_, f32[1024,512]{1,0:T(8,128)S(1)} %get-tuple-element.75.refs_3_), custom_call_target="tpu_custom_call" | custom-call | flops 1024 | bytes 1024 | tf_op jit(solution)/shard_map/sums/pallas_call | solution.py:217
  57.2 0.5 collective-permute-start.14
  57.8 0.1 collective-permute-start.13
  57.9 0.4 own.1
  58.3 1.8 %collective-permute-done.14.refs_0_ = f32[512,512]{1,0:T(8,128)S(1)} collective-permute-done((f32[512,512]{1,0:T(8,128)S(1)}, f32[512,512]{1,0:T(8,128)S(1)}, u32[]{:S(2)}, u32[]{:S(2)}) %collective-permute-start.14) | collective-permute-done | bytes 1048608 | tf_op jit(solution)/shard_map/ppermute | solution.py:341
  60.1 1.0 %close.2.refs_1_ = bf16[1024,512]{1,0:T(8,128)(2,1)} custom-call(f32[1024,512]{1,0:T(8,128)S(1)} %own.1, f32[512,512]{1,0:T(8,128)S(1)} %collective-permute-done.14.refs_0_), custom_call_target="tpu_custom_call" | custom-call | flops 1024 | bytes 1024 | tf_op jit(solution)/shard_map/close/pallas_call | solution.py:275
  61.0 0.5 collective-permute-done.13.refs_0_
  61.6 1.0 %close.3 = bf16[1024,512]{1,0:T(8,128)(2,1)} custom-call(f32[1024,512]{1,0:T(8,128)S(1)} %own.1, f32[512,512]{1,0:T(8,128)S(1)} %collective-permute-done.13.refs_0_, bf16[1024,512]{1,0:T(8,128)(2,1)} %close.2.refs_1_), custom_call_target="tpu_custom_call", output_to_operand_aliasing={{}: (2, {})} | custom-call | flops 1024 | bytes 1024 | tf_op jit(solution)/shard_map/close/pallas_call | solution.py:275
  (1 shorter events, 0.0 us)
Async XLA Ops:
  0.0 29.2 %copy-start = (bf16[2048,512]{1,0:T(8,128)(2,1)S(1)}, bf16[2048,512]{1,0:T(8,128)(2,1)}, u32[]{:S(2)}) copy-start(bf16[2048,512]{1,0:T(8,128)(2,1)} %refs_3_.7) | copy-start | bytes 6291460
  4.0 28.9 %copy-start.3 = (bf16[128,512]{1,0:T(8,128)(2,1)S(1)}, bf16[128,512]{1,0:T(8,128)(2,1)}, u32[]{:S(2)}) copy-start(bf16[128,512]{1,0:T(8,128)(2,1)} %get-tuple-element.63) | copy-start | bytes 393220
  4.0 2.3 %collective-permute-start.3 = (bf16[384,512]{1,0:T(8,128)(2,1)}, bf16[384,512]{1,0:T(8,128)(2,1)S(1)}, u32[]{:S(2)}, u32[]{:S(2)}) collective-permute-start(bf16[384,512]{1,0:T(8,128)(2,1)} %get-tuple-element.47), channel_id=1, source_target_pairs={{0,1},{1,0},{2,3},{3,2},{4,5},{5,4},{6,7},{7,6},{8,9},{9,8},{10,11... | collective-permute-start | bytes 1179656 | tf_op jit(solution)/shard_map/ppermute | solution.py:295
  4.8 6.6 %collective-permute-start.4 = (bf16[128,512]{1,0:T(8,128)(2,1)}, bf16[128,512]{1,0:T(8,128)(2,1)S(1)}, u32[]{:S(2)}, u32[]{:S(2)}) collective-permute-start(bf16[128,512]{1,0:T(8,128)(2,1)} %get-tuple-element.52), channel_id=1, source_target_pairs={{0,2},{1,3},{2,0},{3,1},{4,6},{5,7},{6,4},{7,5},{8,10},{9,11},{10,... | collective-permute-start | bytes 393224 | tf_op jit(solution)/shard_map/ppermute | solution.py:307
  6.0 7.9 %collective-permute-start.2 = (bf16[128,512]{1,0:T(8,128)(2,1)}, bf16[128,512]{1,0:T(8,128)(2,1)S(1)}, u32[]{:S(2)}, u32[]{:S(2)}) collective-permute-start(bf16[128,512]{1,0:T(8,128)(2,1)} %get-tuple-element.46), channel_id=1, source_target_pairs={{0,16},{1,17},{2,18},{3,19},{4,20},{5,21},{6,22},{7,23},{8,24},{9,... | collective-permute-start | bytes 393224 | tf_op jit(solution)/shard_map/ppermute | solution.py:307
  7.1 22.0 %collective-permute-start.6 = (bf16[256,512]{1,0:T(8,128)(2,1)}, bf16[256,512]{1,0:T(8,128)(2,1)S(1)}, u32[]{:S(2)}, u32[]{:S(2)}) collective-permute-start(bf16[256,512]{1,0:T(8,128)(2,1)} %get-tuple-element.55), channel_id=1, source_target_pairs={{0,4},{1,7},{2,6},{3,5},{4,0},{5,3},{6,2},{7,1},{8,12},{9,15},{10,... | collective-permute-start | bytes 786440 | tf_op jit(solution)/shard_map/ppermute | solution.py:307
  9.4 8.5 %collective-permute-start = (bf16[128,512]{1,0:T(8,128)(2,1)}, bf16[128,512]{1,0:T(8,128)(2,1)S(1)}, u32[]{:S(2)}, u32[]{:S(2)}) collective-permute-start(bf16[128,512]{1,0:T(8,128)(2,1)} %get-tuple-element.44), channel_id=1, source_target_pairs={{0,18},{1,19},{2,16},{3,17},{4,22},{5,23},{6,20},{7,21},{8,26},{9,... | collective-permute-start | bytes 393224 | tf_op jit(solution)/shard_map/ppermute | solution.py:307
  11.4 23.7 %collective-permute-start.5 = (bf16[256,512]{1,0:T(8,128)(2,1)}, bf16[256,512]{1,0:T(8,128)(2,1)S(1)}, u32[]{:S(2)}, u32[]{:S(2)}) collective-permute-start(bf16[256,512]{1,0:T(8,128)(2,1)} %get-tuple-element.53), channel_id=1, source_target_pairs={{0,8},{1,11},{2,10},{3,9},{4,12},{5,15},{6,14},{7,13},{8,0},{9,3},... | collective-permute-start | bytes 786440 | tf_op jit(solution)/shard_map/ppermute | solution.py:307
  12.6 12.0 %collective-permute-start.10 = (bf16[128,512]{1,0:T(8,128)(2,1)}, bf16[128,512]{1,0:T(8,128)(2,1)S(1)}, u32[]{:S(2)}, u32[]{:S(2)}) collective-permute-start(bf16[128,512]{1,0:T(8,128)(2,1)} %get-tuple-element.65), channel_id=1, source_target_pairs={{0,20},{1,21},{2,22},{3,23},{4,16},{5,17},{6,18},{7,19},{8,28},{9,... | collective-permute-start | bytes 393224 | tf_op jit(solution)/shard_map/ppermute | solution.py:307
  13.9 19.1 %collective-permute-start.8 = (bf16[128,512]{1,0:T(8,128)(2,1)}, bf16[128,512]{1,0:T(8,128)(2,1)S(1)}, u32[]{:S(2)}, u32[]{:S(2)}) collective-permute-start(bf16[128,512]{1,0:T(8,128)(2,1)} %get-tuple-element.62), channel_id=1, source_target_pairs={{0,22},{1,23},{2,20},{3,21},{4,18},{5,19},{6,16},{7,17},{8,30},{9,... | collective-permute-start | bytes 393224 | tf_op jit(solution)/shard_map/ppermute | solution.py:307
  17.9 26.9 %collective-permute-start.12 = (bf16[256,512]{1,0:T(8,128)(2,1)}, bf16[256,512]{1,0:T(8,128)(2,1)S(1)}, u32[]{:S(2)}, u32[]{:S(2)}) collective-permute-start(bf16[256,512]{1,0:T(8,128)(2,1)} %get-tuple-element.68), channel_id=1, source_target_pairs={{0,12},{1,15},{2,14},{3,13},{4,8},{5,11},{6,10},{7,9},{8,4},{9,7},... | collective-permute-start | bytes 786440 | tf_op jit(solution)/shard_map/ppermute | solution.py:307
  24.6 16.8 %collective-permute-start.1 = (bf16[128,512]{1,0:T(8,128)(2,1)}, bf16[128,512]{1,0:T(8,128)(2,1)S(1)}, u32[]{:S(2)}, u32[]{:S(2)}) collective-permute-start(bf16[128,512]{1,0:T(8,128)(2,1)} %get-tuple-element.45), channel_id=1, source_target_pairs={{0,24},{1,25},{2,26},{3,27},{4,28},{5,29},{6,30},{7,31},{8,16},{9,... | collective-permute-start | bytes 393224 | tf_op jit(solution)/shard_map/ppermute | solution.py:307
  29.2 18.5 %collective-permute-start.11 = (bf16[128,512]{1,0:T(8,128)(2,1)}, bf16[128,512]{1,0:T(8,128)(2,1)S(1)}, u32[]{:S(2)}, u32[]{:S(2)}) collective-permute-start(bf16[128,512]{1,0:T(8,128)(2,1)} %get-tuple-element.66), channel_id=1, source_target_pairs={{0,26},{1,27},{2,24},{3,25},{4,30},{5,31},{6,28},{7,29},{8,18},{9,... | collective-permute-start | bytes 393224 | tf_op jit(solution)/shard_map/ppermute | solution.py:307
  29.2 0.9 %copy-start.1 = (bf16[128,512]{1,0:T(8,128)(2,1)S(1)}, bf16[128,512]{1,0:T(8,128)(2,1)}, u32[]{:S(2)}) copy-start(bf16[128,512]{1,0:T(8,128)(2,1)} %get-tuple-element.54.refs_0_) | copy-start | bytes 393220
  33.0 20.1 %collective-permute-start.9 = (bf16[128,512]{1,0:T(8,128)(2,1)S(1)}, bf16[128,512]{1,0:T(8,128)(2,1)S(1)}, u32[]{:S(2)}, u32[]{:S(2)}) collective-permute-start(bf16[128,512]{1,0:T(8,128)(2,1)S(1)} %copy-done.3), channel_id=1, source_target_pairs={{0,28},{1,29},{2,30},{3,31},{4,24},{5,25},{6,26},{7,27},{8,20},{9,... | collective-permute-start | bytes 393224 | tf_op jit(solution)/shard_map/ppermute | solution.py:307
  35.1 6.3 %copy-start.2 = (bf16[128,512]{1,0:T(8,128)(2,1)S(1)}, bf16[128,512]{1,0:T(8,128)(2,1)}, u32[]{:S(2)}) copy-start(bf16[128,512]{1,0:T(8,128)(2,1)} %get-tuple-element.59) | copy-start | bytes 393220
  41.5 14.4 %collective-permute-start.7 = (bf16[128,512]{1,0:T(8,128)(2,1)S(1)}, bf16[128,512]{1,0:T(8,128)(2,1)S(1)}, u32[]{:S(2)}, u32[]{:S(2)}) collective-permute-start(bf16[128,512]{1,0:T(8,128)(2,1)S(1)} %copy-done.2), channel_id=1, source_target_pairs={{0,30},{1,31},{2,28},{3,29},{4,26},{5,27},{6,24},{7,25},{8,22},{9,... | collective-permute-start | bytes 393224 | tf_op jit(solution)/shard_map/ppermute | solution.py:307
  57.2 2.8 %collective-permute-start.14 = (f32[512,512]{1,0:T(8,128)S(1)}, f32[512,512]{1,0:T(8,128)S(1)}, u32[]{:S(2)}, u32[]{:S(2)}) collective-permute-start(f32[512,512]{1,0:T(8,128)S(1)} %get-tuple-element.78), channel_id=1, source_target_pairs={{0,1},{1,0},{2,3},{3,2},{4,5},{5,4},{6,7},{7,6},{8,9},{9,8},{10,11... | collective-permute-start | bytes 3145736 | tf_op jit(solution)/shard_map/ppermute | solution.py:341
  57.8 3.8 %collective-permute-start.13 = (f32[512,512]{1,0:T(8,128)S(1)}, f32[512,512]{1,0:T(8,128)S(1)}, u32[]{:S(2)}, u32[]{:S(2)}) collective-permute-start(f32[512,512]{1,0:T(8,128)S(1)} %get-tuple-element.77), channel_id=1, source_target_pairs={{0,1},{1,0},{2,3},{3,2},{4,5},{5,4},{6,7},{7,6},{8,9},{9,8},{10,11... | collective-permute-start | bytes 3145736 | tf_op jit(solution)/shard_map/ppermute | solution.py:341

commit v4 on v3

--- a/solution.py
+++ b/solution.py
@@ -47,8 +47,6 @@
         def _():
             where[ids[s]] = s
 
-    for s in range(slots):
-        pltpu.make_async_copy(points.at[s], held.at[s], reads.at[s]).wait()
     targets = [(k, out) for k, out in zip(alone, singles)]
     targets += [(k + 1 - core, give.at[pl.ds(i * rows, rows)]) for i, k in enumerate(paired)]
     targets += [(k + core, out.at[pl.ds(0, rows)]) for k, out in zip(paired, keeps)]
@@ -57,11 +55,19 @@
 
         @pl.when(slot >= 0)
         def _():
-            pltpu.make_async_copy(held.at[jnp.maximum(slot, 0)], out, writes.at[i]).start()
+            at = jnp.maximum(slot, 0)
+            pltpu.make_async_copy(points.at[0], held.at[at], reads.at[at]).wait()
+            pltpu.make_async_copy(held.at[at], out, writes.at[i]).start()
 
         @pl.when(slot < 0)
         def _():
             pltpu.make_async_copy(zeros, out, writes.at[i]).start()
+
+    for s in range(slots):
+
+        @pl.when(s >= counts[0])
+        def _():
+            pltpu.make_async_copy(points.at[s], held.at[s], reads.at[s]).wait()
 
     for i, (k, out) in enumerate(targets):
         pltpu.make_async_copy(zeros, out, writes.at[i]).wait()
@@ -295,6 +301,7 @@
     give = lax.ppermute(give, "copy", [(k, k ^ 1) for k in range(replicas)])
     both = merge([keeps[k] for k in paired], give)
     arrived = {0: singles[0]}
+    centroids = after(centroids, give)
 
     def send(k, *others):
         array = singles[k] if k in singles else both[paired.index(k)]

time: 62.7 us -> 62.6 us (level)
  no operation moved by 1% of the time
where the time goes in v4:
time: 62.6 us; the launch traced here: 62.4 us
  starting transfers between devices  26.1 us (42%)
  Pallas kernels  19.2 us (31%)
  waiting for transfers between devices  15.2 us (24%)
  between operations  0.93 us (1%)
  local copies, waits for them, and re-layouts  0.91 us (1%)
    ppermute x12, starting transfers between devices, send(): arrived[k] = lax.ppermute(array, ('cluster', 'copy'), pairs)  24.3 us
    pallas_call x6, Pallas kernels, sums(): pl.pallas_call(functools.partial(sums_kernel, len(xs), replicas, last), o...  13.3 us
    ppermute x12, waiting for transfers between devices, send(): arrived[k] = lax.ppermute(array, ('cluster', 'copy'), pairs)  12.6 us
    pallas_call x1, Pallas kernels, stage(): pl.pallas_call(functools.partial(stage_kernel, alone, paired), out_shape=...  2.79 us
    ppermute x2, waiting for transfers between devices, local(): lax.ppermute(shares[(r - 1) * HALVES + h], 'copy', [(i, (i + r) % replica...  2.32 us
    pallas_call x2, Pallas kernels, close(): pl.pallas_call(functools.partial(close_kernel, h, terms), out_shape=jax.S...  1.91 us
  transfers between devices with their start and end apart: 15, of which 8 were waited for; matrix products, arithmetic and copies ran while one was open for 0% of the time, Pallas kernels for 23%

profile of v4, /device:TPU:17, one launch (start us, length us, event | category | flops | bytes accessed | tf_op | source)
XLA Modules:
  0.0 62.4 jit_solution(14040804248336190277)
XLA Ops:
  0.0 0.0 copy-start
  0.8 2.8 %stage.1 = (bf16[128,512]{1,0:T(8,128)(2,1)}, bf16[128,512]{1,0:T(8,128)(2,1)}, bf16[128,512]{1,0:T(8,128)(2,1)}, bf16[128,512]{1,0:T(8,128)(2,1)}, bf16[128,512...) custom-call(s32[16]{0:T(128)} %ids_in.1, ...), custom_call_target="tpu_custom_call" | custom-call | tf_op jit(solution)/shard_map/stage/pallas_call | solution.py:80
  3.6 0.0 copy-start.3
  3.6 1.0 %collective-permute-start.3 = (bf16[384,512]{1,0:T(8,128)(2,1)}, bf16[384,512]{1,0:T(8,128)(2,1)S(1)}, u32[]{:S(2)}, u32[]{:S(2)}) collective-permute-start(bf16[384,512]{1,0:T(8,128)(2,1)} %get-tuple-element.48), channel_id=1, source_target_pairs={{0,1},{1,0},{2,3},{3,2},{4,5},{5,4},{6,7},{7,6},{8,9},{9,8},{10,11... | collective-permute-start | bytes 1179656 | tf_op jit(solution)/shard_map/ppermute | solution.py:301
  4.6 1.3 %collective-permute-start.4 = (bf16[128,512]{1,0:T(8,128)(2,1)}, bf16[128,512]{1,0:T(8,128)(2,1)S(1)}, u32[]{:S(2)}, u32[]{:S(2)}) collective-permute-start(bf16[128,512]{1,0:T(8,128)(2,1)} %get-tuple-element.53), channel_id=1, source_target_pairs={{0,2},{1,3},{2,0},{3,1},{4,6},{5,7},{6,4},{7,5},{8,10},{9,11},{10,... | collective-permute-start | bytes 393224 | tf_op jit(solution)/shard_map/ppermute | solution.py:314
  5.9 0.0 collective-permute-start.2
  5.9 0.3 collective-permute-done.3.got
  6.2 0.8 %merge.1 = (bf16[256,512]{1,0:T(8,128)(2,1)}, bf16[256,512]{1,0:T(8,128)(2,1)}, bf16[256,512]{1,0:T(8,128)(2,1)}) custom-call(bf16[384,512]{1,0:T(8,128)(2,1)S(1)} %collective-permute-done.3.got, bf16[256,512]{1,0:T(8,128)(2,1)} %get-tuple-element.49.refs_0_, ...), custom_call_target="tpu_custom_call", output_to_operand_aliasing={{0}: (1, {}), {1}: (2, {}), {2}: (3, {})} | custom-call | tf_op jit(solution)/shard_map/merge/pallas_call | solution.py:115
  7.0 2.2 %collective-permute-start.6 = (bf16[256,512]{1,0:T(8,128)(2,1)}, bf16[256,512]{1,0:T(8,128)(2,1)S(1)}, u32[]{:S(2)}, u32[]{:S(2)}) collective-permute-start(bf16[256,512]{1,0:T(8,128)(2,1)} %get-tuple-element.57), channel_id=1, source_target_pairs={{0,4},{1,7},{2,6},{3,5},{4,0},{5,3},{6,2},{7,1},{8,12},{9,15},{10,... | collective-permute-start | bytes 786440 | tf_op jit(solution)/shard_map/ppermute | solution.py:314
  9.2 2.0 %collective-permute-start = (bf16[128,512]{1,0:T(8,128)(2,1)}, bf16[128,512]{1,0:T(8,128)(2,1)S(1)}, u32[]{:S(2)}, u32[]{:S(2)}) collective-permute-start(bf16[128,512]{1,0:T(8,128)(2,1)} %get-tuple-element.45), channel_id=1, source_target_pairs={{0,18},{1,19},{2,16},{3,17},{4,22},{5,23},{6,20},{7,21},{8,26},{9,... | collective-permute-start | bytes 393224 | tf_op jit(solution)/shard_map/ppermute | solution.py:314
  11.2 0.0 collective-permute-done.4.refs_1_
  11.2 1.1 %collective-permute-start.5 = (bf16[256,512]{1,0:T(8,128)(2,1)}, bf16[256,512]{1,0:T(8,128)(2,1)S(1)}, u32[]{:S(2)}, u32[]{:S(2)}) collective-permute-start(bf16[256,512]{1,0:T(8,128)(2,1)} %get-tuple-element.54), channel_id=1, source_target_pairs={{0,8},{1,11},{2,10},{3,9},{4,12},{5,15},{6,14},{7,13},{8,0},{9,3},... | collective-permute-start | bytes 786440 | tf_op jit(solution)/shard_map/ppermute | solution.py:314
  12.3 1.4 %collective-permute-start.10 = (bf16[128,512]{1,0:T(8,128)(2,1)}, bf16[128,512]{1,0:T(8,128)(2,1)S(1)}, u32[]{:S(2)}, u32[]{:S(2)}) collective-permute-start(bf16[128,512]{1,0:T(8,128)(2,1)} %get-tuple-element.67), channel_id=1, source_target_pairs={{0,20},{1,21},{2,22},{3,23},{4,16},{5,17},{6,18},{7,19},{8,28},{9,... | collective-permute-start | bytes 393224 | tf_op jit(solution)/shard_map/ppermute | solution.py:314
  13.7 0.0 collective-permute-done.2.refs_0_
  13.7 3.0 %collective-permute-start.8 = (bf16[128,512]{1,0:T(8,128)(2,1)}, bf16[128,512]{1,0:T(8,128)(2,1)S(1)}, u32[]{:S(2)}, u32[]{:S(2)}) collective-permute-start(bf16[128,512]{1,0:T(8,128)(2,1)} %get-tuple-element.64), channel_id=1, source_target_pairs={{0,22},{1,23},{2,20},{3,21},{4,18},{5,19},{6,16},{7,17},{8,30},{9,... | collective-permute-start | bytes 393224 | tf_op jit(solution)/shard_map/ppermute | solution.py:314
  16.7 1.0 %collective-permute-done.refs_1_ = bf16[128,512]{1,0:T(8,128)(2,1)S(1)} collective-permute-done((bf16[128,512]{1,0:T(8,128)(2,1)}, bf16[128,512]{1,0:T(8,128)(2,1)S(1)}, u32[]{:S(2)}, u32[]{:S(2)}) %collective-permute-start) | collective-permute-done | bytes 131104 | tf_op jit(solution)/shard_map/ppermute | solution.py:314
  17.7 6.8 %collective-permute-start.12 = (bf16[256,512]{1,0:T(8,128)(2,1)}, bf16[256,512]{1,0:T(8,128)(2,1)S(1)}, u32[]{:S(2)}, u32[]{:S(2)}) collective-permute-start(bf16[256,512]{1,0:T(8,128)(2,1)} %get-tuple-element.70), channel_id=1, source_target_pairs={{0,12},{1,15},{2,14},{3,13},{4,8},{5,11},{6,10},{7,9},{8,4},{9,7},... | collective-permute-start | bytes 786440 | tf_op jit(solution)/shard_map/ppermute | solution.py:314
  24.5 0.0 collective-permute-done.10.refs_0_
  24.5 4.6 %collective-permute-start.1 = (bf16[128,512]{1,0:T(8,128)(2,1)}, bf16[128,512]{1,0:T(8,128)(2,1)S(1)}, u32[]{:S(2)}, u32[]{:S(2)}) collective-permute-start(bf16[128,512]{1,0:T(8,128)(2,1)} %get-tuple-element.46), channel_id=1, source_target_pairs={{0,24},{1,25},{2,26},{3,27},{4,28},{5,29},{6,30},{7,31},{8,16},{9,... | collective-permute-start | bytes 393224 | tf_op jit(solution)/shard_map/ppermute | solution.py:314
  29.1 0.0 collective-permute-done.6.refs_2_
  29.1 0.0 collective-permute-start.11
  29.1 0.0 copy-done
  29.1 0.0 copy-start.1
  29.1 0.9 %copy-done.1 = bf16[128,512]{1,0:T(8,128)(2,1)S(1)} copy-done((bf16[128,512]{1,0:T(8,128)(2,1)S(1)}, bf16[128,512]{1,0:T(8,128)(2,1)}, u32[]{:S(2)}) %copy-start.1) | copy-done | bytes 131096
  30.0 2.9 %sums.6 = (f32[1024,512]{1,0:T(8,128)S(1)}, f32[1024,512]{1,0:T(8,128)S(1)}) custom-call(bf16[128,512]{1,0:T(8,128)(2,1)S(1)} %copy-done.1, bf16[128,512]{1,0:T(8,128)(2,1)S(1)} %collective-permute-done.4.refs_1_, bf16[256,512]{1,0:T(8,128)(2,1)S(1)} %collective-permute-done.6.refs_2_, bf16[2048,512]{1,0:T(8,128)(2,1)S(1)} %copy-done), custom_call_target="tpu_custom_call" | custom-call | flops 1024 | bytes 1024 | tf_op jit(solution)/shard_map/sums/pallas_call | solution.py:223
  32.9 0.0 collective-permute-done.8.refs_1_
  32.9 0.0 copy-done.3
  32.9 2.0 %collective-permute-start.9 = (bf16[128,512]{1,0:T(8,128)(2,1)S(1)}, bf16[128,512]{1,0:T(8,128)(2,1)S(1)}, u32[]{:S(2)}, u32[]{:S(2)}) collective-permute-start(bf16[128,512]{1,0:T(8,128)(2,1)S(1)} %copy-done.3), channel_id=1, source_target_pairs={{0,28},{1,29},{2,30},{3,31},{4,24},{5,25},{6,26},{7,27},{8,20},{9,... | collective-permute-start | bytes 393224 | tf_op jit(solution)/shard_map/ppermute | solution.py:314
  34.9 0.0 collective-permute-done.5.refs_2_
  34.9 2.9 %sums.7 = (f32[1024,512]{1,0:T(8,128)S(1)}, f32[1024,512]{1,0:T(8,128)S(1)}) custom-call(bf16[128,512]{1,0:T(8,128)(2,1)S(1)} %collective-permute-done.2.refs_0_, bf16[128,512]{1,0:T(8,128)(2,1)S(1)} %collective-permute-done.refs_1_, bf16[256,512]{1,0:T(8,128)(2,1)S(1)} %collective-permute-done.5.refs_2_, bf16[2048,512]{1,0:T(8,128)(2,1)S(1)} %copy-done, ...), custom_call_target="tpu_custom_call" | custom-call | flops 1024 | bytes 1024 | tf_op jit(solution)/shard_map/sums/pallas_call | solution.py:223
  37.8 3.6 %collective-permute-done.1.refs_0_ = bf16[128,512]{1,0:T(8,128)(2,1)S(1)} collective-permute-done((bf16[128,512]{1,0:T(8,128)(2,1)}, bf16[128,512]{1,0:T(8,128)(2,1)S(1)}, u32[]{:S(2)}, u32[]{:S(2)}) %collective-permute-start.1) | collective-permute-done | bytes 131104 | tf_op jit(solution)/shard_map/ppermute | solution.py:314
  41.4 0.0 copy-done.2
  41.4 0.0 collective-permute-start.7
  41.4 3.4 %collective-permute-done.12.refs_2_ = bf16[256,512]{1,0:T(8,128)(2,1)S(1)} collective-permute-done((bf16[256,512]{1,0:T(8,128)(2,1)}, bf16[256,512]{1,0:T(8,128)(2,1)S(1)}, u32[]{:S(2)}, u32[]{:S(2)}) %collective-permute-start.12) | collective-permute-done | bytes 262176 | tf_op jit(solution)/shard_map/ppermute | solution.py:314
  44.7 2.9 %sums.8 = (f32[1024,512]{1,0:T(8,128)S(1)}, f32[1024,512]{1,0:T(8,128)S(1)}) custom-call(bf16[128,512]{1,0:T(8,128)(2,1)S(1)} %collective-permute-done.10.refs_0_, bf16[128,512]{1,0:T(8,128)(2,1)S(1)} %collective-permute-done.8.refs_1_, bf16[256,512]{1,0:T(8,128)(2,1)S(1)} %collective-permute-done.12.refs_2_, bf16[2048,512]{1,0:T(8,128)(2,1)S(1)} %copy-done, ...), custom_call_target="tpu_custom_call" | custom-call | flops 1024 | bytes 1024 | tf_op jit(solution)/shard_map/sums/pallas_call | solution.py:223
  47.6 0.0 collective-permute-done.11.refs_1_
  47.6 1.8 %sums.9 = (f32[1024,512]{1,0:T(8,128)S(1)}, f32[1024,512]{1,0:T(8,128)S(1)}) custom-call(bf16[128,512]{1,0:T(8,128)(2,1)S(1)} %collective-permute-done.1.refs_0_, bf16[128,512]{1,0:T(8,128)(2,1)S(1)} %collective-permute-done.11.refs_1_, bf16[2048,512]{1,0:T(8,128)(2,1)S(1)} %copy-done, f32[1024,512]{1,0:T(8,128)S(1)} %get-tuple-element.72.refs_3_, ...), custom_call_target="tpu_custom_call" | custom-call | flops 1024 | bytes 1024 | tf_op jit(solution)/shard_map/sums/pallas_call | solution.py:223
  49.4 3.5 %collective-permute-done.9.refs_0_ = bf16[128,512]{1,0:T(8,128)(2,1)S(1)} collective-permute-done((bf16[128,512]{1,0:T(8,128)(2,1)S(1)}, bf16[128,512]{1,0:T(8,128)(2,1)S(1)}, u32[]{:S(2)}, u32[]{:S(2)}) %collective-permute-start.9) | collective-permute-done | bytes 131104 | tf_op jit(solution)/shard_map/ppermute | solution.py:314
  52.9 1.6 %sums.10 = (f32[1024,512]{1,0:T(8,128)S(1)}, f32[1024,512]{1,0:T(8,128)S(1)}) custom-call(bf16[128,512]{1,0:T(8,128)(2,1)S(1)} %collective-permute-done.9.refs_0_, bf16[2048,512]{1,0:T(8,128)(2,1)S(1)} %copy-done, f32[1024,512]{1,0:T(8,128)S(1)} %get-tuple-element.74.refs_2_, f32[1024,512]{1,0:T(8,128)S(1)} %get-tuple-element.75.refs_3_), custom_call_target="tpu_custom_call" | custom-call | flops 1024 | bytes 1024 | tf_op jit(solution)/shard_map/sums/pallas_call | solution.py:223
  54.5 1.1 %collective-permute-done.7.refs_0_ = bf16[128,512]{1,0:T(8,128)(2,1)S(1)} collective-permute-done((bf16[128,512]{1,0:T(8,128)(2,1)S(1)}, bf16[128,512]{1,0:T(8,128)(2,1)S(1)}, u32[]{:S(2)}, u32[]{:S(2)}) %collective-permute-start.7) | collective-permute-done | bytes 131104 | tf_op jit(solution)/shard_map/ppermute | solution.py:314
  55.6 1.3 %sums.11 = (bf16[1024,128]{1,0:T(8,128)(2,1)S(1)}, f32[512,512]{1,0:T(8,128)S(1)}, f32[512,512]{1,0:T(8,128)S(1)}) custom-call(bf16[128,512]{1,0:T(8,128)(2,1)S(1)} %collective-permute-done.7.refs_0_, bf16[2048,512]{1,0:T(8,128)(2,1)S(1)} %copy-done, f32[1024,512]{1,0:T(8,128)S(1)} %get-tuple-element.76.refs_2_, f32[1024,512]{1,0:T(8,128)S(1)} %get-tuple-element.77.refs_3_), custom_call_target="tpu_custom_call" | custom-call | flops 1024 | bytes 1024 | tf_op jit(solution)/shard_map/sums/pallas_call | solution.py:223
  56.9 0.7 %collective-permute-start.14 = (f32[512,512]{1,0:T(8,128)S(1)}, f32[512,512]{1,0:T(8,128)S(1)}, u32[]{:S(2)}, u32[]{:S(2)}) collective-permute-start(f32[512,512]{1,0:T(8,128)S(1)} %get-tuple-element.80), channel_id=1, source_target_pairs={{0,1},{1,0},{2,3},{3,2},{4,5},{5,4},{6,7},{7,6},{8,9},{9,8},{10,11... | collective-permute-start | bytes 3145736 | tf_op jit(solution)/shard_map/ppermute | solution.py:348
  57.6 0.1 collective-permute-start.13
  57.7 0.4 own.1
  58.1 1.8 %collective-permute-done.14.refs_0_ = f32[512,512]{1,0:T(8,128)S(1)} collective-permute-done((f32[512,512]{1,0:T(8,128)S(1)}, f32[512,512]{1,0:T(8,128)S(1)}, u32[]{:S(2)}, u32[]{:S(2)}) %collective-permute-start.14) | collective-permute-done | bytes 1048608 | tf_op jit(solution)/shard_map/ppermute | solution.py:348
  59.9 1.0 %close.2.refs_1_ = bf16[1024,512]{1,0:T(8,128)(2,1)} custom-call(f32[1024,512]{1,0:T(8,128)S(1)} %own.1, f32[512,512]{1,0:T(8,128)S(1)} %collective-permute-done.14.refs_0_), custom_call_target="tpu_custom_call" | custom-call | flops 1024 | bytes 1024 | tf_op jit(solution)/shard_map/close/pallas_call | solution.py:281
  60.9 0.5 collective-permute-done.13.refs_0_
  61.4 1.0 %close.3 = bf16[1024,512]{1,0:T(8,128)(2,1)} custom-call(f32[1024,512]{1,0:T(8,128)S(1)} %own.1, f32[512,512]{1,0:T(8,128)S(1)} %collective-permute-done.13.refs_0_, bf16[1024,512]{1,0:T(8,128)(2,1)} %close.2.refs_1_), custom_call_target="tpu_custom_call", output_to_operand_aliasing={{}: (2, {})} | custom-call | flops 1024 | bytes 1024 | tf_op jit(solution)/shard_map/close/pallas_call | solution.py:281
  (1 shorter events, 0.0 us)
Async XLA Ops:
  0.0 29.1 %copy-start = (bf16[2048,512]{1,0:T(8,128)(2,1)S(1)}, bf16[2048,512]{1,0:T(8,128)(2,1)}, u32[]{:S(2)}) copy-start(bf16[2048,512]{1,0:T(8,128)(2,1)} %refs_3_.3) | copy-start | bytes 6291460
  3.6 29.3 %copy-start.3 = (bf16[128,512]{1,0:T(8,128)(2,1)S(1)}, bf16[128,512]{1,0:T(8,128)(2,1)}, u32[]{:S(2)}) copy-start(bf16[128,512]{1,0:T(8,128)(2,1)} %get-tuple-element.65) | copy-start | bytes 393220
  3.6 2.6 %collective-permute-start.3 = (bf16[384,512]{1,0:T(8,128)(2,1)}, bf16[384,512]{1,0:T(8,128)(2,1)S(1)}, u32[]{:S(2)}, u32[]{:S(2)}) collective-permute-start(bf16[384,512]{1,0:T(8,128)(2,1)} %get-tuple-element.48), channel_id=1, source_target_pairs={{0,1},{1,0},{2,3},{3,2},{4,5},{5,4},{6,7},{7,6},{8,9},{9,8},{10,11... | collective-permute-start | bytes 1179656 | tf_op jit(solution)/shard_map/ppermute | solution.py:301
  4.6 6.6 %collective-permute-start.4 = (bf16[128,512]{1,0:T(8,128)(2,1)}, bf16[128,512]{1,0:T(8,128)(2,1)S(1)}, u32[]{:S(2)}, u32[]{:S(2)}) collective-permute-start(bf16[128,512]{1,0:T(8,128)(2,1)} %get-tuple-element.53), channel_id=1, source_target_pairs={{0,2},{1,3},{2,0},{3,1},{4,6},{5,7},{6,4},{7,5},{8,10},{9,11},{10,... | collective-permute-start | bytes 393224 | tf_op jit(solution)/shard_map/ppermute | solution.py:314
  5.9 7.8 %collective-permute-start.2 = (bf16[128,512]{1,0:T(8,128)(2,1)}, bf16[128,512]{1,0:T(8,128)(2,1)S(1)}, u32[]{:S(2)}, u32[]{:S(2)}) collective-permute-start(bf16[128,512]{1,0:T(8,128)(2,1)} %get-tuple-element.47), channel_id=1, source_target_pairs={{0,16},{1,17},{2,18},{3,19},{4,20},{5,21},{6,22},{7,23},{8,24},{9,... | collective-permute-start | bytes 393224 | tf_op jit(solution)/shard_map/ppermute | solution.py:314
  7.0 22.1 %collective-permute-start.6 = (bf16[256,512]{1,0:T(8,128)(2,1)}, bf16[256,512]{1,0:T(8,128)(2,1)S(1)}, u32[]{:S(2)}, u32[]{:S(2)}) collective-permute-start(bf16[256,512]{1,0:T(8,128)(2,1)} %get-tuple-element.57), channel_id=1, source_target_pairs={{0,4},{1,7},{2,6},{3,5},{4,0},{5,3},{6,2},{7,1},{8,12},{9,15},{10,... | collective-permute-start | bytes 786440 | tf_op jit(solution)/shard_map/ppermute | solution.py:314
  9.2 8.5 %collective-permute-start = (bf16[128,512]{1,0:T(8,128)(2,1)}, bf16[128,512]{1,0:T(8,128)(2,1)S(1)}, u32[]{:S(2)}, u32[]{:S(2)}) collective-permute-start(bf16[128,512]{1,0:T(8,128)(2,1)} %get-tuple-element.45), channel_id=1, source_target_pairs={{0,18},{1,19},{2,16},{3,17},{4,22},{5,23},{6,20},{7,21},{8,26},{9,... | collective-permute-start | bytes 393224 | tf_op jit(solution)/shard_map/ppermute | solution.py:314
  11.2 23.7 %collective-permute-start.5 = (bf16[256,512]{1,0:T(8,128)(2,1)}, bf16[256,512]{1,0:T(8,128)(2,1)S(1)}, u32[]{:S(2)}, u32[]{:S(2)}) collective-permute-start(bf16[256,512]{1,0:T(8,128)(2,1)} %get-tuple-element.54), channel_id=1, source_target_pairs={{0,8},{1,11},{2,10},{3,9},{4,12},{5,15},{6,14},{7,13},{8,0},{9,3},... | collective-permute-start | bytes 786440 | tf_op jit(solution)/shard_map/ppermute | solution.py:314
  12.3 12.2 %collective-permute-start.10 = (bf16[128,512]{1,0:T(8,128)(2,1)}, bf16[128,512]{1,0:T(8,128)(2,1)S(1)}, u32[]{:S(2)}, u32[]{:S(2)}) collective-permute-start(bf16[128,512]{1,0:T(8,128)(2,1)} %get-tuple-element.67), channel_id=1, source_target_pairs={{0,20},{1,21},{2,22},{3,23},{4,16},{5,17},{6,18},{7,19},{8,28},{9,... | collective-permute-start | bytes 393224 | tf_op jit(solution)/shard_map/ppermute | solution.py:314
  13.7 19.2 %collective-permute-start.8 = (bf16[128,512]{1,0:T(8,128)(2,1)}, bf16[128,512]{1,0:T(8,128)(2,1)S(1)}, u32[]{:S(2)}, u32[]{:S(2)}) collective-permute-start(bf16[128,512]{1,0:T(8,128)(2,1)} %get-tuple-element.64), channel_id=1, source_target_pairs={{0,22},{1,23},{2,20},{3,21},{4,18},{5,19},{6,16},{7,17},{8,30},{9,... | collective-permute-start | bytes 393224 | tf_op jit(solution)/shard_map/ppermute | solution.py:314
  17.7 27.0 %collective-permute-start.12 = (bf16[256,512]{1,0:T(8,128)(2,1)}, bf16[256,512]{1,0:T(8,128)(2,1)S(1)}, u32[]{:S(2)}, u32[]{:S(2)}) collective-permute-start(bf16[256,512]{1,0:T(8,128)(2,1)} %get-tuple-element.70), channel_id=1, source_target_pairs={{0,12},{1,15},{2,14},{3,13},{4,8},{5,11},{6,10},{7,9},{8,4},{9,7},... | collective-permute-start | bytes 786440 | tf_op jit(solution)/shard_map/ppermute | solution.py:314
  24.5 16.9 %collective-permute-start.1 = (bf16[128,512]{1,0:T(8,128)(2,1)}, bf16[128,512]{1,0:T(8,128)(2,1)S(1)}, u32[]{:S(2)}, u32[]{:S(2)}) collective-permute-start(bf16[128,512]{1,0:T(8,128)(2,1)} %get-tuple-element.46), channel_id=1, source_target_pairs={{0,24},{1,25},{2,26},{3,27},{4,28},{5,29},{6,30},{7,31},{8,16},{9,... | collective-permute-start | bytes 393224 | tf_op jit(solution)/shard_map/ppermute | solution.py:314
  29.1 18.5 %collective-permute-start.11 = (bf16[128,512]{1,0:T(8,128)(2,1)}, bf16[128,512]{1,0:T(8,128)(2,1)S(1)}, u32[]{:S(2)}, u32[]{:S(2)}) collective-permute-start(bf16[128,512]{1,0:T(8,128)(2,1)} %get-tuple-element.68), channel_id=1, source_target_pairs={{0,26},{1,27},{2,24},{3,25},{4,30},{5,31},{6,28},{7,29},{8,18},{9,... | collective-permute-start | bytes 393224 | tf_op jit(solution)/shard_map/ppermute | solution.py:314
  29.1 0.9 %copy-start.1 = (bf16[128,512]{1,0:T(8,128)(2,1)S(1)}, bf16[128,512]{1,0:T(8,128)(2,1)}, u32[]{:S(2)}) copy-start(bf16[128,512]{1,0:T(8,128)(2,1)} %get-tuple-element.56.refs_0_) | copy-start | bytes 393220
  32.9 20.0 %collective-permute-start.9 = (bf16[128,512]{1,0:T(8,128)(2,1)S(1)}, bf16[128,512]{1,0:T(8,128)(2,1)S(1)}, u32[]{:S(2)}, u32[]{:S(2)}) collective-permute-start(bf16[128,512]{1,0:T(8,128)(2,1)S(1)} %copy-done.3), channel_id=1, source_target_pairs={{0,28},{1,29},{2,30},{3,31},{4,24},{5,25},{6,26},{7,27},{8,20},{9,... | collective-permute-start | bytes 393224 | tf_op jit(solution)/shard_map/ppermute | solution.py:314
  34.9 6.5 %copy-start.2 = (bf16[128,512]{1,0:T(8,128)(2,1)S(1)}, bf16[128,512]{1,0:T(8,128)(2,1)}, u32[]{:S(2)}) copy-start(bf16[128,512]{1,0:T(8,128)(2,1)} %get-tuple-element.61) | copy-start | bytes 393220
  41.4 14.2 %collective-permute-start.7 = (bf16[128,512]{1,0:T(8,128)(2,1)S(1)}, bf16[128,512]{1,0:T(8,128)(2,1)S(1)}, u32[]{:S(2)}, u32[]{:S(2)}) collective-permute-start(bf16[128,512]{1,0:T(8,128)(2,1)S(1)} %copy-done.2), channel_id=1, source_target_pairs={{0,30},{1,31},{2,28},{3,29},{4,26},{5,27},{6,24},{7,25},{8,22},{9,... | collective-permute-start | bytes 393224 | tf_op jit(solution)/shard_map/ppermute | solution.py:314
  56.9 3.0 %collective-permute-start.14 = (f32[512,512]{1,0:T(8,128)S(1)}, f32[512,512]{1,0:T(8,128)S(1)}, u32[]{:S(2)}, u32[]{:S(2)}) collective-permute-start(f32[512,512]{1,0:T(8,128)S(1)} %get-tuple-element.80), channel_id=1, source_target_pairs={{0,1},{1,0},{2,3},{3,2},{4,5},{5,4},{6,7},{7,6},{8,9},{9,8},{10,11... | collective-permute-start | bytes 3145736 | tf_op jit(solution)/shard_map/ppermute | solution.py:348
  57.6 3.8 %collective-permute-start.13 = (f32[512,512]{1,0:T(8,128)S(1)}, f32[512,512]{1,0:T(8,128)S(1)}, u32[]{:S(2)}, u32[]{:S(2)}) collective-permute-start(f32[512,512]{1,0:T(8,128)S(1)} %get-tuple-element.79), channel_id=1, source_target_pairs={{0,1},{1,0},{2,3},{3,2},{4,5},{5,4},{6,7},{7,6},{8,9},{9,8},{10,11... | collective-permute-start | bytes 3145736 | tf_op jit(solution)/shard_map/ppermute | solution.py:348

commit v5 on v4

--- a/solution.py
+++ b/solution.py
@@ -30,7 +30,7 @@
 
 def stage_kernel(alone, paired, ids_in, counts, points, *refs):
     singles, rest = refs[: len(alone)], refs[len(alone) :]
-    keeps, (give, where, ids, held, zeros, reads, writes, small) = rest[: len(paired)], rest[len(paired) :]
+    kept, give, where, ids, held, zeros, reads, writes, small = rest
     slots, rows = points.shape[:2]
     me, core = lax.axis_index("cluster"), lax.rem(lax.axis_index("copy"), 2)
     ids_copy = pltpu.make_async_copy(ids_in, ids, small)
@@ -49,7 +49,8 @@
 
     targets = [(k, out) for k, out in zip(alone, singles)]
     targets += [(k + 1 - core, give.at[pl.ds(i * rows, rows)]) for i, k in enumerate(paired)]
-    targets += [(k + core, out.at[pl.ds(0, rows)]) for k, out in zip(paired, keeps)]
+    targets += [(k + core, kept.at[pl.ds(i * rows, rows)]) for i, k in enumerate(paired)]
+    targets += [(0, kept.at[pl.ds(len(paired) * rows, rows)])]
     for i, (k, out) in enumerate(targets):
         slot = where[me ^ k]
 
@@ -79,49 +80,52 @@
     hbm = lambda n: pltpu.HBM((n, feature), points.dtype)
     outs = pl.pallas_call(
         functools.partial(stage_kernel, alone, paired),
-        out_shape=[hbm(rows)] * len(alone) + [hbm(2 * rows)] * len(paired) + [hbm(len(paired) * rows)],
+        out_shape=[hbm(rows)] * len(alone) + [hbm((1 + len(paired)) * rows), hbm(len(paired) * rows)],
         in_specs=[spec, pl.BlockSpec(memory_space=pltpu.SMEM), spec],
-        out_specs=[spec] * (len(alone) + len(paired) + 1),
+        out_specs=[spec] * (len(alone) + 2),
         scratch_shapes=[
             pltpu.SMEM((owners,), jnp.int32),
             pltpu.SMEM(ids.shape, jnp.int32),
             pltpu.VMEM(points.shape, points.dtype),
             pltpu.VMEM((rows, feature), points.dtype),
             pltpu.SemaphoreType.DMA((points.shape[0],)),
-            pltpu.SemaphoreType.DMA((len(alone) + 2 * len(paired),)),
+            pltpu.SemaphoreType.DMA((len(alone) + 2 * len(paired) + 1,)),
             pltpu.SemaphoreType.DMA,
         ],
         compiler_params=pltpu.CompilerParams(vmem_limit_bytes=16 * MIB),
         name="stage",
     )(in_hbm(ids), counts, in_hbm(points))
-    return dict(zip(alone, outs)), dict(zip(paired, outs[len(alone) : -1])), outs[-1]
-
-
-def merge_kernel(got, *refs):
-    outs, sems = refs[len(refs) // 2 : -1], refs[-1]
-    rows = got.shape[0] // len(outs)
-    copies = [
-        pltpu.make_async_copy(got.at[pl.ds(i * rows, rows)], out.at[pl.ds(rows, rows)], sems.at[i])
-        for i, out in enumerate(outs)
-    ]
+    return dict(zip(alone, outs)), outs[-2], outs[-1]
+
+
+def merge_kernel(kept, got, *refs):
+    outs, own, sems = refs[:-2], refs[-2], refs[-1]
+    rows = own.shape[0]
+    copies = []
+    for i, out in enumerate(outs):
+        for j, source in enumerate((kept, got)):
+            there = out.at[pl.ds(j * rows, rows)]
+            copies.append(pltpu.make_async_copy(source.at[pl.ds(i * rows, rows)], there, sems.at[i, j]))
+    copies.append(pltpu.make_async_copy(kept.at[pl.ds(len(outs) * rows, rows)], own, sems.at[len(outs), 0]))
     for copy in copies:
         copy.start()
     for copy in copies:
         copy.wait()
 
 
-def merge(keeps, got):
-    spec = pl.BlockSpec(memory_space=pltpu.HBM)
+def merge(kept, got, rows):
+    pairs = got.shape[0] // rows
+    hbm, vmem = pl.BlockSpec(memory_space=pltpu.HBM), pl.BlockSpec(memory_space=pltpu.VMEM)
     return pl.pallas_call(
         merge_kernel,
-        out_shape=[pltpu.HBM(k.shape, k.dtype) for k in keeps],
-        in_specs=[pl.BlockSpec(memory_space=pltpu.VMEM)] + [spec] * len(keeps),
-        out_specs=[spec] * len(keeps),
-        input_output_aliases={1 + i: i for i in range(len(keeps))},
-        scratch_shapes=[pltpu.SemaphoreType.DMA((len(keeps),))],
+        out_shape=[pltpu.HBM((2 * rows, got.shape[1]), got.dtype)] * pairs
+        + [jax.ShapeDtypeStruct((rows, got.shape[1]), got.dtype)],
+        in_specs=[vmem, vmem],
+        out_specs=[hbm] * pairs + [vmem],
+        scratch_shapes=[pltpu.SemaphoreType.DMA((pairs + 1, 2))],
         compiler_params=pltpu.CompilerParams(vmem_limit_bytes=16 * MIB),
         name="merge",
-    )(in_vmem(got), *keeps)
+    )(in_vmem(kept), in_vmem(got))
 
 
 def turns(xs):
@@ -297,10 +301,10 @@
     assert owners >= 16 and owners & (owners - 1) == 0 and replicas % 2 == 0
     half = owners // 2
     far, paired = list(range(half, owners)), list(range(2, half, 2))
-    singles, keeps, give = stage(points, block_ids, block_counts, owners, far + [0, 1], paired)
+    singles, kept, give = stage(points, block_ids, block_counts, owners, far + [1], paired)
     give = lax.ppermute(give, "copy", [(k, k ^ 1) for k in range(replicas)])
-    both = merge([keeps[k] for k in paired], give)
-    arrived = {0: singles[0]}
+    *both, mine = merge(kept, give, points.shape[1])
+    arrived = {0: mine}
     centroids = after(centroids, give)
 
     def send(k, *others):

time: 62.6 us -> 62.6 us (level)
  starting transfers between devices: 26.1 us -> 25.2 us
where the time goes in v5:
time: 62.6 us; the launch traced here: 62.5 us
  starting transfers between devices  25.2 us (40%)
  Pallas kernels  19.6 us (31%)
  waiting for transfers between devices  15.7 us (25%)
  local copies, waits for them, and re-layouts  1.05 us (2%)
  between operations  0.92 us (1%)
    ppermute x12, starting transfers between devices, send(): arrived[k] = lax.ppermute(array, ('cluster', 'copy'), pairs)  23.9 us
    pallas_call x6, Pallas kernels, sums(): pl.pallas_call(functools.partial(sums_kernel, len(xs), replicas, last), o...  13.3 us
    ppermute x12, waiting for transfers between devices, send(): arrived[k] = lax.ppermute(array, ('cluster', 'copy'), pairs)  13.2 us
    pallas_call x1, Pallas kernels, stage(): pl.pallas_call(functools.partial(stage_kernel, alone, paired), out_shape=...  3.02 us
    ppermute x2, waiting for transfers between devices, local(): lax.ppermute(shares[(r - 1) * HALVES + h], 'copy', [(i, (i + r) % replica...  2.32 us
    pallas_call x2, Pallas kernels, close(): pl.pallas_call(functools.partial(close_kernel, h, terms), out_shape=jax.S...  1.91 us
  transfers between devices with their start and end apart: 15, of which 8 were waited for; matrix products, arithmetic and copies ran while one was open for 0% of the time, Pallas kernels for 23%

profile of v5, /device:TPU:17, one launch (start us, length us, event | category | flops | bytes accessed | tf_op | source)
XLA Modules:
  0.0 62.5 jit_solution(3983174754037996614)
XLA Ops:
  0.0 0.0 copy-start
  0.8 3.0 %stage.1 = (bf16[128,512]{1,0:T(8,128)(2,1)}, bf16[128,512]{1,0:T(8,128)(2,1)}, bf16[128,512]{1,0:T(8,128)(2,1)}, bf16[128,512]{1,0:T(8,128)(2,1)}, bf16[128,512...) custom-call(s32[16]{0:T(128)} %ids_in.1, ...), custom_call_target="tpu_custom_call" | custom-call | tf_op jit(solution)/shard_map/stage/pallas_call | solution.py:81
  3.8 0.7 %collective-permute-start.3 = (bf16[384,512]{1,0:T(8,128)(2,1)}, bf16[384,512]{1,0:T(8,128)(2,1)S(1)}, u32[]{:S(2)}, u32[]{:S(2)}) collective-permute-start(bf16[384,512]{1,0:T(8,128)(2,1)} %get-tuple-element.47), channel_id=1, source_target_pairs={{0,1},{1,0},{2,3},{3,2},{4,5},{5,4},{6,7},{7,6},{8,9},{9,8},{10,11... | collective-permute-start | bytes 1179656 | tf_op jit(solution)/shard_map/ppermute | solution.py:305
  4.5 1.4 %collective-permute-start.4 = (bf16[128,512]{1,0:T(8,128)(2,1)}, bf16[128,512]{1,0:T(8,128)(2,1)S(1)}, u32[]{:S(2)}, u32[]{:S(2)}) collective-permute-start(bf16[128,512]{1,0:T(8,128)(2,1)} %get-tuple-element.49), channel_id=1, source_target_pairs={{0,2},{1,3},{2,0},{3,1},{4,6},{5,7},{6,4},{7,5},{8,10},{9,11},{10,... | collective-permute-start | bytes 393224 | tf_op jit(solution)/shard_map/ppermute | solution.py:318
  5.9 0.0 collective-permute-start.2
  5.9 0.2 collective-permute-done.3.got
  6.0 0.0 copy-start.1
  6.1 1.0 %copy-done.1 = bf16[512,512]{1,0:T(8,128)(2,1)S(1)} copy-done((bf16[512,512]{1,0:T(8,128)(2,1)S(1)}, bf16[512,512]{1,0:T(8,128)(2,1)}, u32[]{:S(2)}) %copy-start.1) | copy-done | bytes 524312
  7.1 0.0 copy-start.3
  7.1 0.9 %merge.1 = (bf16[256,512]{1,0:T(8,128)(2,1)}, bf16[256,512]{1,0:T(8,128)(2,1)}, bf16[256,512]{1,0:T(8,128)(2,1)}, bf16[128,512]{1,0:T(8,128)(2,1)S(1)}) custom-call(bf16[512,512]{1,0:T(8,128)(2,1)S(1)} %copy-done.1, bf16[384,512]{1,0:T(8,128)(2,1)S(1)} %collective-permute-done.3.got), custom_call_target="tpu_custom_call" | custom-call | tf_op jit(solution)/shard_map/merge/pallas_call | solution.py:119
  8.0 2.3 %collective-permute-start.6 = (bf16[256,512]{1,0:T(8,128)(2,1)}, bf16[256,512]{1,0:T(8,128)(2,1)S(1)}, u32[]{:S(2)}, u32[]{:S(2)}) collective-permute-start(bf16[256,512]{1,0:T(8,128)(2,1)} %get-tuple-element.53), channel_id=1, source_target_pairs={{0,4},{1,7},{2,6},{3,5},{4,0},{5,3},{6,2},{7,1},{8,12},{9,15},{10,... | collective-permute-start | bytes 786440 | tf_op jit(solution)/shard_map/ppermute | solution.py:318
  10.4 2.0 %collective-permute-start = (bf16[128,512]{1,0:T(8,128)(2,1)}, bf16[128,512]{1,0:T(8,128)(2,1)S(1)}, u32[]{:S(2)}, u32[]{:S(2)}) collective-permute-start(bf16[128,512]{1,0:T(8,128)(2,1)} %get-tuple-element.43), channel_id=1, source_target_pairs={{0,18},{1,19},{2,16},{3,17},{4,22},{5,23},{6,20},{7,21},{8,26},{9,... | collective-permute-start | bytes 393224 | tf_op jit(solution)/shard_map/ppermute | solution.py:318
  12.4 0.0 collective-permute-done.4.refs_1_
  12.4 1.3 %collective-permute-start.5 = (bf16[256,512]{1,0:T(8,128)(2,1)}, bf16[256,512]{1,0:T(8,128)(2,1)S(1)}, u32[]{:S(2)}, u32[]{:S(2)}) collective-permute-start(bf16[256,512]{1,0:T(8,128)(2,1)} %get-tuple-element.50), channel_id=1, source_target_pairs={{0,8},{1,11},{2,10},{3,9},{4,12},{5,15},{6,14},{7,13},{8,0},{9,3},... | collective-permute-start | bytes 786440 | tf_op jit(solution)/shard_map/ppermute | solution.py:318
  13.6 1.2 %collective-permute-start.10 = (bf16[128,512]{1,0:T(8,128)(2,1)}, bf16[128,512]{1,0:T(8,128)(2,1)S(1)}, u32[]{:S(2)}, u32[]{:S(2)}) collective-permute-start(bf16[128,512]{1,0:T(8,128)(2,1)} %get-tuple-element.63), channel_id=1, source_target_pairs={{0,20},{1,21},{2,22},{3,23},{4,16},{5,17},{6,18},{7,19},{8,28},{9,... | collective-permute-start | bytes 393224 | tf_op jit(solution)/shard_map/ppermute | solution.py:318
  14.9 0.0 collective-permute-done.2.refs_0_
  14.9 2.9 %collective-permute-start.8 = (bf16[128,512]{1,0:T(8,128)(2,1)}, bf16[128,512]{1,0:T(8,128)(2,1)S(1)}, u32[]{:S(2)}, u32[]{:S(2)}) collective-permute-start(bf16[128,512]{1,0:T(8,128)(2,1)} %get-tuple-element.60), channel_id=1, source_target_pairs={{0,22},{1,23},{2,20},{3,21},{4,18},{5,19},{6,16},{7,17},{8,30},{9,... | collective-permute-start | bytes 393224 | tf_op jit(solution)/shard_map/ppermute | solution.py:318
  17.7 0.7 %collective-permute-done.refs_1_ = bf16[128,512]{1,0:T(8,128)(2,1)S(1)} collective-permute-done((bf16[128,512]{1,0:T(8,128)(2,1)}, bf16[128,512]{1,0:T(8,128)(2,1)S(1)}, u32[]{:S(2)}, u32[]{:S(2)}) %collective-permute-start) | collective-permute-done | bytes 131104 | tf_op jit(solution)/shard_map/ppermute | solution.py:318
  18.4 5.4 %collective-permute-start.12 = (bf16[256,512]{1,0:T(8,128)(2,1)}, bf16[256,512]{1,0:T(8,128)(2,1)S(1)}, u32[]{:S(2)}, u32[]{:S(2)}) collective-permute-start(bf16[256,512]{1,0:T(8,128)(2,1)} %get-tuple-element.66), channel_id=1, source_target_pairs={{0,12},{1,15},{2,14},{3,13},{4,8},{5,11},{6,10},{7,9},{8,4},{9,7},... | collective-permute-start | bytes 786440 | tf_op jit(solution)/shard_map/ppermute | solution.py:318
  23.9 0.9 %collective-permute-done.10.refs_0_ = bf16[128,512]{1,0:T(8,128)(2,1)S(1)} collective-permute-done((bf16[128,512]{1,0:T(8,128)(2,1)}, bf16[128,512]{1,0:T(8,128)(2,1)S(1)}, u32[]{:S(2)}, u32[]{:S(2)}) %collective-permute-start.10) | collective-permute-done | bytes 131104 | tf_op jit(solution)/shard_map/ppermute | solution.py:318
  24.8 3.8 %collective-permute-start.1 = (bf16[128,512]{1,0:T(8,128)(2,1)}, bf16[128,512]{1,0:T(8,128)(2,1)S(1)}, u32[]{:S(2)}, u32[]{:S(2)}) collective-permute-start(bf16[128,512]{1,0:T(8,128)(2,1)} %get-tuple-element.44), channel_id=1, source_target_pairs={{0,24},{1,25},{2,26},{3,27},{4,28},{5,29},{6,30},{7,31},{8,16},{9,... | collective-permute-start | bytes 393224 | tf_op jit(solution)/shard_map/ppermute | solution.py:318
  28.6 0.0 collective-permute-done.6.refs_2_
  28.6 0.0 collective-permute-start.11
  28.6 0.0 copy-done
  28.6 2.9 %sums.6 = (f32[1024,512]{1,0:T(8,128)S(1)}, f32[1024,512]{1,0:T(8,128)S(1)}) custom-call(bf16[128,512]{1,0:T(8,128)(2,1)S(1)} %get-tuple-element.52.refs_0_, bf16[128,512]{1,0:T(8,128)(2,1)S(1)} %collective-permute-done.4.refs_1_, bf16[256,512]{1,0:T(8,128)(2,1)S(1)} %collective-permute-done.6.refs_2_, bf16[2048,512]{1,0:T(8,128)(2,1)S(1)} %copy-done), custom_call_target="tpu_custom_call" | custom-call | flops 1024 | bytes 1024 | tf_op jit(solution)/shard_map/sums/pallas_call | solution.py:227
  31.4 0.0 collective-permute-done.8.refs_1_
  31.5 0.0 copy-done.3
  31.5 2.2 %collective-permute-start.9 = (bf16[128,512]{1,0:T(8,128)(2,1)S(1)}, bf16[128,512]{1,0:T(8,128)(2,1)S(1)}, u32[]{:S(2)}, u32[]{:S(2)}) collective-permute-start(bf16[128,512]{1,0:T(8,128)(2,1)S(1)} %copy-done.3), channel_id=1, source_target_pairs={{0,28},{1,29},{2,30},{3,31},{4,24},{5,25},{6,26},{7,27},{8,20},{9,... | collective-permute-start | bytes 393224 | tf_op jit(solution)/shard_map/ppermute | solution.py:318
  33.6 0.0 collective-permute-done.5.refs_2_
  33.6 2.9 %sums.7 = (f32[1024,512]{1,0:T(8,128)S(1)}, f32[1024,512]{1,0:T(8,128)S(1)}) custom-call(bf16[128,512]{1,0:T(8,128)(2,1)S(1)} %collective-permute-done.2.refs_0_, bf16[128,512]{1,0:T(8,128)(2,1)S(1)} %collective-permute-done.refs_1_, bf16[256,512]{1,0:T(8,128)(2,1)S(1)} %collective-permute-done.5.refs_2_, bf16[2048,512]{1,0:T(8,128)(2,1)S(1)} %copy-done, ...), custom_call_target="tpu_custom_call" | custom-call | flops 1024 | bytes 1024 | tf_op jit(solution)/shard_map/sums/pallas_call | solution.py:227
  36.5 0.0 collective-permute-done.1.refs_0_
  36.5 0.0 copy-done.2
  36.6 1.4 %collective-permute-start.7 = (bf16[128,512]{1,0:T(8,128)(2,1)S(1)}, bf16[128,512]{1,0:T(8,128)(2,1)S(1)}, u32[]{:S(2)}, u32[]{:S(2)}) collective-permute-start(bf16[128,512]{1,0:T(8,128)(2,1)S(1)} %copy-done.2), channel_id=1, source_target_pairs={{0,30},{1,31},{2,28},{3,29},{4,26},{5,27},{6,24},{7,25},{8,22},{9,... | collective-permute-start | bytes 393224 | tf_op jit(solution)/shard_map/ppermute | solution.py:318
  37.9 0.0 collective-permute-done.12.refs_2_
  37.9 2.9 %sums.8 = (f32[1024,512]{1,0:T(8,128)S(1)}, f32[1024,512]{1,0:T(8,128)S(1)}) custom-call(bf16[128,512]{1,0:T(8,128)(2,1)S(1)} %collective-permute-done.10.refs_0_, bf16[128,512]{1,0:T(8,128)(2,1)S(1)} %collective-permute-done.8.refs_1_, bf16[256,512]{1,0:T(8,128)(2,1)S(1)} %collective-permute-done.12.refs_2_, bf16[2048,512]{1,0:T(8,128)(2,1)S(1)} %copy-done, ...), custom_call_target="tpu_custom_call" | custom-call | flops 1024 | bytes 1024 | tf_op jit(solution)/shard_map/sums/pallas_call | solution.py:227
  40.8 5.4 %collective-permute-done.11.refs_1_ = bf16[128,512]{1,0:T(8,128)(2,1)S(1)} collective-permute-done((bf16[128,512]{1,0:T(8,128)(2,1)}, bf16[128,512]{1,0:T(8,128)(2,1)S(1)}, u32[]{:S(2)}, u32[]{:S(2)}) %collective-permute-start.11) | collective-permute-done | bytes 131104 | tf_op jit(solution)/shard_map/ppermute | solution.py:318
  46.3 1.8 %sums.9 = (f32[1024,512]{1,0:T(8,128)S(1)}, f32[1024,512]{1,0:T(8,128)S(1)}) custom-call(bf16[128,512]{1,0:T(8,128)(2,1)S(1)} %collective-permute-done.1.refs_0_, bf16[128,512]{1,0:T(8,128)(2,1)S(1)} %collective-permute-done.11.refs_1_, bf16[2048,512]{1,0:T(8,128)(2,1)S(1)} %copy-done, f32[1024,512]{1,0:T(8,128)S(1)} %get-tuple-element.68.refs_3_, ...), custom_call_target="tpu_custom_call" | custom-call | flops 1024 | bytes 1024 | tf_op jit(solution)/shard_map/sums/pallas_call | solution.py:227
  48.0 5.3 %collective-permute-done.9.refs_0_ = bf16[128,512]{1,0:T(8,128)(2,1)S(1)} collective-permute-done((bf16[128,512]{1,0:T(8,128)(2,1)S(1)}, bf16[128,512]{1,0:T(8,128)(2,1)S(1)}, u32[]{:S(2)}, u32[]{:S(2)}) %collective-permute-start.9) | collective-permute-done | bytes 131104 | tf_op jit(solution)/shard_map/ppermute | solution.py:318
  53.3 1.6 %sums.10 = (f32[1024,512]{1,0:T(8,128)S(1)}, f32[1024,512]{1,0:T(8,128)S(1)}) custom-call(bf16[128,512]{1,0:T(8,128)(2,1)S(1)} %collective-permute-done.9.refs_0_, bf16[2048,512]{1,0:T(8,128)(2,1)S(1)} %copy-done, f32[1024,512]{1,0:T(8,128)S(1)} %get-tuple-element.70.refs_2_, f32[1024,512]{1,0:T(8,128)S(1)} %get-tuple-element.71.refs_3_), custom_call_target="tpu_custom_call" | custom-call | flops 1024 | bytes 1024 | tf_op jit(solution)/shard_map/sums/pallas_call | solution.py:227
  54.9 0.9 %collective-permute-done.7.refs_0_ = bf16[128,512]{1,0:T(8,128)(2,1)S(1)} collective-permute-done((bf16[128,512]{1,0:T(8,128)(2,1)S(1)}, bf16[128,512]{1,0:T(8,128)(2,1)S(1)}, u32[]{:S(2)}, u32[]{:S(2)}) %collective-permute-start.7) | collective-permute-done | bytes 131104 | tf_op jit(solution)/shard_map/ppermute | solution.py:318
  55.8 1.4 %sums.11 = (bf16[1024,128]{1,0:T(8,128)(2,1)S(1)}, f32[512,512]{1,0:T(8,128)S(1)}, f32[512,512]{1,0:T(8,128)S(1)}) custom-call(bf16[128,512]{1,0:T(8,128)(2,1)S(1)} %collective-permute-done.7.refs_0_, bf16[2048,512]{1,0:T(8,128)(2,1)S(1)} %copy-done, f32[1024,512]{1,0:T(8,128)S(1)} %get-tuple-element.72.refs_2_, f32[1024,512]{1,0:T(8,128)S(1)} %get-tuple-element.73.refs_3_), custom_call_target="tpu_custom_call" | custom-call | flops 1024 | bytes 1024 | tf_op jit(solution)/shard_map/sums/pallas_call | solution.py:227
  57.1 0.6 %collective-permute-start.14 = (f32[512,512]{1,0:T(8,128)S(1)}, f32[512,512]{1,0:T(8,128)S(1)}, u32[]{:S(2)}, u32[]{:S(2)}) collective-permute-start(f32[512,512]{1,0:T(8,128)S(1)} %get-tuple-element.76), channel_id=1, source_target_pairs={{0,1},{1,0},{2,3},{3,2},{4,5},{5,4},{6,7},{7,6},{8,9},{9,8},{10,11... | collective-permute-start | bytes 3145736 | tf_op jit(solution)/shard_map/ppermute | solution.py:352
  57.8 0.1 collective-permute-start.13
  57.9 0.4 own.1
  58.3 1.8 %collective-permute-done.14.refs_0_ = f32[512,512]{1,0:T(8,128)S(1)} collective-permute-done((f32[512,512]{1,0:T(8,128)S(1)}, f32[512,512]{1,0:T(8,128)S(1)}, u32[]{:S(2)}, u32[]{:S(2)}) %collective-permute-start.14) | collective-permute-done | bytes 1048608 | tf_op jit(solution)/shard_map/ppermute | solution.py:352
  60.1 1.0 %close.2.refs_1_ = bf16[1024,512]{1,0:T(8,128)(2,1)} custom-call(f32[1024,512]{1,0:T(8,128)S(1)} %own.1, f32[512,512]{1,0:T(8,128)S(1)} %collective-permute-done.14.refs_0_), custom_call_target="tpu_custom_call" | custom-call | flops 1024 | bytes 1024 | tf_op jit(solution)/shard_map/close/pallas_call | solution.py:285
  61.0 0.5 collective-permute-done.13.refs_0_
  61.6 1.0 %close.3 = bf16[1024,512]{1,0:T(8,128)(2,1)} custom-call(f32[1024,512]{1,0:T(8,128)S(1)} %own.1, f32[512,512]{1,0:T(8,128)S(1)} %collective-permute-done.13.refs_0_, bf16[1024,512]{1,0:T(8,128)(2,1)} %close.2.refs_1_), custom_call_target="tpu_custom_call", output_to_operand_aliasing={{}: (2, {})} | custom-call | flops 1024 | bytes 1024 | tf_op jit(solution)/shard_map/close/pallas_call | solution.py:285
  (1 shorter events, 0.0 us)
Async XLA Ops:
  0.0 28.6 %copy-start = (bf16[2048,512]{1,0:T(8,128)(2,1)S(1)}, bf16[2048,512]{1,0:T(8,128)(2,1)}, u32[]{:S(2)}) copy-start(bf16[2048,512]{1,0:T(8,128)(2,1)} %refs_3_.3) | copy-start | bytes 6291460
  3.8 2.2 %collective-permute-start.3 = (bf16[384,512]{1,0:T(8,128)(2,1)}, bf16[384,512]{1,0:T(8,128)(2,1)S(1)}, u32[]{:S(2)}, u32[]{:S(2)}) collective-permute-start(bf16[384,512]{1,0:T(8,128)(2,1)} %get-tuple-element.47), channel_id=1, source_target_pairs={{0,1},{1,0},{2,3},{3,2},{4,5},{5,4},{6,7},{7,6},{8,9},{9,8},{10,11... | collective-permute-start | bytes 1179656 | tf_op jit(solution)/shard_map/ppermute | solution.py:305
  4.5 7.9 %collective-permute-start.4 = (bf16[128,512]{1,0:T(8,128)(2,1)}, bf16[128,512]{1,0:T(8,128)(2,1)S(1)}, u32[]{:S(2)}, u32[]{:S(2)}) collective-permute-start(bf16[128,512]{1,0:T(8,128)(2,1)} %get-tuple-element.49), channel_id=1, source_target_pairs={{0,2},{1,3},{2,0},{3,1},{4,6},{5,7},{6,4},{7,5},{8,10},{9,11},{10,... | collective-permute-start | bytes 393224 | tf_op jit(solution)/shard_map/ppermute | solution.py:318
  5.9 9.0 %collective-permute-start.2 = (bf16[128,512]{1,0:T(8,128)(2,1)}, bf16[128,512]{1,0:T(8,128)(2,1)S(1)}, u32[]{:S(2)}, u32[]{:S(2)}) collective-permute-start(bf16[128,512]{1,0:T(8,128)(2,1)} %get-tuple-element.45), channel_id=1, source_target_pairs={{0,16},{1,17},{2,18},{3,19},{4,20},{5,21},{6,22},{7,23},{8,24},{9,... | collective-permute-start | bytes 393224 | tf_op jit(solution)/shard_map/ppermute | solution.py:318
  6.0 1.0 %copy-start.1 = (bf16[512,512]{1,0:T(8,128)(2,1)S(1)}, bf16[512,512]{1,0:T(8,128)(2,1)}, u32[]{:S(2)}) copy-start(bf16[512,512]{1,0:T(8,128)(2,1)} %get-tuple-element.46.kept) | copy-start | bytes 1572868
  7.1 24.4 %copy-start.3 = (bf16[128,512]{1,0:T(8,128)(2,1)S(1)}, bf16[128,512]{1,0:T(8,128)(2,1)}, u32[]{:S(2)}) copy-start(bf16[128,512]{1,0:T(8,128)(2,1)} %get-tuple-element.61) | copy-start | bytes 393220
  8.0 20.5 %collective-permute-start.6 = (bf16[256,512]{1,0:T(8,128)(2,1)}, bf16[256,512]{1,0:T(8,128)(2,1)S(1)}, u32[]{:S(2)}, u32[]{:S(2)}) collective-permute-start(bf16[256,512]{1,0:T(8,128)(2,1)} %get-tuple-element.53), channel_id=1, source_target_pairs={{0,4},{1,7},{2,6},{3,5},{4,0},{5,3},{6,2},{7,1},{8,12},{9,15},{10,... | collective-permute-start | bytes 786440 | tf_op jit(solution)/shard_map/ppermute | solution.py:318
  10.4 8.1 %collective-permute-start = (bf16[128,512]{1,0:T(8,128)(2,1)}, bf16[128,512]{1,0:T(8,128)(2,1)S(1)}, u32[]{:S(2)}, u32[]{:S(2)}) collective-permute-start(bf16[128,512]{1,0:T(8,128)(2,1)} %get-tuple-element.43), channel_id=1, source_target_pairs={{0,18},{1,19},{2,16},{3,17},{4,22},{5,23},{6,20},{7,21},{8,26},{9,... | collective-permute-start | bytes 393224 | tf_op jit(solution)/shard_map/ppermute | solution.py:318
  12.4 21.3 %collective-permute-start.5 = (bf16[256,512]{1,0:T(8,128)(2,1)}, bf16[256,512]{1,0:T(8,128)(2,1)S(1)}, u32[]{:S(2)}, u32[]{:S(2)}) collective-permute-start(bf16[256,512]{1,0:T(8,128)(2,1)} %get-tuple-element.50), channel_id=1, source_target_pairs={{0,8},{1,11},{2,10},{3,9},{4,12},{5,15},{6,14},{7,13},{8,0},{9,3},... | collective-permute-start | bytes 786440 | tf_op jit(solution)/shard_map/ppermute | solution.py:318
  13.6 11.2 %collective-permute-start.10 = (bf16[128,512]{1,0:T(8,128)(2,1)}, bf16[128,512]{1,0:T(8,128)(2,1)S(1)}, u32[]{:S(2)}, u32[]{:S(2)}) collective-permute-start(bf16[128,512]{1,0:T(8,128)(2,1)} %get-tuple-element.63), channel_id=1, source_target_pairs={{0,20},{1,21},{2,22},{3,23},{4,16},{5,17},{6,18},{7,19},{8,28},{9,... | collective-permute-start | bytes 393224 | tf_op jit(solution)/shard_map/ppermute | solution.py:318
  14.9 16.6 %collective-permute-start.8 = (bf16[128,512]{1,0:T(8,128)(2,1)}, bf16[128,512]{1,0:T(8,128)(2,1)S(1)}, u32[]{:S(2)}, u32[]{:S(2)}) collective-permute-start(bf16[128,512]{1,0:T(8,128)(2,1)} %get-tuple-element.60), channel_id=1, source_target_pairs={{0,22},{1,23},{2,20},{3,21},{4,18},{5,19},{6,16},{7,17},{8,30},{9,... | collective-permute-start | bytes 393224 | tf_op jit(solution)/shard_map/ppermute | solution.py:318
  18.4 19.5 %collective-permute-start.12 = (bf16[256,512]{1,0:T(8,128)(2,1)}, bf16[256,512]{1,0:T(8,128)(2,1)S(1)}, u32[]{:S(2)}, u32[]{:S(2)}) collective-permute-start(bf16[256,512]{1,0:T(8,128)(2,1)} %get-tuple-element.66), channel_id=1, source_target_pairs={{0,12},{1,15},{2,14},{3,13},{4,8},{5,11},{6,10},{7,9},{8,4},{9,7},... | collective-permute-start | bytes 786440 | tf_op jit(solution)/shard_map/ppermute | solution.py:318
  24.8 11.8 %collective-permute-start.1 = (bf16[128,512]{1,0:T(8,128)(2,1)}, bf16[128,512]{1,0:T(8,128)(2,1)S(1)}, u32[]{:S(2)}, u32[]{:S(2)}) collective-permute-start(bf16[128,512]{1,0:T(8,128)(2,1)} %get-tuple-element.44), channel_id=1, source_target_pairs={{0,24},{1,25},{2,26},{3,27},{4,28},{5,29},{6,30},{7,31},{8,16},{9,... | collective-permute-start | bytes 393224 | tf_op jit(solution)/shard_map/ppermute | solution.py:318
  28.6 17.7 %collective-permute-start.11 = (bf16[128,512]{1,0:T(8,128)(2,1)}, bf16[128,512]{1,0:T(8,128)(2,1)S(1)}, u32[]{:S(2)}, u32[]{:S(2)}) collective-permute-start(bf16[128,512]{1,0:T(8,128)(2,1)} %get-tuple-element.64), channel_id=1, source_target_pairs={{0,26},{1,27},{2,24},{3,25},{4,30},{5,31},{6,28},{7,29},{8,18},{9,... | collective-permute-start | bytes 393224 | tf_op jit(solution)/shard_map/ppermute | solution.py:318
  31.5 21.8 %collective-permute-start.9 = (bf16[128,512]{1,0:T(8,128)(2,1)S(1)}, bf16[128,512]{1,0:T(8,128)(2,1)S(1)}, u32[]{:S(2)}, u32[]{:S(2)}) collective-permute-start(bf16[128,512]{1,0:T(8,128)(2,1)S(1)} %copy-done.3), channel_id=1, source_target_pairs={{0,28},{1,29},{2,30},{3,31},{4,24},{5,25},{6,26},{7,27},{8,20},{9,... | collective-permute-start | bytes 393224 | tf_op jit(solution)/shard_map/ppermute | solution.py:318
  33.6 2.9 %copy-start.2 = (bf16[128,512]{1,0:T(8,128)(2,1)S(1)}, bf16[128,512]{1,0:T(8,128)(2,1)}, u32[]{:S(2)}) copy-start(bf16[128,512]{1,0:T(8,128)(2,1)} %get-tuple-element.57) | copy-start | bytes 393220
  36.6 19.2 %collective-permute-start.7 = (bf16[128,512]{1,0:T(8,128)(2,1)S(1)}, bf16[128,512]{1,0:T(8,128)(2,1)S(1)}, u32[]{:S(2)}, u32[]{:S(2)}) collective-permute-start(bf16[128,512]{1,0:T(8,128)(2,1)S(1)} %copy-done.2), channel_id=1, source_target_pairs={{0,30},{1,31},{2,28},{3,29},{4,26},{5,27},{6,24},{7,25},{8,22},{9,... | collective-permute-start | bytes 393224 | tf_op jit(solution)/shard_map/ppermute | solution.py:318
  57.1 2.9 %collective-permute-start.14 = (f32[512,512]{1,0:T(8,128)S(1)}, f32[512,512]{1,0:T(8,128)S(1)}, u32[]{:S(2)}, u32[]{:S(2)}) collective-permute-start(f32[512,512]{1,0:T(8,128)S(1)} %get-tuple-element.76), channel_id=1, source_target_pairs={{0,1},{1,0},{2,3},{3,2},{4,5},{5,4},{6,7},{7,6},{8,9},{9,8},{10,11... | collective-permute-start | bytes 3145736 | tf_op jit(solution)/shard_map/ppermute | solution.py:352
  57.8 3.8 %collective-permute-start.13 = (f32[512,512]{1,0:T(8,128)S(1)}, f32[512,512]{1,0:T(8,128)S(1)}, u32[]{:S(2)}, u32[]{:S(2)}) collective-permute-start(f32[512,512]{1,0:T(8,128)S(1)} %get-tuple-element.75), channel_id=1, source_target_pairs={{0,1},{1,0},{2,3},{3,2},{4,5},{5,4},{6,7},{7,6},{8,9},{9,8},{10,11... | collective-permute-start | bytes 3145736 | tf_op jit(solution)/shard_map/ppermute | solution.py:352

commit v6 on v5

--- a/solution.py
+++ b/solution.py
@@ -300,7 +300,8 @@
     replicas = lax.axis_size("copy")
     assert owners >= 16 and owners & (owners - 1) == 0 and replicas % 2 == 0
     half = owners // 2
-    far, paired = list(range(half, owners)), list(range(2, half, 2))
+    far = [half + (i & ~3 | (i & 1) << 1 | i >> 1 & 1) for i in range(half)]
+    paired = list(range(2, half, 2))
     singles, kept, give = stage(points, block_ids, block_counts, owners, far + [1], paired)
     give = lax.ppermute(give, "copy", [(k, k ^ 1) for k in range(replicas)])
     *both, mine = merge(kept, give, points.shape[1])

time: 62.6 us -> 62.3 us (level)
  starting transfers between devices: 25.2 us -> 24.3 us
    ppermute x12, starting transfers between devices: 23.9 us -> 23.1 us  [send(): arrived[k] = lax.ppermute(array, ('cluster', 'copy'), pairs)]
  transfers between devices with their start and end apart: 15 -> 15, of which waited for: 8 -> 7; matrix products, arithmetic and copies ran while one was open for 0% -> 0% of each run, Pallas kernels for 23% -> 23%
where the time goes in v6:
time: 62.3 us; the launch traced here: 62 us
  starting transfers between devices  24.3 us (39%)
  Pallas kernels  19.5 us (31%)
  waiting for transfers between devices  16.2 us (26%)
  local copies, waits for them, and re-layouts  1.05 us (2%)
  between operations  0.92 us (1%)
    ppermute x12, starting transfers between devices, send(): arrived[k] = lax.ppermute(array, ('cluster', 'copy'), pairs)  23.1 us
    ppermute x12, waiting for transfers between devices, send(): arrived[k] = lax.ppermute(array, ('cluster', 'copy'), pairs)  13.7 us
    pallas_call x6, Pallas kernels, sums(): pl.pallas_call(functools.partial(sums_kernel, len(xs), replicas, last), o...  13.3 us
    pallas_call x1, Pallas kernels, stage(): pl.pallas_call(functools.partial(stage_kernel, alone, paired), out_shape=...  2.93 us
    ppermute x2, waiting for transfers between devices, local(): lax.ppermute(shares[(r - 1) * HALVES + h], 'copy', [(i, (i + r) % replica...  2.32 us
    pallas_call x2, Pallas kernels, close(): pl.pallas_call(functools.partial(close_kernel, h, terms), out_shape=jax.S...  1.91 us
  transfers between devices with their start and end apart: 15, of which 7 were waited for; matrix products, arithmetic and copies ran while one was open for 0% of the time, Pallas kernels for 23%

profile of v6, /device:TPU:17, one launch (start us, length us, event | category | flops | bytes accessed | tf_op | source)
XLA Modules:
  0.0 62.0 jit_solution(12581421739088837519)
XLA Ops:
  0.0 0.0 copy-start
  0.8 2.9 %stage.1 = (bf16[128,512]{1,0:T(8,128)(2,1)}, bf16[128,512]{1,0:T(8,128)(2,1)}, bf16[128,512]{1,0:T(8,128)(2,1)}, bf16[128,512]{1,0:T(8,128)(2,1)}, bf16[128,512...) custom-call(s32[16]{0:T(128)} %ids_in.1, ...), custom_call_target="tpu_custom_call" | custom-call | tf_op jit(solution)/shard_map/stage/pallas_call | solution.py:81
  3.7 0.6 %collective-permute-start.3 = (bf16[384,512]{1,0:T(8,128)(2,1)}, bf16[384,512]{1,0:T(8,128)(2,1)S(1)}, u32[]{:S(2)}, u32[]{:S(2)}) collective-permute-start(bf16[384,512]{1,0:T(8,128)(2,1)} %get-tuple-element.47), channel_id=1, source_target_pairs={{0,1},{1,0},{2,3},{3,2},{4,5},{5,4},{6,7},{7,6},{8,9},{9,8},{10,11... | collective-permute-start | bytes 1179656 | tf_op jit(solution)/shard_map/ppermute | solution.py:306
  4.4 1.0 %collective-permute-start.4 = (bf16[128,512]{1,0:T(8,128)(2,1)}, bf16[128,512]{1,0:T(8,128)(2,1)S(1)}, u32[]{:S(2)}, u32[]{:S(2)}) collective-permute-start(bf16[128,512]{1,0:T(8,128)(2,1)} %get-tuple-element.49), channel_id=1, source_target_pairs={{0,2},{1,3},{2,0},{3,1},{4,6},{5,7},{6,4},{7,5},{8,10},{9,11},{10,... | collective-permute-start | bytes 393224 | tf_op jit(solution)/shard_map/ppermute | solution.py:319
  5.4 0.4 collective-permute-start.2
  5.8 0.2 collective-permute-done.3.got
  5.9 0.0 copy-start.1
  5.9 1.0 %copy-done.1 = bf16[512,512]{1,0:T(8,128)(2,1)S(1)} copy-done((bf16[512,512]{1,0:T(8,128)(2,1)S(1)}, bf16[512,512]{1,0:T(8,128)(2,1)}, u32[]{:S(2)}) %copy-start.1) | copy-done | bytes 524312
  7.0 0.0 copy-start.3
  7.0 0.9 %merge.1 = (bf16[256,512]{1,0:T(8,128)(2,1)}, bf16[256,512]{1,0:T(8,128)(2,1)}, bf16[256,512]{1,0:T(8,128)(2,1)}, bf16[128,512]{1,0:T(8,128)(2,1)S(1)}) custom-call(bf16[512,512]{1,0:T(8,128)(2,1)S(1)} %copy-done.1, bf16[384,512]{1,0:T(8,128)(2,1)S(1)} %collective-permute-done.3.got), custom_call_target="tpu_custom_call" | custom-call | tf_op jit(solution)/shard_map/merge/pallas_call | solution.py:119
  7.9 2.3 %collective-permute-start.6 = (bf16[256,512]{1,0:T(8,128)(2,1)}, bf16[256,512]{1,0:T(8,128)(2,1)S(1)}, u32[]{:S(2)}, u32[]{:S(2)}) collective-permute-start(bf16[256,512]{1,0:T(8,128)(2,1)} %get-tuple-element.53), channel_id=1, source_target_pairs={{0,4},{1,7},{2,6},{3,5},{4,0},{5,3},{6,2},{7,1},{8,12},{9,15},{10,... | collective-permute-start | bytes 786440 | tf_op jit(solution)/shard_map/ppermute | solution.py:319
  10.2 1.0 %collective-permute-start = (bf16[128,512]{1,0:T(8,128)(2,1)}, bf16[128,512]{1,0:T(8,128)(2,1)S(1)}, u32[]{:S(2)}, u32[]{:S(2)}) collective-permute-start(bf16[128,512]{1,0:T(8,128)(2,1)} %get-tuple-element.43), channel_id=1, source_target_pairs={{0,20},{1,21},{2,22},{3,23},{4,16},{5,17},{6,18},{7,19},{8,28},{9,... | collective-permute-start | bytes 393224 | tf_op jit(solution)/shard_map/ppermute | solution.py:319
  11.2 0.0 collective-permute-done.4.refs_1_
  11.2 2.3 %collective-permute-start.5 = (bf16[256,512]{1,0:T(8,128)(2,1)}, bf16[256,512]{1,0:T(8,128)(2,1)S(1)}, u32[]{:S(2)}, u32[]{:S(2)}) collective-permute-start(bf16[256,512]{1,0:T(8,128)(2,1)} %get-tuple-element.50), channel_id=1, source_target_pairs={{0,8},{1,11},{2,10},{3,9},{4,12},{5,15},{6,14},{7,13},{8,0},{9,3},... | collective-permute-start | bytes 786440 | tf_op jit(solution)/shard_map/ppermute | solution.py:319
  13.5 1.3 %collective-permute-start.10 = (bf16[128,512]{1,0:T(8,128)(2,1)}, bf16[128,512]{1,0:T(8,128)(2,1)S(1)}, u32[]{:S(2)}, u32[]{:S(2)}) collective-permute-start(bf16[128,512]{1,0:T(8,128)(2,1)} %get-tuple-element.63), channel_id=1, source_target_pairs={{0,18},{1,19},{2,16},{3,17},{4,22},{5,23},{6,20},{7,21},{8,26},{9,... | collective-permute-start | bytes 393224 | tf_op jit(solution)/shard_map/ppermute | solution.py:319
  14.8 0.0 collective-permute-done.2.refs_0_
  14.8 3.1 %collective-permute-start.8 = (bf16[128,512]{1,0:T(8,128)(2,1)}, bf16[128,512]{1,0:T(8,128)(2,1)S(1)}, u32[]{:S(2)}, u32[]{:S(2)}) collective-permute-start(bf16[128,512]{1,0:T(8,128)(2,1)} %get-tuple-element.60), channel_id=1, source_target_pairs={{0,22},{1,23},{2,20},{3,21},{4,18},{5,19},{6,16},{7,17},{8,30},{9,... | collective-permute-start | bytes 393224 | tf_op jit(solution)/shard_map/ppermute | solution.py:319
  17.9 0.0 collective-permute-done.refs_1_
  17.9 4.7 %collective-permute-start.12 = (bf16[256,512]{1,0:T(8,128)(2,1)}, bf16[256,512]{1,0:T(8,128)(2,1)S(1)}, u32[]{:S(2)}, u32[]{:S(2)}) collective-permute-start(bf16[256,512]{1,0:T(8,128)(2,1)} %get-tuple-element.66), channel_id=1, source_target_pairs={{0,12},{1,15},{2,14},{3,13},{4,8},{5,11},{6,10},{7,9},{8,4},{9,7},... | collective-permute-start | bytes 786440 | tf_op jit(solution)/shard_map/ppermute | solution.py:319
  22.6 2.2 %collective-permute-done.10.refs_0_ = bf16[128,512]{1,0:T(8,128)(2,1)S(1)} collective-permute-done((bf16[128,512]{1,0:T(8,128)(2,1)}, bf16[128,512]{1,0:T(8,128)(2,1)S(1)}, u32[]{:S(2)}, u32[]{:S(2)}) %collective-permute-start.10) | collective-permute-done | bytes 131104 | tf_op jit(solution)/shard_map/ppermute | solution.py:319
  24.8 3.1 %collective-permute-start.1 = (bf16[128,512]{1,0:T(8,128)(2,1)}, bf16[128,512]{1,0:T(8,128)(2,1)S(1)}, u32[]{:S(2)}, u32[]{:S(2)}) collective-permute-start(bf16[128,512]{1,0:T(8,128)(2,1)} %get-tuple-element.44), channel_id=1, source_target_pairs={{0,24},{1,25},{2,26},{3,27},{4,28},{5,29},{6,30},{7,31},{8,16},{9,... | collective-permute-start | bytes 393224 | tf_op jit(solution)/shard_map/ppermute | solution.py:319
  27.8 0.0 collective-permute-done.6.refs_2_
  27.9 1.4 %collective-permute-start.11 = (bf16[128,512]{1,0:T(8,128)(2,1)}, bf16[128,512]{1,0:T(8,128)(2,1)S(1)}, u32[]{:S(2)}, u32[]{:S(2)}) collective-permute-start(bf16[128,512]{1,0:T(8,128)(2,1)} %get-tuple-element.64), channel_id=1, source_target_pairs={{0,28},{1,29},{2,30},{3,31},{4,24},{5,25},{6,26},{7,27},{8,20},{9,... | collective-permute-start | bytes 393224 | tf_op jit(solution)/shard_map/ppermute | solution.py:319
  29.3 0.0 copy-done
  29.3 2.9 %sums.6 = (f32[1024,512]{1,0:T(8,128)S(1)}, f32[1024,512]{1,0:T(8,128)S(1)}) custom-call(bf16[128,512]{1,0:T(8,128)(2,1)S(1)} %get-tuple-element.52.refs_0_, bf16[128,512]{1,0:T(8,128)(2,1)S(1)} %collective-permute-done.4.refs_1_, bf16[256,512]{1,0:T(8,128)(2,1)S(1)} %collective-permute-done.6.refs_2_, bf16[2048,512]{1,0:T(8,128)(2,1)S(1)} %copy-done), custom_call_target="tpu_custom_call" | custom-call | flops 1024 | bytes 1024 | tf_op jit(solution)/shard_map/sums/pallas_call | solution.py:227
  32.1 0.0 collective-permute-done.8.refs_1_
  32.1 0.0 copy-done.3
  32.2 1.4 %collective-permute-start.9 = (bf16[128,512]{1,0:T(8,128)(2,1)S(1)}, bf16[128,512]{1,0:T(8,128)(2,1)S(1)}, u32[]{:S(2)}, u32[]{:S(2)}) collective-permute-start(bf16[128,512]{1,0:T(8,128)(2,1)S(1)} %copy-done.3), channel_id=1, source_target_pairs={{0,26},{1,27},{2,24},{3,25},{4,30},{5,31},{6,28},{7,29},{8,18},{9,... | collective-permute-start | bytes 393224 | tf_op jit(solution)/shard_map/ppermute | solution.py:319
  33.5 0.0 collective-permute-done.5.refs_2_
  33.5 2.9 %sums.7 = (f32[1024,512]{1,0:T(8,128)S(1)}, f32[1024,512]{1,0:T(8,128)S(1)}) custom-call(bf16[128,512]{1,0:T(8,128)(2,1)S(1)} %collective-permute-done.2.refs_0_, bf16[128,512]{1,0:T(8,128)(2,1)S(1)} %collective-permute-done.refs_1_, bf16[256,512]{1,0:T(8,128)(2,1)S(1)} %collective-permute-done.5.refs_2_, bf16[2048,512]{1,0:T(8,128)(2,1)S(1)} %copy-done, ...), custom_call_target="tpu_custom_call" | custom-call | flops 1024 | bytes 1024 | tf_op jit(solution)/shard_map/sums/pallas_call | solution.py:227
  36.4 0.0 collective-permute-done.1.refs_0_
  36.4 0.0 copy-done.2
  36.4 1.1 %collective-permute-start.7 = (bf16[128,512]{1,0:T(8,128)(2,1)S(1)}, bf16[128,512]{1,0:T(8,128)(2,1)S(1)}, u32[]{:S(2)}, u32[]{:S(2)}) collective-permute-start(bf16[128,512]{1,0:T(8,128)(2,1)S(1)} %copy-done.2), channel_id=1, source_target_pairs={{0,30},{1,31},{2,28},{3,29},{4,26},{5,27},{6,24},{7,25},{8,22},{9,... | collective-permute-start | bytes 393224 | tf_op jit(solution)/shard_map/ppermute | solution.py:319
  37.6 2.4 %collective-permute-done.12.refs_2_ = bf16[256,512]{1,0:T(8,128)(2,1)S(1)} collective-permute-done((bf16[256,512]{1,0:T(8,128)(2,1)}, bf16[256,512]{1,0:T(8,128)(2,1)S(1)}, u32[]{:S(2)}, u32[]{:S(2)}) %collective-permute-start.12) | collective-permute-done | bytes 262176 | tf_op jit(solution)/shard_map/ppermute | solution.py:319
  39.9 2.9 %sums.8 = (f32[1024,512]{1,0:T(8,128)S(1)}, f32[1024,512]{1,0:T(8,128)S(1)}) custom-call(bf16[128,512]{1,0:T(8,128)(2,1)S(1)} %collective-permute-done.10.refs_0_, bf16[128,512]{1,0:T(8,128)(2,1)S(1)} %collective-permute-done.8.refs_1_, bf16[256,512]{1,0:T(8,128)(2,1)S(1)} %collective-permute-done.12.refs_2_, bf16[2048,512]{1,0:T(8,128)(2,1)S(1)} %copy-done, ...), custom_call_target="tpu_custom_call" | custom-call | flops 1024 | bytes 1024 | tf_op jit(solution)/shard_map/sums/pallas_call | solution.py:227
  42.8 6.9 %collective-permute-done.11.refs_1_ = bf16[128,512]{1,0:T(8,128)(2,1)S(1)} collective-permute-done((bf16[128,512]{1,0:T(8,128)(2,1)}, bf16[128,512]{1,0:T(8,128)(2,1)S(1)}, u32[]{:S(2)}, u32[]{:S(2)}) %collective-permute-start.11) | collective-permute-done | bytes 131104 | tf_op jit(solution)/shard_map/ppermute | solution.py:319
  49.7 1.8 %sums.9 = (f32[1024,512]{1,0:T(8,128)S(1)}, f32[1024,512]{1,0:T(8,128)S(1)}) custom-call(bf16[128,512]{1,0:T(8,128)(2,1)S(1)} %collective-permute-done.1.refs_0_, bf16[128,512]{1,0:T(8,128)(2,1)S(1)} %collective-permute-done.11.refs_1_, bf16[2048,512]{1,0:T(8,128)(2,1)S(1)} %copy-done, f32[1024,512]{1,0:T(8,128)S(1)} %get-tuple-element.68.refs_3_, ...), custom_call_target="tpu_custom_call" | custom-call | flops 1024 | bytes 1024 | tf_op jit(solution)/shard_map/sums/pallas_call | solution.py:227
  51.5 0.0 collective-permute-done.9.refs_0_
  51.5 1.6 %sums.10 = (f32[1024,512]{1,0:T(8,128)S(1)}, f32[1024,512]{1,0:T(8,128)S(1)}) custom-call(bf16[128,512]{1,0:T(8,128)(2,1)S(1)} %collective-permute-done.9.refs_0_, bf16[2048,512]{1,0:T(8,128)(2,1)S(1)} %copy-done, f32[1024,512]{1,0:T(8,128)S(1)} %get-tuple-element.70.refs_2_, f32[1024,512]{1,0:T(8,128)S(1)} %get-tuple-element.71.refs_3_), custom_call_target="tpu_custom_call" | custom-call | flops 1024 | bytes 1024 | tf_op jit(solution)/shard_map/sums/pallas_call | solution.py:227
  53.1 2.3 %collective-permute-done.7.refs_0_ = bf16[128,512]{1,0:T(8,128)(2,1)S(1)} collective-permute-done((bf16[128,512]{1,0:T(8,128)(2,1)S(1)}, bf16[128,512]{1,0:T(8,128)(2,1)S(1)}, u32[]{:S(2)}, u32[]{:S(2)}) %collective-permute-start.7) | collective-permute-done | bytes 131104 | tf_op jit(solution)/shard_map/ppermute | solution.py:319
  55.4 1.3 %sums.11 = (bf16[1024,128]{1,0:T(8,128)(2,1)S(1)}, f32[512,512]{1,0:T(8,128)S(1)}, f32[512,512]{1,0:T(8,128)S(1)}) custom-call(bf16[128,512]{1,0:T(8,128)(2,1)S(1)} %collective-permute-done.7.refs_0_, bf16[2048,512]{1,0:T(8,128)(2,1)S(1)} %copy-done, f32[1024,512]{1,0:T(8,128)S(1)} %get-tuple-element.72.refs_2_, f32[1024,512]{1,0:T(8,128)S(1)} %get-tuple-element.73.refs_3_), custom_call_target="tpu_custom_call" | custom-call | flops 1024 | bytes 1024 | tf_op jit(solution)/shard_map/sums/pallas_call | solution.py:227
  56.7 0.5 collective-permute-start.14
  57.3 0.1 collective-permute-start.13
  57.3 0.4 own.1
  57.8 1.8 %collective-permute-done.14.refs_0_ = f32[512,512]{1,0:T(8,128)S(1)} collective-permute-done((f32[512,512]{1,0:T(8,128)S(1)}, f32[512,512]{1,0:T(8,128)S(1)}, u32[]{:S(2)}, u32[]{:S(2)}) %collective-permute-start.14) | collective-permute-done | bytes 1048608 | tf_op jit(solution)/shard_map/ppermute | solution.py:353
  59.6 1.0 %close.2.refs_1_ = bf16[1024,512]{1,0:T(8,128)(2,1)} custom-call(f32[1024,512]{1,0:T(8,128)S(1)} %own.1, f32[512,512]{1,0:T(8,128)S(1)} %collective-permute-done.14.refs_0_), custom_call_target="tpu_custom_call" | custom-call | flops 1024 | bytes 1024 | tf_op jit(solution)/shard_map/close/pallas_call | solution.py:285
  60.5 0.5 collective-permute-done.13.refs_0_
  61.1 1.0 %close.3 = bf16[1024,512]{1,0:T(8,128)(2,1)} custom-call(f32[1024,512]{1,0:T(8,128)S(1)} %own.1, f32[512,512]{1,0:T(8,128)S(1)} %collective-permute-done.13.refs_0_, bf16[1024,512]{1,0:T(8,128)(2,1)} %close.2.refs_1_), custom_call_target="tpu_custom_call", output_to_operand_aliasing={{}: (2, {})} | custom-call | flops 1024 | bytes 1024 | tf_op jit(solution)/shard_map/close/pallas_call | solution.py:285
  (1 shorter events, 0.0 us)
Async XLA Ops:
  0.0 29.3 %copy-start = (bf16[2048,512]{1,0:T(8,128)(2,1)S(1)}, bf16[2048,512]{1,0:T(8,128)(2,1)}, u32[]{:S(2)}) copy-start(bf16[2048,512]{1,0:T(8,128)(2,1)} %refs_3_.3) | copy-start | bytes 6291460
  3.7 2.2 %collective-permute-start.3 = (bf16[384,512]{1,0:T(8,128)(2,1)}, bf16[384,512]{1,0:T(8,128)(2,1)S(1)}, u32[]{:S(2)}, u32[]{:S(2)}) collective-permute-start(bf16[384,512]{1,0:T(8,128)(2,1)} %get-tuple-element.47), channel_id=1, source_target_pairs={{0,1},{1,0},{2,3},{3,2},{4,5},{5,4},{6,7},{7,6},{8,9},{9,8},{10,11... | collective-permute-start | bytes 1179656 | tf_op jit(solution)/shard_map/ppermute | solution.py:306
  4.4 6.8 %collective-permute-start.4 = (bf16[128,512]{1,0:T(8,128)(2,1)}, bf16[128,512]{1,0:T(8,128)(2,1)S(1)}, u32[]{:S(2)}, u32[]{:S(2)}) collective-permute-start(bf16[128,512]{1,0:T(8,128)(2,1)} %get-tuple-element.49), channel_id=1, source_target_pairs={{0,2},{1,3},{2,0},{3,1},{4,6},{5,7},{6,4},{7,5},{8,10},{9,11},{10,... | collective-permute-start | bytes 393224 | tf_op jit(solution)/shard_map/ppermute | solution.py:319
  5.4 9.4 %collective-permute-start.2 = (bf16[128,512]{1,0:T(8,128)(2,1)}, bf16[128,512]{1,0:T(8,128)(2,1)S(1)}, u32[]{:S(2)}, u32[]{:S(2)}) collective-permute-start(bf16[128,512]{1,0:T(8,128)(2,1)} %get-tuple-element.45), channel_id=1, source_target_pairs={{0,16},{1,17},{2,18},{3,19},{4,20},{5,21},{6,22},{7,23},{8,24},{9,... | collective-permute-start | bytes 393224 | tf_op jit(solution)/shard_map/ppermute | solution.py:319
  5.9 1.0 %copy-start.1 = (bf16[512,512]{1,0:T(8,128)(2,1)S(1)}, bf16[512,512]{1,0:T(8,128)(2,1)}, u32[]{:S(2)}) copy-start(bf16[512,512]{1,0:T(8,128)(2,1)} %get-tuple-element.46.kept) | copy-start | bytes 1572868
  7.0 25.2 %copy-start.3 = (bf16[128,512]{1,0:T(8,128)(2,1)S(1)}, bf16[128,512]{1,0:T(8,128)(2,1)}, u32[]{:S(2)}) copy-start(bf16[128,512]{1,0:T(8,128)(2,1)} %get-tuple-element.61) | copy-start | bytes 393220
  7.9 19.9 %collective-permute-start.6 = (bf16[256,512]{1,0:T(8,128)(2,1)}, bf16[256,512]{1,0:T(8,128)(2,1)S(1)}, u32[]{:S(2)}, u32[]{:S(2)}) collective-permute-start(bf16[256,512]{1,0:T(8,128)(2,1)} %get-tuple-element.53), channel_id=1, source_target_pairs={{0,4},{1,7},{2,6},{3,5},{4,0},{5,3},{6,2},{7,1},{8,12},{9,15},{10,... | collective-permute-start | bytes 786440 | tf_op jit(solution)/shard_map/ppermute | solution.py:319
  10.2 7.7 %collective-permute-start = (bf16[128,512]{1,0:T(8,128)(2,1)}, bf16[128,512]{1,0:T(8,128)(2,1)S(1)}, u32[]{:S(2)}, u32[]{:S(2)}) collective-permute-start(bf16[128,512]{1,0:T(8,128)(2,1)} %get-tuple-element.43), channel_id=1, source_target_pairs={{0,20},{1,21},{2,22},{3,23},{4,16},{5,17},{6,18},{7,19},{8,28},{9,... | collective-permute-start | bytes 393224 | tf_op jit(solution)/shard_map/ppermute | solution.py:319
  11.2 22.3 %collective-permute-start.5 = (bf16[256,512]{1,0:T(8,128)(2,1)}, bf16[256,512]{1,0:T(8,128)(2,1)S(1)}, u32[]{:S(2)}, u32[]{:S(2)}) collective-permute-start(bf16[256,512]{1,0:T(8,128)(2,1)} %get-tuple-element.50), channel_id=1, source_target_pairs={{0,8},{1,11},{2,10},{3,9},{4,12},{5,15},{6,14},{7,13},{8,0},{9,3},... | collective-permute-start | bytes 786440 | tf_op jit(solution)/shard_map/ppermute | solution.py:319
  13.5 11.3 %collective-permute-start.10 = (bf16[128,512]{1,0:T(8,128)(2,1)}, bf16[128,512]{1,0:T(8,128)(2,1)S(1)}, u32[]{:S(2)}, u32[]{:S(2)}) collective-permute-start(bf16[128,512]{1,0:T(8,128)(2,1)} %get-tuple-element.63), channel_id=1, source_target_pairs={{0,18},{1,19},{2,16},{3,17},{4,22},{5,23},{6,20},{7,21},{8,26},{9,... | collective-permute-start | bytes 393224 | tf_op jit(solution)/shard_map/ppermute | solution.py:319
  14.8 17.4 %collective-permute-start.8 = (bf16[128,512]{1,0:T(8,128)(2,1)}, bf16[128,512]{1,0:T(8,128)(2,1)S(1)}, u32[]{:S(2)}, u32[]{:S(2)}) collective-permute-start(bf16[128,512]{1,0:T(8,128)(2,1)} %get-tuple-element.60), channel_id=1, source_target_pairs={{0,22},{1,23},{2,20},{3,21},{4,18},{5,19},{6,16},{7,17},{8,30},{9,... | collective-permute-start | bytes 393224 | tf_op jit(solution)/shard_map/ppermute | solution.py:319
  17.9 22.0 %collective-permute-start.12 = (bf16[256,512]{1,0:T(8,128)(2,1)}, bf16[256,512]{1,0:T(8,128)(2,1)S(1)}, u32[]{:S(2)}, u32[]{:S(2)}) collective-permute-start(bf16[256,512]{1,0:T(8,128)(2,1)} %get-tuple-element.66), channel_id=1, source_target_pairs={{0,12},{1,15},{2,14},{3,13},{4,8},{5,11},{6,10},{7,9},{8,4},{9,7},... | collective-permute-start | bytes 786440 | tf_op jit(solution)/shard_map/ppermute | solution.py:319
  24.8 11.6 %collective-permute-start.1 = (bf16[128,512]{1,0:T(8,128)(2,1)}, bf16[128,512]{1,0:T(8,128)(2,1)S(1)}, u32[]{:S(2)}, u32[]{:S(2)}) collective-permute-start(bf16[128,512]{1,0:T(8,128)(2,1)} %get-tuple-element.44), channel_id=1, source_target_pairs={{0,24},{1,25},{2,26},{3,27},{4,28},{5,29},{6,30},{7,31},{8,16},{9,... | collective-permute-start | bytes 393224 | tf_op jit(solution)/shard_map/ppermute | solution.py:319
  27.9 21.9 %collective-permute-start.11 = (bf16[128,512]{1,0:T(8,128)(2,1)}, bf16[128,512]{1,0:T(8,128)(2,1)S(1)}, u32[]{:S(2)}, u32[]{:S(2)}) collective-permute-start(bf16[128,512]{1,0:T(8,128)(2,1)} %get-tuple-element.64), channel_id=1, source_target_pairs={{0,28},{1,29},{2,30},{3,31},{4,24},{5,25},{6,26},{7,27},{8,20},{9,... | collective-permute-start | bytes 393224 | tf_op jit(solution)/shard_map/ppermute | solution.py:319
  32.2 19.4 %collective-permute-start.9 = (bf16[128,512]{1,0:T(8,128)(2,1)S(1)}, bf16[128,512]{1,0:T(8,128)(2,1)S(1)}, u32[]{:S(2)}, u32[]{:S(2)}) collective-permute-start(bf16[128,512]{1,0:T(8,128)(2,1)S(1)} %copy-done.3), channel_id=1, source_target_pairs={{0,26},{1,27},{2,24},{3,25},{4,30},{5,31},{6,28},{7,29},{8,18},{9,... | collective-permute-start | bytes 393224 | tf_op jit(solution)/shard_map/ppermute | solution.py:319
  33.5 2.9 %copy-start.2 = (bf16[128,512]{1,0:T(8,128)(2,1)S(1)}, bf16[128,512]{1,0:T(8,128)(2,1)}, u32[]{:S(2)}) copy-start(bf16[128,512]{1,0:T(8,128)(2,1)} %get-tuple-element.57) | copy-start | bytes 393220
  36.4 18.9 %collective-permute-start.7 = (bf16[128,512]{1,0:T(8,128)(2,1)S(1)}, bf16[128,512]{1,0:T(8,128)(2,1)S(1)}, u32[]{:S(2)}, u32[]{:S(2)}) collective-permute-start(bf16[128,512]{1,0:T(8,128)(2,1)S(1)} %copy-done.2), channel_id=1, source_target_pairs={{0,30},{1,31},{2,28},{3,29},{4,26},{5,27},{6,24},{7,25},{8,22},{9,... | collective-permute-start | bytes 393224 | tf_op jit(solution)/shard_map/ppermute | solution.py:319
  56.7 2.8 %collective-permute-start.14 = (f32[512,512]{1,0:T(8,128)S(1)}, f32[512,512]{1,0:T(8,128)S(1)}, u32[]{:S(2)}, u32[]{:S(2)}) collective-permute-start(f32[512,512]{1,0:T(8,128)S(1)} %get-tuple-element.76), channel_id=1, source_target_pairs={{0,1},{1,0},{2,3},{3,2},{4,5},{5,4},{6,7},{7,6},{8,9},{9,8},{10,11... | collective-permute-start | bytes 3145736 | tf_op jit(solution)/shard_map/ppermute | solution.py:353
  57.3 3.8 %collective-permute-start.13 = (f32[512,512]{1,0:T(8,128)S(1)}, f32[512,512]{1,0:T(8,128)S(1)}, u32[]{:S(2)}, u32[]{:S(2)}) collective-permute-start(f32[512,512]{1,0:T(8,128)S(1)} %get-tuple-element.75), channel_id=1, source_target_pairs={{0,1},{1,0},{2,3},{3,2},{4,5},{5,4},{6,7},{7,6},{8,9},{9,8},{10,11... | collective-permute-start | bytes 3145736 | tf_op jit(solution)/shard_map/ppermute | solution.py:353
